TPU v7x, 32 devices: a whole 2x2x4 slice. The times are simulated.
32 devices in a mesh: section: 2 (over core), dp: 8 (over z, y), head: 2 (over x).
Axes of the slice: x: 2, y: 2, z: 4, core: 2. Of those that a mesh axis runs over, the one named last changes fastest.
Arguments:
- tokens: bfloat16 [2, 2048, 1152], P(None, 'dp'), may hold values from -6 to 6
- kept_mask: int32 [2, 8, 256], P(None, 'dp'), may hold values 0 or 1
- timesteps: int32 [2, 8], P(None, 'dp'), may hold values from 0 to 999
- labels: int32 [2, 8], P(None, 'dp'), may hold values from 0 to 999
- w_qkv: bfloat16 [2, 1152, 3, 1152], P('section', 'dp', None, 'head'), may hold values from -0.1875 to 0.1875
- b_qv: bfloat16 [2, 2, 1152], P('section', None, 'head'), may hold values from -2 to 2
- w_out: bfloat16 [2, 1152, 1152], P('section', 'head', 'dp'), may hold values from -0.5 to 0.5
- b_out: bfloat16 [2, 1152], P('section'), may hold values from -2 to 2
- w_up: bfloat16 [2, 1152, 4608], P('section', 'dp', 'head'), may hold values from -0.1875 to 0.1875
- b_up: bfloat16 [2, 4608], P('section', 'head'), may hold values from -2 to 2
- w_down: bfloat16 [2, 4608, 1152], P('section', 'head', 'dp'), may hold values from -0.1875 to 0.1875
- b_down: bfloat16 [2, 1152], P('section'), may hold values from -2 to 2
- w_ada: bfloat16 [2, 1152, 6, 1152], P('section', 'dp', None, 'head'), may hold values from -0.1875 to 0.1875
- b_ada: bfloat16 [2, 6, 1152], P('section', None, 'head'), may hold values from -3 to 3
- rel_table: bfloat16 [2, 16, 511], P('section', 'head'), may hold values from -5 to 5
- mask_token: bfloat16 [1152], replicated, may hold values from -5 to 5
- class_table: bfloat16 [1000, 1152], replicated, may hold values from -5 to 5
- out_grad: bfloat16 [2, 2048, 1152], P(None, 'dp'), may hold values from -6 to 6
Outputs:
- block_outputs: float32 [2, 2, 2048, 1152], P('section', None, 'dp')
- input_grads: float32 [2, 2, 2048, 1152], P('section', None, 'dp')
- g_w_qkv: float32 [2, 1152, 3, 1152], P('section', 'dp', None, 'head')
- g_b_qv: float32 [2, 2, 1152], P('section', None, 'head')
- g_w_out: float32 [2, 1152, 1152], P('section', 'head', 'dp')
- g_b_out: float32 [2, 1152], P('section', 'head')
- g_w_up: float32 [2, 1152, 4608], P('section', 'dp', 'head')
- g_b_up: float32 [2, 4608], P('section', 'head')
- g_w_down: float32 [2, 4608, 1152], P('section', 'head', 'dp')
- g_b_down: float32 [2, 1152], P('section', 'head')
- g_w_ada: float32 [2, 1152, 6, 1152], P('section', 'dp', None, 'head')
- g_b_ada: float32 [2, 6, 1152], P('section', None, 'head')
- g_rel_table: float32 [2, 16, 511], P('section', 'head')
- g_mask_token: float32 [1152], P('head')
- g_class_table: float32 [1000, 1152], P(None, 'head')
All inputs are finite; a program needn't handle non-finite values. No bound on the sum of `kept_mask` on one device may be relied on, other than what follows from the above.
Results may differ from a plain program's by a relative error of at most 0.03.
Values may be sent and summed in bfloat16 or wider, within the bound.
A program may use at most 384 MiB of HBM per device.

v0:
```python
from functools import partial
import math

import jax
import jax.numpy as jnp
from jax import lax
from jax.sharding import PartitionSpec as P

PRECISE = lax.Precision.HIGHEST
EPSILON = 1e-06
NEGATIVE = -1e30


def from_behind(value, axis, steps):
    count = lax.axis_size(axis)
    initial, last = (max(0, -steps), min(count, count - steps))
    return lax.ppermute(value, axis, [(source, source + steps) for source in range(initial, last)])


def time_features(step_ids, model_width):
    half_width = model_width // 2
    frequency = jnp.exp(
        -math.log(10000.0) * jnp.arange(half_width).astype(jnp.float32) / half_width
    )
    angles = step_ids.astype(jnp.float32)[..., None] * frequency
    return jnp.concatenate([jnp.cos(angles), jnp.sin(angles)], axis=-1)


def layout(mask_group, image_count, length):
    kept_flags = mask_group.reshape(-1)
    row_count = kept_flags.shape[0]
    slot_ids = jnp.arange(row_count, dtype=jnp.int32)
    source = jnp.where(kept_flags == 1, jnp.cumsum(kept_flags) - 1, row_count)
    image_of = slot_ids // length
    positions = slot_ids % length
    packed_pos = jnp.zeros((row_count,), jnp.int32).at[source].set(positions, mode="drop")
    packed_seg = (
        jnp.full((row_count,), image_count, jnp.int32).at[source].set(image_of, mode="drop")
    )
    return (kept_flags, source, image_of, positions, packed_pos, packed_seg)


def normalize(values_in):
    centered = values_in - jnp.mean(values_in, axis=-1, keepdims=True)
    inverse = lax.rsqrt(jnp.mean(centered * centered, axis=-1, keepdims=True) + EPSILON)
    return (centered * inverse, inverse)


def norm_back(grad_hat, normed, inverse):
    return inverse * (
        grad_hat
        - jnp.mean(grad_hat, axis=-1, keepdims=True)
        - normed * jnp.mean(grad_hat * normed, axis=-1, keepdims=True)
    )


def smooth_gate(values_in):
    return jax.nn.gelu(values_in, approximate=True)


def local_back(function, point, grad_in):
    unused, pull = jax.vjp(function, point)
    return pull(grad_in)[0]


def head_total(partial_sum):
    return lax.psum(partial_sum, "head")


def head_back(partial_sum):
    return lax.psum(partial_sum, "head")


def rel_bias(pos_pick, rel_local, length):
    span = jnp.arange(length, dtype=jnp.int32)
    grid_index = span[:, None] - span[None, :] + length - 1
    skewed = jnp.take(rel_local, grid_index, axis=1)
    left_part = jnp.einsum("ri,hij->hrj", pos_pick, skewed, precision=PRECISE)
    return jnp.einsum("hrj,sj->hrs", left_part, pos_pick, precision=PRECISE)


def logits_of(queries, keys_all, bias, same_seg, score_scale):
    raw = (
        jnp.einsum("qhd,khd->hqk", queries, keys_all, preferred_element_type=jnp.float32)
        * score_scale
    )
    return jnp.where(same_seg[None], raw + bias, NEGATIVE)


def table_sums(grad_logits, pos_pick, length):
    head_local = grad_logits.shape[0]
    left_part = jnp.einsum(
        "ri,hrs->his",
        pos_pick.astype(jnp.bfloat16),
        grad_logits,
        preferred_element_type=jnp.float32,
    )
    square = jnp.einsum("his,sj->hij", left_part, pos_pick, precision=PRECISE)
    flipped = square[:, :, ::-1]
    padded = jnp.pad(flipped, ((0, 0), (0, 0), (0, length)))
    flat = padded.reshape(head_local, 2 * length * length)[:, : length * (2 * length - 1)]
    return jnp.sum(flat.reshape(head_local, length, 2 * length - 1), axis=1)


def forward_block(
    state_in, segment, positions, image_rows, condition, weights, length, image_count
):
    w_qkv, b_qv, w_out, b_out, w_up, b_up, w_down, b_down, w_ada, b_ada, rel_local = weights
    row_count = state_in.shape[0]
    head_local = rel_local.shape[0]
    local_width = w_qkv.shape[2]
    head_dim = local_width // head_local
    score_scale = 1.0 / math.sqrt(head_dim)
    cond_low = jax.nn.silu(condition)
    mod_local = (
        jnp.einsum("id,dke->ike", cond_low, w_ada.astype(jnp.float32), precision=PRECISE) + b_ada
    )
    mod_table = lax.all_gather(mod_local, "head", axis=2, tiled=True)
    picker = (image_rows[:, None] == jnp.arange(image_count)[None, :]).astype(jnp.float32)
    per_row = jnp.einsum("ri,ike->rke", picker, mod_table, precision=PRECISE)
    hat_one, inv_one = normalize(state_in)
    normed = (hat_one * (1.0 + per_row[:, 1]) + per_row[:, 0]).astype(jnp.bfloat16)
    joined = jnp.einsum("rd,dke->rke", normed, w_qkv, preferred_element_type=jnp.float32)
    shape_heads = (row_count, head_local, head_dim)
    queries = (joined[:, 0] + b_qv[0]).astype(jnp.bfloat16).reshape(shape_heads)
    keys_all = joined[:, 1].astype(jnp.bfloat16).reshape(shape_heads)
    values_all = (joined[:, 2] + b_qv[1]).astype(jnp.bfloat16).reshape(shape_heads)
    pos_pick = (positions[:, None] == jnp.arange(length)[None, :]).astype(jnp.float32)
    same_seg = segment[:, None] == segment[None, :]
    logits = logits_of(
        queries, keys_all, rel_bias(pos_pick, rel_local, length), same_seg, score_scale
    )
    row_peak = jnp.max(logits, axis=-1, keepdims=True)
    log_total = row_peak + jnp.log(jnp.sum(jnp.exp(logits - row_peak), axis=-1, keepdims=True))
    att_probs = jnp.exp(logits - log_total)
    att_mixed = jnp.einsum(
        "hqk,khd->qhd",
        att_probs.astype(jnp.bfloat16),
        values_all,
        preferred_element_type=jnp.float32,
    )
    att_mixed = att_mixed.reshape(row_count, local_width).astype(jnp.bfloat16)
    branch = head_total(jnp.dot(att_mixed, w_out, preferred_element_type=jnp.float32)) + b_out
    middle = state_in + per_row[:, 2] * branch
    hat_two, inv_two = normalize(middle)
    normed_two = (hat_two * (1.0 + per_row[:, 4]) + per_row[:, 3]).astype(jnp.bfloat16)
    hidden_pre = jnp.dot(normed_two, w_up, preferred_element_type=jnp.float32) + b_up
    hidden = smooth_gate(hidden_pre).astype(jnp.bfloat16)
    result = head_total(jnp.dot(hidden, w_down, preferred_element_type=jnp.float32)) + b_down
    output = middle + per_row[:, 5] * result
    kept_state = (
        condition,
        cond_low,
        picker,
        mod_table,
        hat_one,
        inv_one,
        normed,
        queries,
        keys_all,
        values_all,
        pos_pick,
        same_seg,
        log_total,
        att_mixed,
        branch,
        hat_two,
        inv_two,
        normed_two,
        hidden_pre,
        hidden,
        result,
    )
    return (output, kept_state)


def backward_block(grad_out, kept_state, weights, length, head_idx):
    w_qkv, b_qv, w_out, b_out, w_up, b_up, w_down, b_down, w_ada, b_ada, rel_local = weights
    (
        condition,
        cond_low,
        picker,
        mod_table,
        hat_one,
        inv_one,
        normed,
        queries,
        keys_all,
        values_all,
        pos_pick,
        same_seg,
        log_total,
        att_mixed,
        branch,
        hat_two,
        inv_two,
        normed_two,
        hidden_pre,
        hidden,
        result,
    ) = kept_state
    row_count = grad_out.shape[0]
    head_local = rel_local.shape[0]
    local_width = w_qkv.shape[2]
    head_dim = local_width // head_local
    score_scale = 1.0 / math.sqrt(head_dim)
    per_row = jnp.einsum("ri,ike->rke", picker, mod_table, precision=PRECISE)
    grad_result = (grad_out * per_row[:, 5]).astype(jnp.bfloat16)
    grad_gate_two = grad_out * result
    grad_b_down = jnp.sum(grad_result.astype(jnp.float32), axis=0)
    grad_down_flip = jnp.einsum(
        "rd,rf->df", grad_result, hidden, preferred_element_type=jnp.float32
    )
    grad_hidden = jnp.einsum("rd,fd->rf", grad_result, w_down, preferred_element_type=jnp.float32)
    grad_pre = local_back(smooth_gate, hidden_pre, grad_hidden).astype(jnp.bfloat16)
    grad_b_up = jnp.sum(grad_pre.astype(jnp.float32), axis=0)
    grad_w_up = jnp.einsum("rd,rf->df", normed_two, grad_pre, preferred_element_type=jnp.float32)
    grad_normed_two = head_back(
        jnp.einsum("rf,df->rd", grad_pre, w_up, preferred_element_type=jnp.float32)
    )
    grad_scale_two = grad_normed_two * hat_two
    grad_mid = grad_out + norm_back(grad_normed_two * (1.0 + per_row[:, 4]), hat_two, inv_two)
    grad_gate_one = grad_mid * branch
    grad_branch = (grad_mid * per_row[:, 2]).astype(jnp.bfloat16)
    grad_b_out = jnp.sum(grad_branch.astype(jnp.float32), axis=0)
    grad_out_flip = jnp.einsum(
        "rd,rc->dc", grad_branch, att_mixed, preferred_element_type=jnp.float32
    )
    shape_heads = (row_count, head_local, head_dim)
    grad_mixed = (
        jnp.einsum("rd,cd->rc", grad_branch, w_out, preferred_element_type=jnp.float32)
        .astype(jnp.bfloat16)
        .reshape(shape_heads)
    )
    logits = logits_of(
        queries, keys_all, rel_bias(pos_pick, rel_local, length), same_seg, score_scale
    )
    att_probs = jnp.exp(logits - log_total)
    grad_probs = jnp.einsum(
        "qhd,khd->hqk", grad_mixed, values_all, preferred_element_type=jnp.float32
    )
    grad_values = jnp.einsum(
        "hqk,qhd->khd",
        att_probs.astype(jnp.bfloat16),
        grad_mixed,
        preferred_element_type=jnp.float32,
    ).astype(jnp.bfloat16)
    row_inner = jnp.sum(att_probs * grad_probs, axis=-1, keepdims=True)
    grad_logits = (att_probs * (grad_probs - row_inner)).astype(jnp.bfloat16)
    grad_queries = (
        jnp.einsum("hqk,khd->qhd", grad_logits, keys_all, preferred_element_type=jnp.float32)
        * score_scale
    ).astype(jnp.bfloat16)
    grad_keys = (
        jnp.einsum("hqk,qhd->khd", grad_logits, queries, preferred_element_type=jnp.float32)
        * score_scale
    ).astype(jnp.bfloat16)
    grad_rel = table_sums(grad_logits, pos_pick, length)
    grad_joined = jnp.stack([grad_queries, grad_keys, grad_values], axis=1).reshape(
        row_count, 3, local_width
    )
    grad_b_qv = jnp.stack(
        [
            jnp.sum(grad_joined[:, 0].astype(jnp.float32), axis=0),
            jnp.sum(grad_joined[:, 2].astype(jnp.float32), axis=0),
        ]
    )
    grad_w_qkv = jnp.einsum("rd,rke->dke", normed, grad_joined, preferred_element_type=jnp.float32)
    grad_normed = head_back(
        jnp.einsum("rke,dke->rd", grad_joined, w_qkv, preferred_element_type=jnp.float32)
    )
    grad_state = grad_mid + norm_back(grad_normed * (1.0 + per_row[:, 1]), hat_one, inv_one)
    grad_rows = jnp.stack(
        [
            grad_normed,
            grad_normed * hat_one,
            grad_gate_one,
            grad_normed_two,
            grad_scale_two,
            grad_gate_two,
        ],
        axis=1,
    )
    grad_mod = jnp.einsum("ri,rke->ike", picker, grad_rows, precision=PRECISE)
    grad_local = lax.dynamic_slice_in_dim(grad_mod, head_idx * local_width, local_width, 2)
    grad_w_ada = jnp.einsum("id,ike->dke", cond_low, grad_local, precision=PRECISE)
    grad_b_ada = jnp.sum(grad_local, axis=0)
    grad_cond_low = jnp.einsum(
        "ike,dke->id", grad_local, w_ada.astype(jnp.float32), precision=PRECISE
    )
    grad_cond = local_back(jax.nn.silu, condition, grad_cond_low)
    big_terms = (grad_w_qkv, grad_out_flip, grad_w_up, grad_down_flip, grad_w_ada)
    small_terms = (grad_b_qv, grad_b_out, grad_b_up, grad_b_down, grad_b_ada, grad_rel)
    return (grad_state, big_terms, small_terms, grad_cond)


def add_terms(total, terms):
    if total is None:
        return terms
    return tuple((first_term + second_term for first_term, second_term in zip(total, terms)))


def per_device(
    tokens,
    kept_mask,
    timesteps,
    labels,
    w_qkv,
    b_qv,
    w_out,
    b_out,
    w_up,
    b_up,
    w_down,
    b_down,
    w_ada,
    b_ada,
    rel_table,
    mask_token,
    class_table,
    out_grad,
):
    micro_count, row_count, model_width = tokens.shape
    image_count = kept_mask.shape[1]
    length = kept_mask.shape[2]
    class_count = class_table.shape[0]
    half_width = model_width // lax.axis_size("head")
    head_idx = lax.axis_index("head")
    section_idx = lax.axis_index("section")
    is_first = section_idx == 0
    gathered = (
        lax.all_gather(w_qkv[0], "dp", axis=0, tiled=True),
        lax.all_gather(w_out[0], "dp", axis=1, tiled=True),
        lax.all_gather(w_up[0], "dp", axis=0, tiled=True),
        lax.all_gather(w_down[0], "dp", axis=1, tiled=True),
        lax.all_gather(w_ada[0], "dp", axis=0, tiled=True),
    )
    weights = (
        gathered[0],
        b_qv[0].astype(jnp.float32),
        gathered[1],
        b_out[0].astype(jnp.float32),
        gathered[2],
        b_up[0].astype(jnp.float32),
        gathered[3],
        b_down[0].astype(jnp.float32),
        gathered[4],
        b_ada[0].astype(jnp.float32),
        rel_table[0].astype(jnp.float32),
    )
    kept_all, source_all, image_all, place_all, packed_pos, packed_seg = jax.vmap(
        partial(layout, image_count=image_count, length=length)
    )(kept_mask)
    label_pick = (labels[..., None] == jnp.arange(class_count)).astype(jnp.bfloat16)
    cond_all = jnp.einsum(
        "mic,cd->mid", label_pick, class_table, preferred_element_type=jnp.float32
    ) + time_features(timesteps, model_width)
    mask_row = mask_token.astype(jnp.float32)
    received = jnp.zeros((row_count, model_width), jnp.bfloat16)
    outs_buf = jnp.zeros((micro_count, row_count, model_width), jnp.float32)
    kept_ticks = []
    for tick_no in range(micro_count + 1):
        micro_now = tick_no - section_idx
        is_valid = (micro_now >= 0) & (micro_now < micro_count)
        micro_idx = jnp.clip(micro_now, 0, micro_count - 1)
        kept_flags = kept_all[micro_idx]
        picked = jnp.take(
            received, jnp.minimum(source_all[micro_idx], row_count - 1), axis=0
        ).astype(jnp.float32)
        placed = jnp.where(kept_flags[:, None] == 1, picked, mask_row[None, :])
        state_in = jnp.where(is_first, tokens[micro_idx].astype(jnp.float32), placed)
        segment = jnp.where(is_first, packed_seg[micro_idx], image_all[micro_idx])
        positions = jnp.where(is_first, packed_pos[micro_idx], place_all[micro_idx])
        image_rows = jnp.minimum(segment, image_count - 1)
        output, kept_state = forward_block(
            state_in,
            segment,
            positions,
            image_rows,
            cond_all[micro_idx],
            weights,
            length,
            image_count,
        )
        outs_buf = jnp.where(
            is_valid, lax.dynamic_update_index_in_dim(outs_buf, output, micro_idx, 0), outs_buf
        )
        kept_ticks.append(kept_state)
        if tick_no < micro_count:
            received = from_behind(output.astype(jnp.bfloat16), "section", 1)
    received_grad = jnp.zeros((row_count, model_width), jnp.bfloat16)
    in_grads = jnp.zeros((micro_count, row_count, model_width), jnp.float32)
    big_sum = None
    small_sum = None
    cond_buf = jnp.zeros((micro_count, image_count, model_width), jnp.float32)
    mask_sum = jnp.zeros((model_width,), jnp.float32)
    for tick_no in range(micro_count + 1):
        micro_now = micro_count - tick_no - section_idx
        is_valid = (micro_now >= 0) & (micro_now < micro_count)
        micro_idx = jnp.clip(micro_now, 0, micro_count - 1)
        cotangent = jnp.where(
            is_first, received_grad.astype(jnp.float32), out_grad[micro_idx].astype(jnp.float32)
        )
        cotangent = jnp.where(is_valid, cotangent, 0.0)
        grad_state, big_terms, small_terms, grad_cond = backward_block(
            cotangent, kept_ticks[micro_count - tick_no], weights, length, head_idx
        )
        in_grads = jnp.where(
            is_valid, lax.dynamic_update_index_in_dim(in_grads, grad_state, micro_idx, 0), in_grads
        )
        kept_flags = kept_all[micro_idx]
        dropped = jnp.where(is_first, 0.0, 1.0 - kept_flags.astype(jnp.float32))
        mask_sum = mask_sum + jnp.sum(grad_state * dropped[:, None], axis=0)
        cond_buf = cond_buf.at[micro_idx].add(jnp.where(is_valid, grad_cond, 0.0))
        small_sum = add_terms(small_sum, small_terms)
        big_sum = add_terms(big_sum, big_terms)
        if tick_no < micro_count:
            packed_grad = (
                jnp.zeros((row_count, model_width), jnp.float32)
                .at[source_all[micro_idx]]
                .add(grad_state, mode="drop")
            )
            received_grad = from_behind(packed_grad.astype(jnp.bfloat16), "section", -1)
    big_sum = (
        lax.psum_scatter(big_sum[0], "dp", scatter_dimension=0, tiled=True),
        lax.psum_scatter(big_sum[1], "dp", scatter_dimension=0, tiled=True),
        lax.psum_scatter(big_sum[2], "dp", scatter_dimension=0, tiled=True),
        lax.psum_scatter(big_sum[3], "dp", scatter_dimension=0, tiled=True),
        lax.psum_scatter(big_sum[4], "dp", scatter_dimension=0, tiled=True),
    )
    grad_out_own = big_sum[1].T
    grad_down_own = big_sum[3].T
    out_half = lax.dynamic_slice_in_dim(small_sum[1], head_idx * half_width, half_width, 0)
    down_half = lax.dynamic_slice_in_dim(small_sum[3], head_idx * half_width, half_width, 0)
    small_total = lax.psum(
        (small_sum[0], out_half, small_sum[2], down_half, small_sum[4], small_sum[5]), "dp"
    )
    class_sum = jnp.einsum(
        "mic,mid->cd", label_pick.astype(jnp.float32), cond_buf, precision=PRECISE
    )
    shared_total = lax.psum((class_sum, 0.5 * mask_sum), ("section", "dp", "head"))
    class_half = lax.dynamic_slice_in_dim(shared_total[0], head_idx * half_width, half_width, 1)
    mask_half = lax.dynamic_slice_in_dim(shared_total[1], head_idx * half_width, half_width, 0)
    return (
        outs_buf[None],
        in_grads[None],
        big_sum[0][None],
        small_total[0][None],
        grad_out_own[None],
        small_total[1][None],
        big_sum[2][None],
        small_total[2][None],
        grad_down_own[None],
        small_total[3][None],
        big_sum[4][None],
        small_total[4][None],
        small_total[5][None],
        mask_half,
        class_half,
    )


def solution(mesh):
    placed = (
        P(None, "dp", None),
        P(None, "dp", None),
        P(None, "dp"),
        P(None, "dp"),
        P("section", "dp", None, "head"),
        P("section", None, "head"),
        P("section", "head", "dp"),
        P("section", None),
        P("section", "dp", "head"),
        P("section", "head"),
        P("section", "head", "dp"),
        P("section", None),
        P("section", "dp", None, "head"),
        P("section", None, "head"),
        P("section", "head", None),
        P(),
        P(),
        P(None, "dp", None),
    )
    return jax.shard_map(
        per_device,
        mesh=mesh,
        in_specs=placed,
        out_specs=(
            P("section", None, "dp", None),
            P("section", None, "dp", None),
            P("section", "dp", None, "head"),
            P("section", None, "head"),
            P("section", "head", "dp"),
            P("section", "head"),
            P("section", "dp", "head"),
            P("section", "head"),
            P("section", "head", "dp"),
            P("section", "head"),
            P("section", "dp", None, "head"),
            P("section", None, "head"),
            P("section", "head", None),
            P("head"),
            P(None, "head"),
        ),
        check_vma=False,
    )
```

profile of v0, /device:TPU:0, one launch (start us, length us, event | category | flops | bytes accessed | tf_op | source)
XLA Modules:
  0.0 2348.7 jit_solution(3177631882948478796)
XLA Ops:
  12.5 24.7 %scatter_fusion.1 = s32[2,256]{1,0:T(2,128)S(1)} fusion(s32[2,256]{1,0:T(2,128)S(1)} %broadcast.890, s32[512]{0:T(512)S(1)} %bitcast.763, s32[512]{0:T(512)S(1)} %bitcast.839), kind=kCustom, calls=%fused_computation.7 | custom fusion | bytes 10240 | tf_op jit(solution)/shard_map/vmap()/scatter | solution.py:36
  38.1 24.7 %scatter_fusion = s32[2,256]{1,0:T(2,128)S(1)} fusion(s32[2,256]{1,0:T(2,128)S(1)} %broadcast.880, s32[512]{0:T(512)S(1)} %bitcast.764, s32[512]{0:T(512)S(1)} %bitcast.838), kind=kCustom, calls=%fused_computation.6 | custom fusion | bytes 10240 | tf_op jit(solution)/shard_map/vmap()/scatter | solution.py:38
  70.6 217.0 %gather_fusion.1 = f32[65536,8]{1,0:T(8,128)} fusion(f32[8,511]{0,1:T(8,128)S(1)} %bitcast_convert_fusion, s32[65536]{0:T(1024)S(1)} %broadcast_clamp_fusion), kind=kCustom, calls=%fused_computation.1.clone | custom fusion | bytes 4456448 | tf_op jit(solution)/shard_map/jit(_take)/gather | solution.py:77
  287.6 19.7 copy.105
  308.0 4.2 fusion.109
  312.2 7.2 fusion.10
  323.0 3.8 fusion.6
  326.7 5.3 all-gather.8
  336.7 4.3 fusion.46
  351.9 43.4 %all-reduce.18.cloned.1.call-done = f32[256,1152]{1,0:T(8,128)} async-done(((f32[256,1152]{1,0:T(8,128)}), f32[256,1152]{1,0:T(8,128)}) %all-reduce.18.cloned.1.call-update) | async-done | bytes 1179664 | tf_op jit(solution)/shard_map/psum | solution.py:67
  400.6 84.0 %all-gather.23.cloned.1.call-done = bf16[1,1152,2304]{2,1,0:T(8,128)(2,1)} async-done(((bf16[1,144,2304]{2,1,0:T(8,128)(2,1)}), bf16[1,1152,2304]{2,1,0:T(8,128)(2,1)}) %all-gather.23.cloned.1.call-update) | async-done | bytes 5308432 | tf_op jit(solution)/shard_map/all_gather | solution.py:334
  484.7 5.8 fusion.48
  490.5 81.7 %all-gather.25.cloned.1.call-done = bf16[1,2304,1152]{1,2,0:T(8,128)(2,1)} async-done(((bf16[1,2304,144]{1,2,0:T(8,128)(2,1)}), bf16[1,2304,1152]{1,2,0:T(8,128)(2,1)}) %all-gather.25.cloned.1.call-update) | async-done | bytes 5308432 | tf_op jit(solution)/shard_map/all_gather | solution.py:335
  572.2 6.3 fusion.22
  579.8 4.2 fusion.107
  584.0 4.9 all-gather.9
  589.0 31.2 %all-reduce.20.cloned.1.call-done = f32[256,1152]{1,0:T(8,128)} async-done(((f32[256,1152]{1,0:T(8,128)}), f32[256,1152]{1,0:T(8,128)}) %all-reduce.20.cloned.1.call-update) | async-done | bytes 1179664 | tf_op jit(solution)/shard_map/psum | solution.py:67
  632.7 4.3 fusion.44
  645.1 42.8 %all-reduce.22.cloned.1.call-done = f32[256,1152]{1,0:T(8,128)} async-done(((f32[256,1152]{1,0:T(8,128)}), f32[256,1152]{1,0:T(8,128)}) %all-reduce.22.cloned.1.call-update) | async-done | bytes 1179664 | tf_op jit(solution)/shard_map/psum | solution.py:67
  693.4 4.3 fusion.51
  703.0 4.2 fusion.105
  707.2 4.7 all-gather.10
  712.1 33.8 %all-reduce.24.cloned.1.call-done = f32[256,1152]{1,0:T(8,128)} async-done(((f32[256,1152]{1,0:T(8,128)}), f32[256,1152]{1,0:T(8,128)}) %all-reduce.24.cloned.1.call-update) | async-done | bytes 1179664 | tf_op jit(solution)/shard_map/psum | solution.py:67
  758.5 4.3 fusion.42
  770.9 42.8 %all-reduce.26.cloned.1.call-done = f32[256,1152]{1,0:T(8,128)} async-done(((f32[256,1152]{1,0:T(8,128)}), f32[256,1152]{1,0:T(8,128)}) %all-reduce.26.cloned.1.call-update) | async-done | bytes 1179664 | tf_op jit(solution)/shard_map/psum | solution.py:67
  821.0 4.7 fusion.54
  833.0 43.0 %all-reduce.28.cloned.1.call-done = f32[256,1152]{1,0:T(8,128)} async-done(((f32[256,1152]{1,0:T(8,128)}), f32[256,1152]{1,0:T(8,128)}) %all-reduce.28.cloned.1.call-update) | async-done | bytes 1179664 | tf_op jit(solution)/shard_map/psum | solution.py:71
  878.3 4.0 convert_reduce_fusion.8
  894.2 42.0 %all-reduce.30.cloned.1.call-done = f32[256,1152]{1,0:T(8,128)} async-done(((f32[256,1152]{1,0:T(8,128)}), f32[256,1152]{1,0:T(8,128)}) %all-reduce.30.cloned.1.call-update) | async-done | bytes 1179664 | tf_op jit(solution)/shard_map/psum | solution.py:71
  942.4 4.7 scatter_custom_fusion
  955.9 5.9 convert_reduce_fusion.1
  962.9 5.2 fusion.26
  968.4 42.8 %all-reduce.32.cloned.1.call-done = f32[256,1152]{1,0:T(8,128)} async-done(((f32[256,1152]{1,0:T(8,128)}), f32[256,1152]{1,0:T(8,128)}) %all-reduce.32.cloned.1.call-update) | async-done | bytes 1179664 | tf_op jit(solution)/shard_map/psum | solution.py:71
  1013.9 4.5 convert_reduce_fusion.7
  1029.3 43.0 %all-reduce.34.cloned.1.call-done = f32[256,1152]{1,0:T(8,128)} async-done(((f32[256,1152]{1,0:T(8,128)}), f32[256,1152]{1,0:T(8,128)}) %all-reduce.34.cloned.1.call-update) | async-done | bytes 1179664 | tf_op jit(solution)/shard_map/psum | solution.py:71
  1074.9 3.8 multiply_reduce_fusion.4
  1078.7 4.7 scatter_custom_fusion.1
  1092.2 5.9 convert_reduce_fusion
  1099.2 5.3 fusion.24
  1104.5 6.3 fusion.18
  1110.8 36.7 %all-reduce.36.cloned.1.call-done = f32[256,1152]{1,0:T(8,128)} async-done(((f32[256,1152]{1,0:T(8,128)}), f32[256,1152]{1,0:T(8,128)}) %all-reduce.36.cloned.1.call-update) | async-done | bytes 1179664 | tf_op jit(solution)/shard_map/psum | solution.py:71
  1150.6 4.2 convert_reduce_fusion.6
  1172.0 62.5 %all-reduce.40.cloned.1.call-done = (f32[256,1152]{1,0:T(8,128)}, f32[256,1152]{1,0:T(8,128)}) async-done(((f32[256,1152]{1,0:T(8,128)}, f32[256,1152]{1,0:T(8,128)}), (f32[256,1152]{1,0:T(8,128)}, f32[256,1152]{1,0:T(8,128)})) %all-reduce.40.cloned.1.call-update) | async-done | bytes 2359312 | tf_op jit(solution)/shard_map/psum | solution.py:67
  1259.8 5.4 fusion.320
  1265.4 7.1 fusion.179
  1272.5 7.0 fusion.176
  1279.6 7.0 fusion.173
  1288.8 4.3 fusion.271
  1302.8 5.0 add_add_fusion
  1314.4 5.6 convolution_add_fusion
  1325.7 5.5 convolution_add_fusion.2
  1332.0 9.3 multiply_add_fusion
  1350.2 15.1 rev.9
  1370.7 8.0 reshape.1113
  1388.5 15.1 rev.10
  1409.0 8.4 reshape.1115
  1430.3 15.2 rev.11
  1450.8 8.0 reshape.1117
  1467.2 39.8 %psum.158 = f32[1152]{0:T(1024)S(1)} all-reduce(f32[1152]{0:T(1024)S(1)} %add_multiply_fusion), channel_id=1, replica_groups=mesh['section'=2,'dp'=8,'head'=2] {'section','dp','head'}, use_global_device_ids=true, to_apply=%region_83.86 | all-reduce | flops 1152 | bytes 9216 | tf_op jit(solution)/shard_map/psum | solution.py:441
  1507.6 39.3 %all-reduce.3 = (f32[1,2,576]{2,1,0:T(2,128)}, f32[1,576]{1,0:T(1,128)}, f32[1,2304]{1,0:T(1,128)}, f32[1,576]{1,0:T(1,128)}, f32[1,6,576]{2,0,1:T(1,128)}, /*index=5*/f32[1,8,511]{2,1,0:T(8,128)}) all-reduce(f32[1,2,576]{2,1,0:T(2,128)S(1)} %fusion.273, ...), channel_id=1, replica_groups=mesh['section'=2,'dp'=8,'head'=2] {'dp'}, use_global_device_ids=true, to_apply=%region_58.61 | all-reduce | flops 12152 | bytes 97216 | tf_op jit(solution)/shard_map/psum | solution.py:435
  1556.5 116.8 %reduce-scatter.6.cloned.1.call-done = f32[144,3,576]{2,0,1:T(8,128)} async-done(((f32[1152,3,576]{2,0,1:T(8,128)}), f32[144,3,576]{2,0,1:T(8,128)}) %reduce-scatter.6.cloned.1.call-update) | async-done | bytes 995344 | tf_op jit(solution)/shard_map/reduce_scatter | solution.py:425
  1673.3 183.5 %reduce-scatter.12.cloned.1.call-done = f32[144,2304]{1,0:T(8,128)} async-done(((f32[1152,2304]{1,0:T(8,128)}), f32[144,2304]{1,0:T(8,128)}) %reduce-scatter.12.cloned.1.call-update) | async-done | bytes 1327120 | tf_op jit(solution)/shard_map/reduce_scatter | solution.py:428
  1856.8 183.3 %reduce-scatter.10.cloned.1.call-done = f32[144,2304]{1,0:T(8,128)} async-done(((f32[1152,2304]{1,0:T(8,128)}), f32[144,2304]{1,0:T(8,128)}) %reduce-scatter.10.cloned.1.call-update) | async-done | bytes 1327120 | tf_op jit(solution)/shard_map/reduce_scatter | solution.py:427
  2040.1 301.4 %reduce-scatter.14.cloned.1.call-done = f32[144,6,576]{2,0,1:T(8,128)} async-done(((f32[1152,6,576]{2,0,1:T(8,128)}), f32[144,6,576]{2,0,1:T(8,128)}) %reduce-scatter.14.cloned.1.call-update) | async-done | bytes 1990672 | tf_op jit(solution)/shard_map/reduce_scatter | solution.py:429
  (794 shorter events, 298.2 us)
Async XLA Ops:
  7.2 56.5 %copy-start = (bf16[1000,1152]{1,0:T(8,128)(2,1)S(1)}, bf16[1000,1152]{1,0:T(8,128)(2,1)}, u32[]{:S(2)}) copy-start(bf16[1000,1152]{1,0:T(8,128)(2,1)} %param.44) | copy-start | bytes 6912004
  7.2 5.2 copy-start.214
  7.2 305.0 %all-gather.17.cloned.1.call-start = ((), (), s32[]{:S(2)}) async-start(), calls=%async_computation.21 | async-start | bytes 9953280 | tf_op jit(solution)/shard_map/all_gather | solution.py:336
  8.0 328.8 %all-gather.19.cloned.1.call-start = ((), (), s32[]{:S(2)}) async-start(), calls=%async_computation.22 | async-start | bytes 4976640 | tf_op jit(solution)/shard_map/all_gather | solution.py:332
  8.7 338.0 %all-gather.21.cloned.1.call-start = ((), (), s32[]{:S(2)}) async-start(), calls=%async_computation.23 | async-start | bytes 1658880 | tf_op jit(solution)/shard_map/all_gather | solution.py:333
  9.4 385.9 %all-reduce.18.cloned.1.call-start = ((), (), s32[]{:S(2)}) async-start(), calls=%async_computation.5 | async-start | bytes 2359296 | tf_op jit(solution)/shard_map/psum | solution.py:67
  11.8 340.0 %copy-start.203 = (s32[1,256]{1,0:T(1,128)}, s32[1,256]{1,0:T(1,128)S(1)}, u32[]{:S(2)}) copy-start(s32[1,256]{1,0:T(1,128)S(1)} %get-tuple-element.162) | copy-start | bytes 3076
  12.5 25.4 %copy-start.207 = (bf16[1,2,576]{2,1,0:T(2,128)(2,1)S(1)}, bf16[1,2,576]{2,1,0:T(2,128)(2,1)}, u32[]{:S(2)}) copy-start(bf16[1,2,576]{2,1,0:T(2,128)(2,1)} %param.33) | copy-start | bytes 6916
  38.1 25.4 %copy-start.200 = (bf16[1152]{0:T(1024)(128)(2,1)S(1)}, bf16[1152]{0:T(1024)(128)(2,1)}, u32[]{:S(2)}) copy-start(bf16[1152]{0:T(1024)(128)(2,1)} %param.43) | copy-start | bytes 6916
  38.1 25.6 %copy-start.208 = (s32[2,1]{0,1:T(1,128)S(1)}, s32[2,1]{0,1:T(1,128)}, u32[]{:S(2)}) copy-start(s32[2,1]{0,1:T(1,128)} %param.31) | copy-start | bytes 28
  62.9 278.9 %copy-start.167 = (s32[256]{0:T(256)}, s32[256]{0:T(256)S(1)}, u32[]{:S(2)}) copy-start(s32[256]{0:T(256)S(1)} %broadcast_select_fusion.12) | copy-start | bytes 3076
  63.5 1172.5 %copy-start.103 = (f32[1152]{0:T(1024)}, f32[1152]{0:T(1024)S(1)}, u32[]{:S(2)}) copy-start(f32[1152]{0:T(1024)S(1)} %convert_element_type.413) | copy-start | bytes 13828
  66.9 265.7 %copy-start.24 = (bf16[256,1152]{1,0:T(8,128)(2,1)}, bf16[256,1152]{1,0:T(8,128)(2,1)S(1)}, u32[]{:S(2)}) copy-start(bf16[256,1152]{1,0:T(8,128)(2,1)S(1)} %gather_fusion) | copy-start | bytes 1769476
  312.2 7.2 copy-start.2
  350.5 44.8 %copy-start.25 = (bf16[256,1152]{1,0:T(8,128)(2,1)S(1)}, bf16[256,1152]{1,0:T(8,128)(2,1)}, u32[]{:S(2)}) copy-start(bf16[256,1152]{1,0:T(8,128)(2,1)} %copy-done.24) | copy-start | bytes 1769476
  350.5 134.1 %all-gather.23.cloned.1.call-start = ((), (), s32[]{:S(2)}) async-start(), calls=%async_computation.24 | async-start | bytes 5971968 | tf_op jit(solution)/shard_map/all_gather | solution.py:334
  351.1 221.1 %all-gather.25.cloned.1.call-start = ((), (), s32[]{:S(2)}) async-start(), calls=%async_computation.25 | async-start | bytes 5971968 | tf_op jit(solution)/shard_map/all_gather | solution.py:335
  351.7 268.5 %all-reduce.20.cloned.1.call-start = ((), (), s32[]{:S(2)}) async-start(), calls=%async_computation.6 | async-start | bytes 2359296 | tf_op jit(solution)/shard_map/psum | solution.py:67
  351.8 132.8 %copy-start.188 = (f32[2304]{0:T(1024)}, f32[2304]{0:T(1024)S(1)}, u32[]{:S(2)}) copy-start(f32[2304]{0:T(1024)S(1)} %convert_reduce_fusion.15) | copy-start | bytes 27652
  397.4 222.8 %copy-start.14 = (f32[256,1152]{1,0:T(8,128)}, f32[256,1152]{1,0:T(8,128)S(1)}, u32[]{:S(2)}) copy-start(f32[256,1152]{1,0:T(8,128)S(1)} %get-tuple-element.129) | copy-start | bytes 3538948
  490.5 88.6 %copy-start.194 = (bf16[1,1152]{1,0:T(2,128)(2,1)S(1)}, bf16[1,1152]{1,0:T(2,128)(2,1)}, u32[]{:S(2)}) copy-start(bf16[1,1152]{1,0:T(2,128)(2,1)} %param.39) | copy-start | bytes 6916
  490.5 89.2 %copy-start.204 = (s32[1,256]{1,0:T(1,128)S(1)}, s32[1,256]{1,0:T(1,128)}, u32[]{:S(2)}) copy-start(s32[1,256]{1,0:T(1,128)} %copy-done.203) | copy-start | bytes 3076
  490.5 89.2 %copy-start.205 = (s32[1,256]{1,0:T(1,128)S(1)}, s32[1,256]{1,0:T(1,128)}, u32[]{:S(2)}) copy-start(s32[1,256]{1,0:T(1,128)} %get-tuple-element.159) | copy-start | bytes 3076
  490.5 89.2 %copy-start.197 = (s32[1,256]{1,0:T(1,128)S(1)}, s32[1,256]{1,0:T(1,128)}, u32[]{:S(2)}) copy-start(s32[1,256]{1,0:T(1,128)} %get-tuple-element.165) | copy-start | bytes 3076
  490.5 89.2 %copy-start.198 = (s32[256]{0:T(256)S(1)}, s32[256]{0:T(256)}, u32[]{:S(2)}) copy-start(s32[256]{0:T(256)} %get-tuple-element.204) | copy-start | bytes 3076
  578.5 109.3 %all-reduce.22.cloned.1.call-start = ((), (), s32[]{:S(2)}) async-start(), calls=%async_computation.7 | async-start | bytes 2359296 | tf_op jit(solution)/shard_map/psum | solution.py:67
  579.7 58.2 %copy-start.169 = (s32[256]{0:T(256)}, s32[256]{0:T(256)S(1)}, u32[]{:S(2)}) copy-start(s32[256]{0:T(256)S(1)} %broadcast_select_fusion.10) | copy-start | bytes 3076
  589.0 36.0 %copy-start.196 = (f32[1,256]{1,0:T(1,128)S(1)}, f32[1,256]{1,0:T(1,128)}, u32[]{:S(2)}) copy-start(f32[1,256]{1,0:T(1,128)} %get-tuple-element.164) | copy-start | bytes 3076
  623.2 5.1 collective-permute-start
  644.8 101.0 %all-reduce.24.cloned.1.call-start = ((), (), s32[]{:S(2)}) async-start(), calls=%async_computation.8 | async-start | bytes 2359296 | tf_op jit(solution)/shard_map/psum | solution.py:67
  690.2 55.7 %copy-start.17 = (f32[256,1152]{1,0:T(8,128)}, f32[256,1152]{1,0:T(8,128)S(1)}, u32[]{:S(2)}) copy-start(f32[256,1152]{1,0:T(8,128)S(1)} %get-tuple-element.122) | copy-start | bytes 3538948
  690.5 8.7 slice-start.9
  693.4 5.7 slice-start.10
  702.3 111.4 %all-reduce.26.cloned.1.call-start = ((), (), s32[]{:S(2)}) async-start(), calls=%async_computation.9 | async-start | bytes 2359296 | tf_op jit(solution)/shard_map/psum | solution.py:67
  702.4 61.2 %copy-start.171 = (s32[256]{0:T(256)}, s32[256]{0:T(256)S(1)}, u32[]{:S(2)}) copy-start(s32[256]{0:T(256)S(1)} %broadcast_select_fusion.8) | copy-start | bytes 3076
  748.8 5.3 collective-permute-start.1
  770.6 105.3 %all-reduce.28.cloned.1.call-start = ((), (), s32[]{:S(2)}) async-start(), calls=%async_computation.10 | async-start | bytes 2359296 | tf_op jit(solution)/shard_map/psum | solution.py:71
  816.0 429.6 %copy-start.12 = (f32[256,1152]{1,0:T(8,128)}, f32[256,1152]{1,0:T(8,128)S(1)}, u32[]{:S(2)}) copy-start(f32[256,1152]{1,0:T(8,128)S(1)} %get-tuple-element.115) | copy-start | bytes 3538948
  817.7 8.0 slice-start.11
  821.0 9.2 slice-start.13
  832.9 103.2 %all-reduce.30.cloned.1.call-start = ((), (), s32[]{:S(2)}) async-start(), calls=%async_computation.11 | async-start | bytes 2359296 | tf_op jit(solution)/shard_map/psum | solution.py:71
  893.1 118.1 %all-reduce.32.cloned.1.call-start = ((), (), s32[]{:S(2)}) async-start(), calls=%async_computation.12 | async-start | bytes 2359296 | tf_op jit(solution)/shard_map/psum | solution.py:71
  949.2 4.2 collective-permute-start.2
  950.5 5.4 copy-start.127
  955.9 6.0 copy-start.105
  968.2 104.1 %all-reduce.34.cloned.1.call-start = ((), (), s32[]{:S(2)}) async-start(), calls=%async_computation.13 | async-start | bytes 2359296 | tf_op jit(solution)/shard_map/psum | solution.py:71
  1029.2 118.3 %all-reduce.36.cloned.1.call-start = ((), (), s32[]{:S(2)}) async-start(), calls=%async_computation.14 | async-start | bytes 2359296 | tf_op jit(solution)/shard_map/psum | solution.py:71
  1085.5 4.2 collective-permute-start.3
  1092.2 5.9 copy-start.107
  1104.5 130.0 %all-reduce.40.cloned.1.call-start = ((), (), s32[]{:S(2)}) async-start(), calls=%async_computation.26 | async-start | bytes 4718592 | tf_op jit(solution)/shard_map/psum | solution.py:67
  1165.5 387.6 %all-reduce.38.cloned.1.call-start = ((), (), s32[]{:S(2)}) async-start(), calls=%async_computation.20 | async-start | bytes 9437184 | tf_op jit(solution)/shard_map/psum | solution.py:441
  1250.9 14.4 slice-start
  1254.4 10.9 slice-start.1
  1257.4 7.9 slice-start.2
  1265.4 7.1 copy-start.159
  1272.5 7.0 copy-start.163
  1279.5 7.0 copy-start.161
  1279.5 9.3 copy-start.209
  1293.2 263.3 %reduce-scatter.8.cloned.1.call-start = ((), (), s32[]{:S(2)}) async-start(), calls=%async_computation.16 | async-start | bytes 3317760 | tf_op jit(solution)/shard_map/reduce_scatter | solution.py:426
  1298.4 374.9 %reduce-scatter.6.cloned.1.call-start = ((), (), s32[]{:S(2)}) async-start(), calls=%async_computation.15 | async-start | bytes 9953280 | tf_op jit(solution)/shard_map/reduce_scatter | solution.py:425
  1307.9 549.0 %reduce-scatter.12.cloned.1.call-start = ((), (), s32[]{:S(2)}) async-start(), calls=%async_computation.18 | async-start | bytes 11943936 | tf_op jit(solution)/shard_map/reduce_scatter | solution.py:428
  1320.1 720.0 %reduce-scatter.10.cloned.1.call-start = ((), (), s32[]{:S(2)}) async-start(), calls=%async_computation.17 | async-start | bytes 11943936 | tf_op jit(solution)/shard_map/reduce_scatter | solution.py:427
  1331.3 1010.3 %reduce-scatter.14.cloned.1.call-start = ((), (), s32[]{:S(2)}) async-start(), calls=%async_computation.19 | async-start | bytes 19906560 | tf_op jit(solution)/shard_map/reduce_scatter | solution.py:429
  1549.9 791.7 %copy-start.1 = (bf16[1000,1152]{1,0:T(8,128)(2,1)S(1)}, bf16[1000,1152]{1,0:T(8,128)(2,1)}, u32[]{:S(2)}) copy-start(bf16[1000,1152]{1,0:T(8,128)(2,1)} %param.44) | copy-start | bytes 6912004
  (192 other events, 445.7 us)
Sparse Core Ops, SparseCore 0:
  10.3 133.4 all-gather.16
  146.0 74.4 all-gather.18
  222.7 41.6 all-gather.20
  350.7 44.5 all-reduce.17
  397.6 87.0 all-gather.22
  486.9 85.2 all-gather.24
  578.7 41.5 all-reduce.19
  644.9 42.8 all-reduce.21
  702.4 43.3 all-reduce.23
  770.8 42.9 all-reduce.25
  833.0 42.8 all-reduce.27
  893.2 42.9 all-reduce.29
  968.3 42.8 all-reduce.31
  1029.3 42.9 all-reduce.33
  1104.6 42.8 all-reduce.35
  1165.7 68.8 all-reduce.39
  1293.3 144.8 all-reduce.37
  1442.2 71.5 reduce-scatter.7
  1518.5 154.8 reduce-scatter.5
  1677.8 179.0 reduce-scatter.11
  1861.0 179.0 reduce-scatter.9
  2045.2 296.3 reduce-scatter.13
where the time goes:
time: 2360 us; the launch traced here: 2350 us
  waiting for transfers between devices  1420 us (60%)
  local copies, waits for them, and re-layouts  443 us (19%)
  matrix products  213 us (9%)
  other arithmetic  147 us (6%)
  blocking collectives  93.9 us (4%)
    reduce_scatter x1, waiting for transfers between devices, per_device(): lax.psum_scatter(big_sum[4], 'dp', scatter_dimension=0, tiled=True)  301 us
    psum x6, waiting for transfers between devices, head_total(): return lax.psum(partial_sum, 'head')  257 us
    gather x2, local copies, waits for them, and re-layouts, rel_bias(): skewed = jnp.take(rel_local, grid_index, axis=1)  237 us
    psum x5, waiting for transfers between devices, head_back(): return lax.psum(partial_sum, 'head')  208 us
    reduce_scatter x1, waiting for transfers between devices, per_device(): lax.psum_scatter(big_sum[3], 'dp', scatter_dimension=0, tiled=True)  184 us
    reduce_scatter x1, waiting for transfers between devices, per_device(): lax.psum_scatter(big_sum[2], 'dp', scatter_dimension=0, tiled=True)  183 us
    reduce_scatter x1, waiting for transfers between devices, per_device(): lax.psum_scatter(big_sum[0], 'dp', scatter_dimension=0, tiled=True)  117 us
    all_gather x1, waiting for transfers between devices, per_device(): lax.all_gather(w_up[0], 'dp', axis=0, tiled=True)  84 us
  transfers between devices with their start and end apart: 26, of which 19 were waited for; matrix products, arithmetic and copies ran while one was open for 23% of the time, Pallas kernels for 0%

commit v1 on v0

v1 whole, which is shorter than its diff:
```python
import math

import jax
import jax.numpy as jnp
from jax import lax
from jax.experimental import pallas as pl
from jax.experimental.pallas import tpu as pltpu
from jax.sharding import PartitionSpec as P

PRECISE = lax.Precision.HIGHEST
EPSILON = 1e-06
NEGATIVE = -1e30
MESH = pl.DeviceIdType.MESH
BF = jnp.bfloat16
F32 = jnp.float32


def time_features(step_ids, model_width):
    half_width = model_width // 2
    frequency = jnp.exp(-math.log(10000.0) * jnp.arange(half_width).astype(F32) / half_width)
    angles = step_ids.astype(F32)[..., None] * frequency
    return jnp.concatenate([jnp.cos(angles), jnp.sin(angles)], axis=-1)


def swap(value, axis):
    return lax.ppermute(value, axis, [(0, 1), (1, 0)])


def pick(index, first, second):
    return jnp.where(index == 0, first, second)


def gather_kernel(chain, x_ref, w_ref, ssem, rsem, lsem):
    pieces = x_ref.shape[0]
    core = lax.axis_index("section")
    dp = lax.axis_index("dp")
    head = lax.axis_index("head")
    z = dp // 2
    y = dp % 2
    mate = z + 1 - 2 * (z % 2)

    def device(c, zz, yy):
        return (c, zz * 2 + yy, head)

    barrier = pltpu.get_barrier_semaphore()

    @pl.when(z < chain - 1)
    def _():
        pl.semaphore_signal(barrier, inc=1, device_id=device(core, z + 1, y), device_id_type=MESH)

    @pl.when(z > 0)
    def _():
        pl.semaphore_signal(barrier, inc=1, device_id=device(core, z - 1, y), device_id_type=MESH)

    pl.semaphore_signal(barrier, inc=1, device_id=device(core, z, 1 - y), device_id_type=MESH)
    pl.semaphore_signal(barrier, inc=1, device_id=device(1 - core, z, y), device_id_type=MESH)

    @pl.when((z > 0) & (z < chain - 1))
    def _():
        pl.semaphore_wait(barrier, 4)

    @pl.when((z == 0) | (z == chain - 1))
    def _():
        pl.semaphore_wait(barrier, 3)

    def block(p, zz, yy):
        return w_ref.at[p, core, zz * 2 + yy]

    def remote(src, dst, p, kind, target):
        return pltpu.make_async_remote_copy(
            src_ref=src,
            dst_ref=dst,
            send_sem=ssem.at[p, kind],
            recv_sem=rsem.at[p, kind],
            device_id=target,
            device_id_type=MESH,
        )

    def up(p, k):
        b = block(p, z - (k - 1), y)
        return remote(x_ref.at[p] if k == 1 else b, b, p, k - 1, device(core, z + 1, y))

    def up_in(p, k):
        b = block(p, z - k, y)
        return remote(b, b, p, k - 1, device(core, z - 1, y))

    def down(p, k):
        b = block(p, z + (k - 1), y)
        return remote(
            x_ref.at[p] if k == 1 else b, b, p, chain + k - 1, device(core, z - 1, y)
        )

    def down_in(p, k):
        b = block(p, z + k, y)
        return remote(b, b, p, chain + k - 1, device(core, z + 1, y))

    def across(p, zz, own=False):
        b = block(p, zz, y)
        return remote(x_ref.at[p] if own else b, b, p, 2 * chain + zz, device(core, z, 1 - y))

    def across_in(p, zz):
        b = block(p, zz, 1 - y)
        return remote(b, b, p, 2 * chain + zz, device(core, z, 1 - y))

    def mate_out(p):
        b = block(p, z, 1 - y)
        return remote(b, b, p, 3 * chain, device(core, mate, y))

    def mate_in(p):
        b = block(p, mate, 1 - y)
        return remote(b, b, p, 3 * chain, device(core, mate, y))

    def other_out(p):
        return remote(
            w_ref.at[p, core], w_ref.at[p, core], p, 3 * chain + 1, device(1 - core, z, y)
        )

    def other_in(p):
        return remote(
            w_ref.at[p, 1 - core], w_ref.at[p, 1 - core], p, 3 * chain + 1, device(1 - core, z, y)
        )

    def local(p):
        return pltpu.make_async_copy(x_ref.at[p], block(p, z, y), lsem.at[p])

    def by_mate(p):
        return p % 2 == 1

    def start(p):
        local(p).start()
        across(p, z, True).start()

        @pl.when(z < chain - 1)
        def _():
            up(p, 1).start()

        @pl.when(z > 0)
        def _():
            down(p, 1).start()

    def step(p, k):
        @pl.when(z >= k)
        def _():
            up_in(p, k).wait_recv()

            @pl.when(z < chain - 1)
            def _():
                up(p, k + 1).start()

            if k == 1 and by_mate(p):

                @pl.when(z % 2 == 0)
                def _():
                    across(p, z - k).start()

            else:
                across(p, z - k).start()

        @pl.when(z + k < chain)
        def _():
            down_in(p, k).wait_recv()

            @pl.when(z > 0)
            def _():
                down(p, k + 1).start()

            if k == 1 and by_mate(p):

                @pl.when(z % 2 == 1)
                def _():
                    across(p, z + k).start()

            else:
                across(p, z + k).start()

    def finish(p):
        local(p).wait()
        for j in range(chain):
            if by_mate(p):

                @pl.when((j != z) & (j != mate))
                def _():
                    across_in(p, j).wait_recv()

            else:
                across_in(p, j).wait_recv()
        if by_mate(p):
            mate_in(p).wait_recv()
        other_out(p).start()

    def drain(p):
        for j in range(chain):
            if by_mate(p):

                @pl.when(j != mate)
                def _():
                    across(p, j).wait_send()

            else:
                across(p, j).wait_send()
        if by_mate(p):
            mate_out(p).wait_send()
        for k in range(1, chain):

            @pl.when((z < chain - 1) & (z >= k - 1))
            def _():
                up(p, k).wait_send()

            @pl.when((z > 0) & (z + k - 1 < chain))
            def _():
                down(p, k).wait_send()

        other_out(p).wait_send()
        other_in(p).wait_recv()

    ahead = min(2, pieces)
    for p in range(ahead):
        start(p)
    for p in range(pieces):
        step(p, 1)
        if by_mate(p):
            across_in(p, z).wait_recv()
            mate_out(p).start()
        if p + ahead < pieces:
            start(p + ahead)
        for k in range(2, chain):
            step(p, k)
        if p > 0:
            finish(p - 1)
    finish(pieces - 1)
    for p in range(pieces):
        drain(p)


def gather_pieces(x, dp_count):
    pieces, rows, cols = x.shape
    chain = dp_count // 2
    kinds = 3 * chain + 2

    def body(*refs):
        gather_kernel(chain, *refs)

    return pl.pallas_call(
        body,
        out_shape=jax.ShapeDtypeStruct((pieces, 2, dp_count, rows, cols), x.dtype),
        in_specs=[pl.BlockSpec(memory_space=pl.ANY)],
        out_specs=pl.BlockSpec(memory_space=pl.ANY),
        scratch_shapes=[
            pltpu.SemaphoreType.DMA((pieces, kinds)),
            pltpu.SemaphoreType.DMA((pieces, kinds)),
            pltpu.SemaphoreType.DMA((pieces,)),
        ],
        compiler_params=pltpu.CompilerParams(collective_id=0, has_side_effects=True),
        name="gather_weights",
    )(x)


def normalize(values_in):
    centered = values_in - jnp.mean(values_in, axis=-1, keepdims=True)
    inverse = lax.rsqrt(jnp.mean(centered * centered, axis=-1, keepdims=True) + EPSILON)
    return (centered * inverse, inverse)


def norm_back(grad_hat, normed, inverse):
    return inverse * (
        grad_hat
        - jnp.mean(grad_hat, axis=-1, keepdims=True)
        - normed * jnp.mean(grad_hat * normed, axis=-1, keepdims=True)
    )


GELU_SCALE = math.sqrt(2.0 / math.pi)


def gelu_both(v):
    inner = GELU_SCALE * (v + 0.044715 * v * v * v)
    t = jnp.tanh(inner)
    slope = 0.5 * (1.0 + t) + 0.5 * v * (1.0 - t * t) * GELU_SCALE * (1.0 + 3 * 0.044715 * v * v)
    return 0.5 * v * (1.0 + t), slope


def nn(a, b):
    return lax.dot_general(a, b, (((1,), (0,)), ((), ())), preferred_element_type=F32)


def nt(a, b):
    return lax.dot_general(a, b, (((1,), (1,)), ((), ())), preferred_element_type=F32)


def tn(a, b):
    return lax.dot_general(a, b, (((0,), (0,)), ((), ())), preferred_element_type=F32)


def head_sum(partial_sum):
    own = partial_sum.astype(BF)
    return own.astype(F32) + swap(own, "head").astype(F32)


def forward(x, mod, wa, wu, wd, b_qv, b_out, b_up, b_down, bias, heads, head_dim):
    hw = heads // 2 * head_dim
    scale = 1.0 / math.sqrt(head_dim)
    hat1, inv1 = normalize(x)
    n1 = (hat1 * (1.0 + mod[1]) + mod[0]).astype(BF)
    branch = 0.0
    q, k, v, o, p = [], [], [], [], []
    for half in range(2):
        r = nn(n1, wa[half][:, hw:])
        bq = b_qv[0, half * hw : (half + 1) * hw]
        bv = b_qv[1, half * hw : (half + 1) * hw]
        q.append((r[:, :hw] + bq).astype(BF))
        k.append(r[:, hw : 2 * hw].astype(BF))
        v.append((r[:, 2 * hw :] + bv).astype(BF))
        outs = []
        for i in range(heads // 2):
            at = slice(i * head_dim, (i + 1) * head_dim)
            z = nt(q[half][:, at], k[half][:, at]) * scale + bias[half * heads // 2 + i]
            e = jnp.exp(z - jnp.max(z, axis=-1, keepdims=True))
            probs = (e / jnp.sum(e, axis=-1, keepdims=True)).astype(BF)
            p.append(probs)
            outs.append(nn(probs, v[half][:, at]).astype(BF))
        o.append(jnp.concatenate(outs, axis=1))
        branch = branch + nt(o[half], wa[half][:, :hw])
    branch = head_sum(branch) + b_out
    xm = x + mod[2] * branch
    hat2, inv2 = normalize(xm)
    n2 = (hat2 * (1.0 + mod[4]) + mod[3]).astype(BF)
    y = 0.0
    hidden, slope = [], []
    for half in range(2):
        hp = nn(n2, wu[half]) + b_up[half * wu.shape[2] : (half + 1) * wu.shape[2]]
        value, sl = gelu_both(hp)
        hidden.append(value.astype(BF))
        slope.append(sl)
        y = y + nt(hidden[half], wd[half])
    y = head_sum(y) + b_down
    out = xm + mod[5] * y
    return out, (hat1, inv1, n1, q, k, v, p, o, branch, hat2, inv2, n2, hidden, slope, y)


def both(value):
    c = lax.axis_index("section")
    got = swap(value, "section")
    return pick(c, value, got), pick(c, got, value)


def mine(c, pair):
    return pick(c, pair[0], pair[1])


def paired(lhs, rhs_halves):
    c = lax.axis_index("section")
    lhs_all = jnp.concatenate([lhs, swap(lhs, "section")], axis=0)
    got = swap(mine(1 - c, rhs_halves), "section")
    rhs_all = jnp.concatenate([mine(c, rhs_halves), got], axis=0)
    return tn(lhs_all, rhs_all).astype(BF)


def backward(d, mod, wa, wu, wd, kept, heads, head_dim):
    hat1, inv1, n1, q, k, v, p, o, branch, hat2, inv2, n2, hidden, slope, y = kept
    hw = heads // 2 * head_dim
    scale = 1.0 / math.sqrt(head_dim)
    dy = (d * mod[5]).astype(BF)
    g_gate2 = jnp.sum(d * y, axis=0)
    g_b_down = jnp.sum(dy.astype(F32), axis=0)
    dpre = [(nn(dy, wd[half]) * slope[half]).astype(BF) for half in range(2)]
    g_b_up = jnp.concatenate([jnp.sum(v_.astype(F32), axis=0) for v_ in dpre])
    dn2 = head_sum(nt(dpre[0], wu[0]) + nt(dpre[1], wu[1]))
    g_d = paired(dy, hidden)
    g_u = paired(n2, dpre)
    dxm = d + norm_back(dn2 * (1.0 + mod[4]), hat2, inv2)
    g_shift2 = jnp.sum(dn2, axis=0)
    g_scale2 = jnp.sum(dn2 * hat2, axis=0)
    g_gate1 = jnp.sum(dxm * branch, axis=0)
    dattn = (dxm * mod[2]).astype(BF)
    g_b_out = jnp.sum(dattn.astype(F32), axis=0)
    dn1 = 0.0
    dqkv, dz_all = [], []
    for half in range(2):
        do = nn(dattn, wa[half][:, :hw]).astype(BF)
        dq, dk, dv = [], [], []
        for i in range(heads // 2):
            at = slice(i * head_dim, (i + 1) * head_dim)
            probs = p[half * heads // 2 + i]
            dv.append(tn(probs, do[:, at]).astype(BF))
            ds = nt(do[:, at], v[half][:, at])
            pf = probs.astype(F32)
            dz = (pf * (ds - jnp.sum(pf * ds, axis=-1, keepdims=True))).astype(BF)
            dz_all.append(dz)
            dq.append((nn(dz, k[half][:, at]) * scale).astype(BF))
            dk.append((tn(dz, q[half][:, at]) * scale).astype(BF))
        dqkv.append(jnp.concatenate(dq + dk + dv, axis=1))
        dn1 = dn1 + nt(dqkv[half], wa[half][:, hw:])
    dn1 = head_sum(dn1)
    g_a = jnp.concatenate([paired(dattn, o), paired(n1, dqkv)], axis=1)
    sums = [jnp.sum(v_.astype(F32), axis=0) for v_ in dqkv]
    g_b_qv = jnp.concatenate([sums[0][:hw], sums[1][:hw], sums[0][2 * hw :], sums[1][2 * hw :]])
    dx = dxm + norm_back(dn1 * (1.0 + mod[1]), hat1, inv1)
    dmod = jnp.stack(
        [jnp.sum(dn1, axis=0), jnp.sum(dn1 * hat1, axis=0), g_gate1, g_shift2, g_scale2, g_gate2]
    )
    return dx, (g_a, g_u, g_d), (g_b_qv, g_b_out, g_b_up, g_b_down), dmod, dz_all


def toeplitz(rel, length):
    span = jnp.arange(length, dtype=jnp.int32)
    return jnp.take(rel, span[:, None] - span[None, :] + length - 1, axis=1)


def diagonals(square, length):
    heads = square.shape[0]
    padded = jnp.pad(square[:, :, ::-1], ((0, 0), (0, 0), (0, length)))
    flat = padded.reshape(heads, 2 * length * length)[:, : length * (2 * length - 1)]
    return jnp.sum(flat.reshape(heads, length, 2 * length - 1), axis=1)


def per_device(
    tokens,
    kept_mask,
    timesteps,
    labels,
    w_qkv,
    b_qv,
    w_out,
    b_out,
    w_up,
    b_up,
    w_down,
    b_down,
    w_ada,
    b_ada,
    rel_table,
    mask_token,
    class_table,
    out_grad,
):
    micro, rows, width = tokens.shape
    length = kept_mask.shape[2]
    classes = class_table.shape[0]
    heads = rel_table.shape[1]
    lw = w_qkv.shape[3]
    head_dim = lw // heads
    hw = lw // 2
    ff = w_up.shape[2]
    fw = ff // 2
    dp_count = lax.axis_size("dp")
    c = lax.axis_index("section")
    dp = lax.axis_index("dp")
    h = lax.axis_index("head")

    qkv = jnp.transpose(w_qkv[0], (1, 0, 2))
    out_t = w_out[0].T
    down_t = w_down[0].T
    pack = []
    for half in range(2):
        at = slice(half * hw, (half + 1) * hw)
        fat = slice(half * fw, (half + 1) * fw)
        a = jnp.concatenate([out_t[:, at], qkv[0][:, at], qkv[1][:, at], qkv[2][:, at]], axis=1)
        pack.append(jnp.stack([a, w_up[0][:, fat], down_t[:, fat]]))
    keep = mine(c, pack)
    got = swap(mine(1 - c, pack), "section")
    own = jnp.concatenate([pick(c, keep, got), pick(c, got, keep)])
    full = gather_pieces(own, dp_count)
    full = full.reshape(2, 3, 2, width, own.shape[2])

    ids = lax.all_gather(jnp.stack([labels[:, 0], timesteps[:, 0]]), "dp")
    labels_all = ids[:, 0].reshape(-1)
    steps_all = ids[:, 1].reshape(-1)
    label_pick = (labels_all[:, None] == jnp.arange(classes)[None, :]).astype(BF)
    cond = nn(label_pick, class_table) + time_features(steps_all, width)
    cond_low = jax.nn.silu(cond)
    fr = width // dp_count
    cond_part = lax.dynamic_slice_in_dim(cond_low, dp * fr, fr, 1)
    ada = w_ada[0].astype(F32).reshape(fr, 6 * lw)
    part = jnp.dot(cond_part, ada, precision=PRECISE).reshape(dp_count, micro, 6, lw)
    summed = jnp.sum(lax.all_to_all(part, "dp", 0, 0, tiled=True), axis=0) + b_ada[0].astype(F32)
    mod_own = mine(c, summed)
    mod_got = swap(mine(1 - c, summed), "section")
    mod_half = jnp.stack([pick(c, mod_own, mod_got), pick(c, mod_got, mod_own)])
    mod_other = swap(mod_half, "head")
    mod = jnp.concatenate(
        [pick(h, mod_half, mod_other), pick(h, mod_other, mod_half)], axis=2
    )

    def shared(value):
        return both(value[0].astype(BF))

    b_qv2, b_out2, b_up2, b_down2, rel2 = [
        [v.astype(F32) for v in shared(t)] for t in (b_qv, b_out, b_up, b_down, rel_table)
    ]

    kept = kept_mask[c, 0]
    source = jnp.cumsum(kept) - 1
    count = jnp.sum(kept)
    span = jnp.arange(length, dtype=jnp.int32)
    place = ((kept[:, None] == 1) & (source[:, None] == span[None, :])).astype(BF)
    pad = span >= count
    pos = place.T + (pad[:, None] & (span[None, :] == 0)).astype(BF)
    same = pad[:, None] == pad[None, :]
    t0 = toeplitz(rel2[0], length).astype(BF)
    left = jnp.einsum("ri,hij->hrj", pos, t0, preferred_element_type=F32).astype(BF)
    bias0 = jnp.einsum("hrj,sj->hrs", left, pos, preferred_element_type=F32)
    bias0 = jnp.where(same[None], bias0, NEGATIVE)
    bias1 = toeplitz(rel2[1], length)

    def weights(s):
        return full[s, 0], full[s, 1], full[s, 2]

    x0 = tokens[c].astype(F32)
    e, saved0 = forward(
        x0, mod[0], *weights(0), b_qv2[0], b_out2[0], b_up2[0], b_down2[0], bias0, heads, head_dim
    )
    placed = nn(place, e.astype(BF)) + (1 - kept)[:, None] * mask_token.astype(F32)[None, :]
    out1, saved1 = forward(
        placed, mod[1], *weights(1), b_qv2[1], b_out2[1], b_up2[1], b_down2[1], bias1, heads, head_dim
    )
    d = out_grad[c].astype(F32)
    da, big1, small1, dmod1, dz1 = backward(d, mod[1], *weights(1), saved1, heads, head_dim)
    mask_sum = jnp.sum(da * (1 - kept)[:, None].astype(F32), axis=0)
    de = tn(place, da.astype(BF))
    dtok, big0, small0, dmod0, dz0 = backward(de, mod[0], *weights(0), saved0, heads, head_dim)
    rel1 = diagonals(jnp.stack(dz1).astype(F32), length)
    sq = jnp.einsum("ri,hrs->his", pos, jnp.stack(dz0), preferred_element_type=F32)
    sq = jnp.einsum("his,sj->hij", sq, pos.astype(F32), precision=PRECISE)
    rel0 = diagonals(sq, length)

    red = []
    for s, big in ((1, big1), (0, big0)):
        red.append([lax.psum_scatter(t, "dp", scatter_dimension=0, tiled=True) for t in big])
    red = jnp.stack([jnp.stack(red[1]), jnp.stack(red[0])]).astype(F32)
    g_own = mine(c, red)
    g_got = swap(mine(1 - c, red), "section")
    g0, g1 = pick(c, g_own, g_got), pick(c, g_got, g_own)
    g_qkv = jnp.stack(
        [
            jnp.concatenate([g0[0][:, i * hw : (i + 1) * hw], g1[0][:, i * hw : (i + 1) * hw]], axis=1)
            for i in (1, 2, 3)
        ],
        axis=1,
    )
    g_out = jnp.concatenate([g0[0][:, :hw], g1[0][:, :hw]], axis=1).T
    g_up = jnp.concatenate([g0[1], g1[1]], axis=1)
    g_down = jnp.concatenate([g0[2], g1[2]], axis=1).T

    half_w = width // 2

    def half(v):
        return lax.dynamic_slice_in_dim(v, h * half_w, half_w, v.ndim - 1)

    vecs = []
    for small, rel in ((small0, rel0), (small1, rel1)):
        vecs.append(
            jnp.concatenate([small[0], half(small[1]), small[2], half(small[3]), rel.reshape(-1)])
        )
    mask_half = half(mask_sum)
    sent = jnp.concatenate([mine(1 - c, vecs), mask_half])
    total = jnp.concatenate([mine(c, vecs), mask_half]) + swap(sent, "section")
    total = lax.psum(total, "dp")
    cuts = [2 * lw, half_w, ff, half_w, heads * (2 * length - 1), half_w]
    parts = []
    at = 0
    for n in cuts:
        parts.append(total[at : at + n])
        at += n
    g_b_qv = parts[0].reshape(2, lw)
    g_rel = parts[4].reshape(heads, 2 * length - 1)

    dm = [half(dmod0), half(dmod1)]
    dm_own = mine(c, dm)
    dm_got = swap(mine(1 - c, dm), "section")
    dm_pair = jnp.stack([pick(c, dm_own, dm_got), pick(c, dm_got, dm_own)])
    dm_all = lax.all_gather(dm_pair, "dp").reshape(dp_count * micro, 6 * lw)
    g_ada = jnp.einsum("id,ie->de", cond_part, dm_all, precision=PRECISE).reshape(fr, 6, lw)
    g_b_ada = jnp.sum(dm_all, axis=0).reshape(6, lw)
    dcl = jnp.einsum("ie,de->id", dm_all, ada, precision=PRECISE)
    dcl = lax.psum(dcl, ("section", "head"))
    dcl = lax.all_gather(dcl, "dp", axis=1, tiled=True)
    sig = jax.nn.sigmoid(cond)
    dcond = half(dcl * (sig * (1.0 + cond * (1.0 - sig))))
    g_class = jnp.einsum("ic,id->cd", label_pick.astype(F32), dcond, precision=PRECISE)

    def settle(first, second):
        got = swap(pick(c, second, first), "section")
        own_part = pick(c, first, second)
        return jnp.stack([pick(c, own_part, got), pick(c, got, own_part)])[None]

    return (
        settle(e, out1),
        settle(dtok, da),
        g_qkv[None],
        g_b_qv[None],
        g_out[None],
        parts[1][None],
        g_up[None],
        parts[2][None],
        g_down[None],
        parts[3][None],
        g_ada[None],
        g_b_ada[None],
        g_rel[None],
        parts[5],
        g_class,
    )


def solution(mesh):
    placed = (
        P(None, "dp", None),
        P(None, "dp", None),
        P(None, "dp"),
        P(None, "dp"),
        P("section", "dp", None, "head"),
        P("section", None, "head"),
        P("section", "head", "dp"),
        P("section", None),
        P("section", "dp", "head"),
        P("section", "head"),
        P("section", "head", "dp"),
        P("section", None),
        P("section", "dp", None, "head"),
        P("section", None, "head"),
        P("section", "head", None),
        P(),
        P(),
        P(None, "dp", None),
    )
    return jax.shard_map(
        per_device,
        mesh=mesh,
        in_specs=placed,
        out_specs=(
            P("section", None, "dp", None),
            P("section", None, "dp", None),
            P("section", "dp", None, "head"),
            P("section", None, "head"),
            P("section", "head", "dp"),
            P("section", "head"),
            P("section", "dp", "head"),
            P("section", "head"),
            P("section", "head", "dp"),
            P("section", "head"),
            P("section", "dp", None, "head"),
            P("section", None, "head"),
            P("section", "head", None),
            P("head"),
            P(None, "head"),
        ),
        check_vma=False,
    )
```

time: 2360 us -> 1450 us (0.61)
  waiting for transfers between devices: 1420 us -> 195 us
  Pallas kernels: 0 us -> 168 us
  local copies, waits for them, and re-layouts: 443 us -> 609 us
  other arithmetic: 147 us -> 103 us
  blocking collectives: 93.9 us -> 132 us
    reduce_scatter x5 -> x6, waiting for transfers between devices: 785 us -> 143 us  [per_device(): lax.psum_scatter(t, 'dp', scatter_dimension=0, tiled=True)]
    psum x12 -> x0, waiting for transfers between devices: 464 us -> none  [the longest x6 257 us: head_total(): return lax.psum(partial_sum, 'head')]
    gather x5 -> x4, local copies, waits for them, and re-layouts: 241 us -> 482 us  [toeplitz(): return jnp.take(rel, span[:, None] - span[None, :] + length - 1, axis=1)]
    pallas_call x0 -> x1, Pallas kernels: none -> 168 us  [gather_pieces(): pl.pallas_call(body, out_shape=jax.ShapeDtypeStruct((pieces, 2, dp_count,...]
    all_gather x5 -> x0, waiting for transfers between devices: 166 us -> none  [the longest x1 84 us: per_device(): lax.all_gather(w_up[0], 'dp', axis=0, tiled=True)]
    all_gather x3, blocking collectives: 14.9 us -> 83.3 us  [the longest x1 31 us: per_device(): dm_all = lax.all_gather(dm_pair, 'dp').reshape(dp_count * micro, 6 * lw)]
    scatter x2 -> x0, local copies, waits for them, and re-layouts: 49.5 us -> none  [the longest x1 24.7 us: layout(): jnp.zeros((row_count,), jnp.int32).at[source].set(positions, mode='drop')]
    ppermute x4 -> x37, waiting for transfers between devices: 5.65 us -> 51.2 us  [swap(): return lax.ppermute(value, axis, [(0, 1), (1, 0)])]
  transfers between devices with their start and end apart: 26 -> 44, of which waited for: 19 -> 9; matrix products, arithmetic and copies ran while one was open for 23% -> 59% of each run, Pallas kernels for 0% -> 12%
where the time goes in v1:
time: 1450 us; the launch traced here: 1440 us
  local copies, waits for them, and re-layouts  609 us (42%)
  waiting for transfers between devices  195 us (13%)
  matrix products  192 us (13%)
  Pallas kernels  168 us (12%)
  blocking collectives  132 us (9%)
  other arithmetic  103 us (7%)
  starting transfers between devices  20.7 us (1%)
  between operations  19.6 us (1%)
    gather x4, local copies, waits for them, and re-layouts, toeplitz(): return jnp.take(rel, span[:, None] - span[None, :] + length - 1, axis=1)  482 us
    pallas_call x1, Pallas kernels, gather_pieces(): pl.pallas_call(body, out_shape=jax.ShapeDtypeStruct((pieces, 2, dp_count,...  168 us
    reduce_scatter x6, waiting for transfers between devices, per_device(): lax.psum_scatter(t, 'dp', scatter_dimension=0, tiled=True)  143 us
    dot_general x50, matrix products, nn(): lax.dot_general(a, b, (((1,), (0,)), ((), ())), preferred_element_type=F32)  74.5 us
    dot_general x48, matrix products, nt(): lax.dot_general(a, b, (((1,), (1,)), ((), ())), preferred_element_type=F32)  54.5 us
    ppermute x37, waiting for transfers between devices, swap(): return lax.ppermute(value, axis, [(0, 1), (1, 0)])  51.2 us
    dot_general x41, matrix products, tn(): lax.dot_general(a, b, (((0,), (0,)), ((), ())), preferred_element_type=F32)  48.6 us
    psum x1, blocking collectives, per_device(): total = lax.psum(total, 'dp')  36.3 us
  transfers between devices with their start and end apart: 44, of which 9 were waited for; matrix products, arithmetic and copies ran while one was open for 59% of the time, Pallas kernels for 12%

profile of v1, /device:TPU:0, one launch (start us, length us, event | category | flops | bytes accessed | tf_op | source)
XLA Modules:
  0.0 1439.9 jit_solution(1400338401330837843)
XLA Ops:
  20.0 21.8 %all-gather.2 = s32[8,2,2]{2,1,0:T(2,128)S(1)} all-gather(s32[1,2,2]{2,1,0:T(2,128)S(1)} %add_bitcast_fusion), channel_id=2, replica_groups=mesh['section'=2,'dp'=8,'head'=2] {'dp'}, dimensions={0}, use_global_device_ids=true | all-gather | bytes 144 | tf_op jit(solution)/shard_map/all_gather | solution.py:465
  41.9 2.6 copy.119
  44.5 2.6 reshape.410
  54.4 3.4 all-to-all-start
  67.3 229.3 %gather_fusion = bf16[65536,8]{1,0:T(8,128)(2,1)} fusion(bf16[8,511]{0,1:T(8,128)(2,1)S(1)} %get-tuple-element.174, s32[65536]{0:T(1024)S(1)} %broadcast_clamp_fusion), kind=kCustom, calls=%fused_computation.clone | custom fusion | bytes 2359296 | tf_op jit(solution)/shard_map/jit(_take)/gather | solution.py:406
  296.5 15.9 %copy.129 = bf16[256,256,8]{0,1,2:T(8,128)(2,1)S(1)} copy(bf16[256,256,8]{2,1,0:T(8,128)(2,1)} %bitcast.489) | data formatting | bytes 2097152 | tf_op jit(solution)/shard_map/jit(_take)/gather | solution.py:406
  322.5 168.1 %gather_weights.1 = bf16[6,2,8,144,1152]{4,3,2,1,0:T(8,128)(2,1)} custom-call(bf16[6,144,1152]{2,1,0:T(8,128)(2,1)} %pad_maximum_fusion.2.refs_0_), custom_call_target="tpu_custom_call" | custom-call | tf_op jit(solution)/shard_map/gather_weights/pallas_call | solution.py:243
  490.6 6.6 slice_bitcast_fusion.4
  497.3 3.8 fusion.552
  502.4 3.3 fusion.557
  514.6 12.7 collective-permute-done.5
  529.3 3.0 fusion.13
  532.3 4.7 broadcast_select_fusion.10
  537.0 3.2 fusion.14
  540.3 12.4 fusion.3
  554.3 217.0 %gather_fusion.1 = f32[65536,8]{1,0:T(8,128)} fusion(f32[8,511]{0,1:T(8,128)S(1)} %get-tuple-element.173, s32[65536]{0:T(1024)S(1)} %copy-done.61), kind=kCustom, calls=%fused_computation.1.clone | custom fusion | bytes 4456448 | tf_op jit(solution)/shard_map/jit(_take)/gather | solution.py:406
  771.3 19.6 %copy.133 = f32[256,256,8]{0,1,2:T(8,128)} copy(f32[256,256,8]{2,1,0:T(8,128)} %bitcast.488) | data formatting | bytes 4194304 | tf_op jit(solution)/shard_map/jit(_take)/gather | solution.py:406
  798.0 3.6 fusion.563
  803.9 3.5 fusion.568
  815.8 12.4 collective-permute-done.10
  830.7 3.1 fusion.17
  833.9 5.1 broadcast_select_fusion.8
  843.2 4.0 broadcast_select_fusion.9
  858.1 9.0 collective-permute-done.13
  869.4 12.3 collective-permute-done.11
  881.8 3.7 broadcast_select_fusion.14
  893.2 4.5 convolution_convert_fusion.1
  921.9 4.6 convolution_convert_fusion
  943.8 3.6 fusion.25
  947.5 15.7 %rev.7 = f32[8,256,256]{1,2,0:T(8,128)} reverse(bf16[8,256,256]{1,2,0:T(8,128)(2,1)} %get-tuple-element.56), dimensions={2} | reverse | bytes 3145728 | tf_op jit(solution)/shard_map/rev | solution.py:411
  963.1 2.9 copy.151
  966.0 4.4 pad_bitcast_fusion
  970.4 2.6 fusion
  973.6 4.0 convolution_convert_fusion.4
  977.5 4.1 copy.137
  983.0 2.7 convolution_convert_fusion.6
  988.0 4.4 pad_maximum_fusion.1
  992.9 4.5 collective-permute-done.14
  1002.8 4.0 convert_reduce_fusion.6
  1006.8 4.5 broadcast_select_fusion.11
  1012.1 2.8 fusion.12
  1015.0 3.0 fusion.11
  1025.3 8.1 reshape.418
  1033.5 2.7 reduce_sum.765
  1040.2 4.8 convolution_convert_fusion.2
  1045.2 2.6 multiply_reduce_fusion.4
  1047.9 2.9 multiply_reduce_fusion.5
  1057.3 4.6 convolution_convert_fusion.3
  1088.1 3.8 convolution_convert_fusion.5
  1091.9 4.3 copy.135
  1100.3 4.3 pad_maximum_fusion
  1104.6 3.2 fusion.20
  1107.8 15.0 %rev.6 = f32[8,256,256]{2,1,0:T(8,128)S(1)} reverse(f32[8,256,256]{2,1,0:T(8,128)} %fusion.20), dimensions={2} | reverse | bytes 4194304 | tf_op jit(solution)/shard_map/rev | solution.py:411
  1129.0 8.0 reshape.415
  1137.1 2.9 reduce_sum.758
  1143.8 36.3 %psum.14 = f32[9272]{0:T(1024)S(1)} all-reduce(f32[9272]{0:T(1024)S(1)} %fusion.338), channel_id=1, replica_groups=mesh['section'=2,'dp'=8,'head'=2] {'dp'}, use_global_device_ids=true, to_apply=%region_89.91 | all-reduce | flops 9272 | bytes 74176 | tf_op jit(solution)/shard_map/psum | solution.py:557
  1186.0 3.6 broadcast_select_fusion.12
  1191.6 69.3 %reduce-scatter.9.cloned.1.call-done = bf16[144,1152]{1,0:T(8,128)(2,1)} async-done(((bf16[1152,1152]{1,0:T(8,128)(2,1)}), bf16[144,1152]{1,0:T(8,128)(2,1)}) %reduce-scatter.9.cloned.1.call-update) | async-done | bytes 331792 | tf_op jit(solution)/shard_map/reduce_scatter | solution.py:528
  1260.9 74.0 %reduce-scatter.7.cloned.1.call-done = bf16[144,1152]{1,0:T(8,128)(2,1)} async-done(((bf16[1152,1152]{1,0:T(8,128)(2,1)}), bf16[144,1152]{1,0:T(8,128)(2,1)}) %reduce-scatter.7.cloned.1.call-update) | async-done | bytes 331792 | tf_op jit(solution)/shard_map/reduce_scatter | solution.py:528
  1339.3 31.0 %all-gather.1 = f32[16,6,576]{2,1,0:T(8,128)S(1)} all-gather(f32[2,6,576]{2,1,0:T(8,128)S(1)} %pad_maximum_fusion.12), channel_id=3, replica_groups=mesh['section'=2,'dp'=8,'head'=2] {'dp'}, dimensions={0}, use_global_device_ids=true | all-gather | bytes 248832 | tf_op jit(solution)/shard_map/all_gather | solution.py:571
  1372.1 12.1 psum.15
  1384.1 30.5 %all-gather.3 = f32[8,144,16]{1,2,0:T(8,128)S(1)} all-gather(f32[1,144,16]{1,2,0:T(8,128)S(1)} %bitcast.511), channel_id=1, replica_groups=mesh['section'=2,'dp'=8,'head'=2] {'dp'}, dimensions={0}, use_global_device_ids=true | all-gather | bytes 82944 | tf_op jit(solution)/shard_map/all_gather | solution.py:576
  1414.9 3.3 convolution_bitcast_fusion
  1418.2 2.7 fusion.337
  (1114 shorter events, 231.4 us)
Async XLA Ops:
  7.2 42.6 %copy-start = (bf16[1000,1152]{1,0:T(8,128)(2,1)S(1)}, bf16[1000,1152]{1,0:T(8,128)(2,1)}, u32[]{:S(2)}) copy-start(bf16[1000,1152]{1,0:T(8,128)(2,1)} %param.36) | copy-start | bytes 6912004
  8.1 56.9 %collective-permute-start.6 = (bf16[1152]{0:T(1024)(128)(2,1)S(1)}, bf16[1152]{0:T(1024)(128)(2,1)S(1)}, u32[]{:S(2)}, u32[]{:S(2)}) collective-permute-start(bf16[1152]{0:T(1024)(128)(2,1)S(1)} %reduce.15), channel_id=1, source_target_pairs={{0,16},{16,0},{1,17},{17,1},{2,18},{18,2},{3,19},{19,3},{4,20},{20... | collective-permute-start | bytes 6920 | tf_op jit(solution)/shard_map/ppermute | solution.py:26
  18.7 300.5 %collective-permute-start.2 = (bf16[3,144,1152]{2,1,0:T(8,128)(2,1)}, bf16[3,144,1152]{2,1,0:T(8,128)(2,1)}, u32[]{:S(2)}, u32[]{:S(2)}) collective-permute-start(bf16[3,144,1152]{2,1,0:T(8,128)(2,1)} %broadcast_select_fusion), channel_id=1, source_target_pairs={{0,16},{16,0},{1,17},{17,1},{2,18},{18,2},{3,19},{19,3},{4,20},{20... | collective-permute-start | bytes 2985992 | tf_op jit(solution)/shard_map/ppermute | solution.py:26
  19.5 46.7 %collective-permute-start.4 = (bf16[8,511]{0,1:T(8,128)(2,1)}, bf16[8,511]{0,1:T(8,128)(2,1)}, u32[]{:S(2)}, u32[]{:S(2)}) collective-permute-start(bf16[8,511]{0,1:T(8,128)(2,1)} %bitcast.33), channel_id=1, source_target_pairs={{0,16},{16,0},{1,17},{17,1},{2,18},{18,2},{3,19},{19,3},{4,20},{20... | collective-permute-start | bytes 24536 | tf_op jit(solution)/shard_map/ppermute | solution.py:26
  54.4 11.5 all-to-all-start
  57.8 1132.4 %reduce-scatter.15.cloned.1.call-start = ((), (), s32[]{:S(2)}) async-start(), calls=%async_computation.11 | async-start | bytes 2985984 | tf_op jit(solution)/shard_map/reduce_scatter | solution.py:528
  57.9 6.3 collective-permute-start.3
  58.6 455.3 %collective-permute-start.7 = (bf16[2304]{0:T(1024)(128)(2,1)}, bf16[2304]{0:T(1024)(128)(2,1)}, u32[]{:S(2)}, u32[]{:S(2)}) collective-permute-start(bf16[2304]{0:T(1024)(128)(2,1)} %reduce.19), channel_id=1, source_target_pairs={{0,16},{16,0},{1,17},{17,1},{2,18},{18,2},{3,19},{19,3},{4,20},{20... | collective-permute-start | bytes 13832 | tf_op jit(solution)/shard_map/ppermute | solution.py:26
  59.4 254.7 %copy-start.258 = (pred[256]{0:T(512)(128)(4,1)}, pred[256]{0:T(512)(128)(4,1)S(1)}, u32[]{:S(2)}) copy-start(pred[256]{0:T(512)(128)(4,1)S(1)} %get-tuple-element.112) | copy-start | bytes 772
  61.3 252.8 %copy-start.296 = (pred[256]{0:T(512)(128)(4,1)}, pred[256]{0:T(512)(128)(4,1)S(1)}, u32[]{:S(2)}) copy-start(pred[256]{0:T(512)(128)(4,1)S(1)} %get-tuple-element.313) | copy-start | bytes 772
  61.3 252.8 %copy-start.316 = (pred[256]{0:T(512)(128)(4,1)}, pred[256]{0:T(512)(128)(4,1)S(1)}, u32[]{:S(2)}) copy-start(pred[256]{0:T(512)(128)(4,1)S(1)} %get-tuple-element.312) | copy-start | bytes 772
  62.0 252.1 %copy-start.214 = (s32[256]{0:T(256)}, s32[256]{0:T(256)S(1)}, u32[]{:S(2)}) copy-start(s32[256]{0:T(256)S(1)} %add_bitcast_fusion.1) | copy-start | bytes 3076
  62.2 255.8 %copy-start.212 = (f32[256]{0:T(256)}, f32[256]{0:T(256)S(1)}, u32[]{:S(2)}) copy-start(f32[256]{0:T(256)S(1)} %broadcast_multiply_fusion.11) | copy-start | bytes 3076
  62.5 255.5 %copy-start.254 = (f32[256]{0:T(256)}, f32[256]{0:T(256)S(1)}, u32[]{:S(2)}) copy-start(f32[256]{0:T(256)S(1)} %add_rsqrt_fusion.3) | copy-start | bytes 3076
  62.8 251.3 %copy-start.173 = (pred[256,256]{0,1:T(8,128)(4,1)}, pred[256,256]{0,1:T(8,128)(4,1)S(1)}, u32[]{:S(2)}) copy-start(pred[256,256]{0,1:T(8,128)(4,1)S(1)} %copy.127) | copy-start | bytes 196612
  64.2 448.4 %collective-permute-start.9 = (bf16[1152]{0:T(1024)(128)(2,1)}, bf16[1152]{0:T(1024)(128)(2,1)}, u32[]{:S(2)}, u32[]{:S(2)}) collective-permute-start(bf16[1152]{0:T(1024)(128)(2,1)} %reduce.20), channel_id=1, source_target_pairs={{0,16},{16,0},{1,17},{17,1},{2,18},{18,2},{3,19},{19,3},{4,20},{20... | collective-permute-start | bytes 6920 | tf_op jit(solution)/shard_map/ppermute | solution.py:26
  66.1 246.4 %collective-permute-start = (f32[6,576]{1,0:T(8,128)S(1)}, f32[6,576]{1,0:T(8,128)S(1)}, u32[]{:S(2)}, u32[]{:S(2)}) collective-permute-start(f32[6,576]{1,0:T(8,128)S(1)} %bitcast.512), channel_id=1, source_target_pairs={{0,16},{16,0},{1,17},{17,1},{2,18},{18,2},{3,19},{19,3},{4,20},{20... | collective-permute-start | bytes 41480 | tf_op jit(solution)/shard_map/ppermute | solution.py:26
  312.5 4.1 collective-permute-start.1
  511.6 15.7 %collective-permute-start.5 = (bf16[256,1152]{1,0:T(8,128)(2,1)S(1)}, bf16[256,1152]{1,0:T(8,128)(2,1)S(1)}, u32[]{:S(2)}, u32[]{:S(2)}) collective-permute-start(bf16[256,1152]{1,0:T(8,128)(2,1)S(1)} %fusion.2), channel_id=1, source_target_pairs={{0,1},{1,0},{2,3},{3,2},{4,5},{5,4},{6,7},{7,6},{8,9},{9,8},{10,11... | collective-permute-start | bytes 1769480 | tf_op jit(solution)/shard_map/ppermute | solution.py:26
  552.7 241.5 %copy-start.62 = (bf16[256,1152]{1,0:T(8,128)(2,1)}, bf16[256,1152]{1,0:T(8,128)(2,1)S(1)}, u32[]{:S(2)}) copy-start(bf16[256,1152]{1,0:T(8,128)(2,1)S(1)} %fusion.3) | copy-start | bytes 1769476
  552.7 241.5 %collective-permute-start.8 = (bf16[256,1152]{1,0:T(8,128)(2,1)S(1)}, bf16[256,1152]{1,0:T(8,128)(2,1)S(1)}, u32[]{:S(2)}, u32[]{:S(2)}) collective-permute-start(bf16[256,1152]{1,0:T(8,128)(2,1)S(1)} %fusion.3), channel_id=1, source_target_pairs={{0,1},{1,0},{2,3},{3,2},{4,5},{5,4},{6,7},{7,6},{8,9},{9,8},{10,11... | collective-permute-start | bytes 1769480 | tf_op jit(solution)/shard_map/ppermute | solution.py:26
  792.8 294.3 %collective-permute-start.20 = (bf16[256,1152]{1,0:T(8,128)(2,1)}, bf16[256,1152]{1,0:T(8,128)(2,1)}, u32[]{:S(2)}, u32[]{:S(2)}) collective-permute-start(bf16[256,1152]{1,0:T(8,128)(2,1)} %fusion.49), channel_id=1, source_target_pairs={{0,16},{16,0},{1,17},{17,1},{2,18},{18,2},{3,19},{19,3},{4,20},{20... | collective-permute-start | bytes 1769480 | tf_op jit(solution)/shard_map/ppermute | solution.py:26
  793.8 302.5 %collective-permute-start.19 = (bf16[256,288]{0,1:T(8,128)(2,1)}, bf16[256,288]{0,1:T(8,128)(2,1)}, u32[]{:S(2)}, u32[]{:S(2)}) collective-permute-start(bf16[256,288]{0,1:T(8,128)(2,1)} %get-tuple-element.170), channel_id=1, source_target_pairs={{0,16},{16,0},{1,17},{17,1},{2,18},{18,2},{3,19},{19,3},{4,20},{20... | collective-permute-start | bytes 442376 | tf_op jit(solution)/shard_map/ppermute | solution.py:26
  794.3 44.7 %slice-start = ((s8[31850496]{0:T(1024)(128)(4,1)}), s8[4194304]{0:T(1024)(128)(4,1)S(1)}, s32[]{:S(2)}) async-start(s8[31850496]{0:T(1024)(128)(4,1)} %bitcast.480), calls=%async_computation.13 | async-start | bytes 8388608
  795.1 86.6 %copy-start.4 = (f32[256,1152]{1,0:T(8,128)}, f32[256,1152]{1,0:T(8,128)S(1)}, u32[]{:S(2)}) copy-start(f32[256,1152]{1,0:T(8,128)S(1)} %multiply_add_fusion.8) | copy-start | bytes 3538948
  796.9 42.2 %slice-start.1 = ((s8[31850496]{0:T(1024)(128)(4,1)}), s8[4194304]{0:T(1024)(128)(4,1)S(1)}, s32[]{:S(2)}) async-start(s8[31850496]{0:T(1024)(128)(4,1)} %bitcast.480), calls=%async_computation.14 | async-start | bytes 8388608
  801.8 89.8 %copy-start.123 = (bf16[256,288]{0,1:T(8,128)(2,1)}, bf16[256,288]{0,1:T(8,128)(2,1)S(1)}, u32[]{:S(2)}) copy-start(bf16[256,288]{0,1:T(8,128)(2,1)S(1)} %get-tuple-element.148) | copy-start | bytes 442372
  809.0 82.5 %copy-start.99 = (bf16[256,256]{0,1:T(8,128)(2,1)}, bf16[256,256]{0,1:T(8,128)(2,1)S(1)}, u32[]{:S(2)}) copy-start(bf16[256,256]{0,1:T(8,128)(2,1)S(1)} %divide_convert_fusion.5) | copy-start | bytes 393220
  809.5 81.1 %copy-start.101 = (bf16[256,256]{0,1:T(8,128)(2,1)}, bf16[256,256]{0,1:T(8,128)(2,1)S(1)}, u32[]{:S(2)}) copy-start(bf16[256,256]{0,1:T(8,128)(2,1)S(1)} %divide_convert_fusion.6) | copy-start | bytes 393220
  809.8 78.3 %copy-start.103 = (bf16[256,256]{0,1:T(8,128)(2,1)}, bf16[256,256]{0,1:T(8,128)(2,1)S(1)}, u32[]{:S(2)}) copy-start(bf16[256,256]{0,1:T(8,128)(2,1)S(1)} %divide_convert_fusion.7) | copy-start | bytes 393220
  812.9 15.3 %collective-permute-start.10 = (bf16[256,1152]{1,0:T(8,128)(2,1)S(1)}, bf16[256,1152]{1,0:T(8,128)(2,1)S(1)}, u32[]{:S(2)}, u32[]{:S(2)}) collective-permute-start(bf16[256,1152]{1,0:T(8,128)(2,1)S(1)} %fusion.4), channel_id=1, source_target_pairs={{0,1},{1,0},{2,3},{3,2},{4,5},{5,4},{6,7},{7,6},{8,9},{9,8},{10,11... | collective-permute-start | bytes 1769480 | tf_op jit(solution)/shard_map/ppermute | solution.py:26
  815.1 157.9 %collective-permute-start.28 = (bf16[256,1152]{1,0:T(8,128)(2,1)}, bf16[256,1152]{1,0:T(8,128)(2,1)}, u32[]{:S(2)}, u32[]{:S(2)}) collective-permute-start(bf16[256,1152]{1,0:T(8,128)(2,1)} %add_convert_fusion.1), channel_id=1, source_target_pairs={{0,16},{16,0},{1,17},{17,1},{2,18},{18,2},{3,19},{19,3},{4,20},{20... | collective-permute-start | bytes 1769480 | tf_op jit(solution)/shard_map/ppermute | solution.py:26
  833.7 58.8 %collective-permute-start.30 = (bf16[256,1152]{1,0:T(8,128)(2,1)}, bf16[256,1152]{1,0:T(8,128)(2,1)}, u32[]{:S(2)}, u32[]{:S(2)}) collective-permute-start(bf16[256,1152]{1,0:T(8,128)(2,1)} %add_convert_fusion), channel_id=1, source_target_pairs={{0,16},{16,0},{1,17},{17,1},{2,18},{18,2},{3,19},{19,3},{4,20},{20... | collective-permute-start | bytes 1769480 | tf_op jit(solution)/shard_map/ppermute | solution.py:26
  851.5 15.5 %collective-permute-start.13 = (bf16[256,1152]{1,0:T(8,128)(2,1)S(1)}, bf16[256,1152]{1,0:T(8,128)(2,1)S(1)}, u32[]{:S(2)}, u32[]{:S(2)}) collective-permute-start(bf16[256,1152]{1,0:T(8,128)(2,1)S(1)} %fusion.8), channel_id=1, source_target_pairs={{0,1},{1,0},{2,3},{3,2},{4,5},{5,4},{6,7},{7,6},{8,9},{9,8},{10,11... | collective-permute-start | bytes 1769480 | tf_op jit(solution)/shard_map/ppermute | solution.py:26
  867.1 14.6 %collective-permute-start.11 = (bf16[256,1152]{1,0:T(8,128)(2,1)S(1)}, bf16[256,1152]{1,0:T(8,128)(2,1)S(1)}, u32[]{:S(2)}, u32[]{:S(2)}) collective-permute-start(bf16[256,1152]{1,0:T(8,128)(2,1)S(1)} %fusion.5), channel_id=1, source_target_pairs={{0,1},{1,0},{2,3},{3,2},{4,5},{5,4},{6,7},{7,6},{8,9},{9,8},{10,11... | collective-permute-start | bytes 1769480 | tf_op jit(solution)/shard_map/ppermute | solution.py:26
  881.7 11.3 collective-permute-start.31
  892.5 28.9 %collective-permute-start.33 = (bf16[256,1152]{1,0:T(8,128)(2,1)}, bf16[256,1152]{1,0:T(8,128)(2,1)}, u32[]{:S(2)}, u32[]{:S(2)}) collective-permute-start(bf16[256,1152]{1,0:T(8,128)(2,1)} %broadcast_select_fusion.4), channel_id=1, source_target_pairs={{0,16},{16,0},{1,17},{17,1},{2,18},{18,2},{3,19},{19,3},{4,20},{20... | collective-permute-start | bytes 1769480 | tf_op jit(solution)/shard_map/ppermute | solution.py:26
  893.1 28.9 %collective-permute-start.32 = (bf16[256,1152]{1,0:T(8,128)(2,1)}, bf16[256,1152]{1,0:T(8,128)(2,1)}, u32[]{:S(2)}, u32[]{:S(2)}) collective-permute-start(bf16[256,1152]{1,0:T(8,128)(2,1)} %get-tuple-element.136), channel_id=1, source_target_pairs={{0,16},{16,0},{1,17},{17,1},{2,18},{18,2},{3,19},{19,3},{4,20},{20... | collective-permute-start | bytes 1769480 | tf_op jit(solution)/shard_map/ppermute | solution.py:26
  897.7 292.5 %reduce-scatter.17.cloned.1.call-start = ((), (), s32[]{:S(2)}) async-start(), calls=%async_computation.12 | async-start | bytes 2985984 | tf_op jit(solution)/shard_map/reduce_scatter | solution.py:528
  921.4 61.6 %collective-permute-start.26 = (bf16[256,1152]{1,0:T(8,128)(2,1)}, bf16[256,1152]{1,0:T(8,128)(2,1)}, u32[]{:S(2)}, u32[]{:S(2)}) collective-permute-start(bf16[256,1152]{1,0:T(8,128)(2,1)} %get-tuple-element.75), channel_id=1, source_target_pairs={{0,16},{16,0},{1,17},{17,1},{2,18},{18,2},{3,19},{19,3},{4,20},{20... | collective-permute-start | bytes 1769480 | tf_op jit(solution)/shard_map/ppermute | solution.py:26
  926.6 263.7 %reduce-scatter.13.cloned.1.call-start = ((), (), s32[]{:S(2)}) async-start(), calls=%async_computation.10 | async-start | bytes 2985984 | tf_op jit(solution)/shard_map/reduce_scatter | solution.py:528
  942.5 30.9 %collective-permute-start.29 = (bf16[256,864]{0,1:T(8,128)(2,1)}, bf16[256,864]{0,1:T(8,128)(2,1)}, u32[]{:S(2)}, u32[]{:S(2)}) collective-permute-start(bf16[256,864]{0,1:T(8,128)(2,1)} %get-tuple-element.145), channel_id=1, source_target_pairs={{0,16},{16,0},{1,17},{17,1},{2,18},{18,2},{3,19},{19,3},{4,20},{20... | collective-permute-start | bytes 1327112 | tf_op jit(solution)/shard_map/ppermute | solution.py:26
  973.0 66.8 %collective-permute-start.25 = (bf16[256,1152]{1,0:T(8,128)(2,1)}, bf16[256,1152]{1,0:T(8,128)(2,1)}, u32[]{:S(2)}, u32[]{:S(2)}) collective-permute-start(bf16[256,1152]{1,0:T(8,128)(2,1)} %broadcast_select_fusion.6), channel_id=1, source_target_pairs={{0,16},{16,0},{1,17},{17,1},{2,18},{18,2},{3,19},{19,3},{4,20},{20... | collective-permute-start | bytes 1769480 | tf_op jit(solution)/shard_map/ppermute | solution.py:26
  973.5 8.2 collective-permute-start.27
  981.7 15.8 %collective-permute-start.14 = (bf16[256,1152]{1,0:T(8,128)(2,1)S(1)}, bf16[256,1152]{1,0:T(8,128)(2,1)}, u32[]{:S(2)}, u32[]{:S(2)}) collective-permute-start(bf16[256,1152]{1,0:T(8,128)(2,1)S(1)} %fusion), channel_id=1, source_target_pairs={{0,1},{1,0},{2,3},{3,2},{4,5},{5,4},{6,7},{7,6},{8,9},{9,8},{10,11... | collective-permute-start | bytes 1769480 | tf_op jit(solution)/shard_map/ppermute | solution.py:26
  992.5 199.1 %reduce-scatter.11.cloned.1.call-start = ((), (), s32[]{:S(2)}) async-start(), calls=%async_computation.9 | async-start | bytes 2985984 | tf_op jit(solution)/shard_map/reduce_scatter | solution.py:528
  1002.2 37.5 %collective-permute-start.24 = (bf16[256,1152]{1,0:T(8,128)(2,1)}, bf16[256,1152]{1,0:T(8,128)(2,1)}, u32[]{:S(2)}, u32[]{:S(2)}) collective-permute-start(bf16[256,1152]{1,0:T(8,128)(2,1)} %get-tuple-element.93), channel_id=1, source_target_pairs={{0,16},{16,0},{1,17},{17,1},{2,18},{18,2},{3,19},{19,3},{4,20},{20... | collective-permute-start | bytes 1769480 | tf_op jit(solution)/shard_map/ppermute | solution.py:26
  1018.0 27.1 %collective-permute-start.15 = (bf16[256,1152]{1,0:T(8,128)(2,1)S(1)}, bf16[256,1152]{1,0:T(8,128)(2,1)}, u32[]{:S(2)}, u32[]{:S(2)}) collective-permute-start(bf16[256,1152]{1,0:T(8,128)(2,1)S(1)} %fusion.11), channel_id=1, source_target_pairs={{0,1},{1,0},{2,3},{3,2},{4,5},{5,4},{6,7},{7,6},{8,9},{9,8},{10,11... | collective-permute-start | bytes 1769480 | tf_op jit(solution)/shard_map/ppermute | solution.py:26
  1039.7 17.0 %collective-permute-start.22 = (bf16[256,1152]{1,0:T(8,128)(2,1)}, bf16[256,1152]{1,0:T(8,128)(2,1)}, u32[]{:S(2)}, u32[]{:S(2)}) collective-permute-start(bf16[256,1152]{1,0:T(8,128)(2,1)} %copy-done.140), channel_id=1, source_target_pairs={{0,16},{16,0},{1,17},{17,1},{2,18},{18,2},{3,19},{19,3},{4,20},{20... | collective-permute-start | bytes 1769480 | tf_op jit(solution)/shard_map/ppermute | solution.py:26
  1039.7 100.8 %collective-permute-start.12 = (f32[256,1152]{1,0:T(8,128)}, f32[256,1152]{1,0:T(8,128)}, u32[]{:S(2)}, u32[]{:S(2)}) collective-permute-start(f32[256,1152]{1,0:T(8,128)} %get-tuple-element.106), channel_id=1, source_target_pairs={{0,16},{16,0},{1,17},{17,1},{2,18},{18,2},{3,19},{19,3},{4,20},{20... | collective-permute-start | bytes 3538952 | tf_op jit(solution)/shard_map/ppermute | solution.py:26
  1045.1 12.1 collective-permute-start.23
  1053.9 207.0 %reduce-scatter.9.cloned.1.call-start = ((), (), s32[]{:S(2)}) async-start(), calls=%async_computation.8 | async-start | bytes 2985984 | tf_op jit(solution)/shard_map/reduce_scatter | solution.py:528
  1056.7 39.5 %collective-permute-start.18 = (bf16[256,1152]{1,0:T(8,128)(2,1)}, bf16[256,1152]{1,0:T(8,128)(2,1)}, u32[]{:S(2)}, u32[]{:S(2)}) collective-permute-start(bf16[256,1152]{1,0:T(8,128)(2,1)} %copy-done.136), channel_id=1, source_target_pairs={{0,16},{16,0},{1,17},{17,1},{2,18},{18,2},{3,19},{19,3},{4,20},{20... | collective-permute-start | bytes 1769480 | tf_op jit(solution)/shard_map/ppermute | solution.py:26
  1073.0 261.9 %reduce-scatter.7.cloned.1.call-start = ((), (), s32[]{:S(2)}) async-start(), calls=%async_computation.7 | async-start | bytes 2985984 | tf_op jit(solution)/shard_map/reduce_scatter | solution.py:528
  1080.9 7.2 collective-permute-start.21
  1087.2 96.8 %collective-permute-start.16 = (bf16[256,1152]{1,0:T(8,128)(2,1)}, bf16[256,1152]{1,0:T(8,128)(2,1)}, u32[]{:S(2)}, u32[]{:S(2)}) collective-permute-start(bf16[256,1152]{1,0:T(8,128)(2,1)} %fusion.1), channel_id=1, source_target_pairs={{0,1},{1,0},{2,3},{3,2},{4,5},{5,4},{6,7},{7,6},{8,9},{9,8},{10,11... | collective-permute-start | bytes 1769480 | tf_op jit(solution)/shard_map/ppermute | solution.py:26
  1140.4 3.3 collective-permute-start.35
  1142.2 41.9 %copy-start.12 = (bf16[2,256,1152]{2,1,0:T(8,128)(2,1)S(1)}, bf16[2,256,1152]{2,1,0:T(8,128)(2,1)}, u32[]{:S(2)}) copy-start(bf16[2,256,1152]{2,1,0:T(8,128)(2,1)} %param.20) | copy-start | bytes 3538948
  1142.2 41.9 %copy-start.189 = (f32[1152]{0:T(1024)S(1)}, f32[1152]{0:T(1024)}, u32[]{:S(2)}) copy-start(f32[1152]{0:T(1024)} %copy-done.188) | copy-start | bytes 13828
  1143.8 42.2 %copy-start.7 = (f32[256,1152]{1,0:T(8,128)S(1)}, f32[256,1152]{1,0:T(8,128)}, u32[]{:S(2)}) copy-start(f32[256,1152]{1,0:T(8,128)} %copy-done.6) | copy-start | bytes 3538948
  1189.6 231.3 %collective-permute-start.17 = (f32[256,1152]{1,0:T(8,128)}, f32[256,1152]{1,0:T(8,128)}, u32[]{:S(2)}, u32[]{:S(2)}) collective-permute-start(f32[256,1152]{1,0:T(8,128)} %get-tuple-element.104), channel_id=1, source_target_pairs={{0,16},{16,0},{1,17},{17,1},{2,18},{18,2},{3,19},{19,3},{4,20},{20... | collective-permute-start | bytes 3538952 | tf_op jit(solution)/shard_map/ppermute | solution.py:26
  1189.7 149.4 %collective-permute-start.36 = (f32[6,576]{1,0:T(8,128)S(1)}, f32[6,576]{1,0:T(8,128)S(1)}, u32[]{:S(2)}, u32[]{:S(2)}) collective-permute-start(f32[6,576]{1,0:T(8,128)S(1)} %dynamic-slice_select_fusion), channel_id=1, source_target_pairs={{0,16},{16,0},{1,17},{17,1},{2,18},{18,2},{3,19},{19,3},{4,20},{20... | collective-permute-start | bytes 41480 | tf_op jit(solution)/shard_map/ppermute | solution.py:26
  1339.2 84.7 %collective-permute-start.34 = (f32[3,144,1152]{2,1,0:T(8,128)}, f32[3,144,1152]{2,1,0:T(8,128)}, u32[]{:S(2)}, u32[]{:S(2)}) collective-permute-start(f32[3,144,1152]{2,1,0:T(8,128)} %select_bitcast_fusion.1), channel_id=1, source_target_pairs={{0,16},{16,0},{1,17},{17,1},{2,18},{18,2},{3,19},{19,3},{4,20},{20... | collective-permute-start | bytes 5971976 | tf_op jit(solution)/shard_map/ppermute | solution.py:26
  1370.4 44.4 %copy-start.184 = (f32[16,144]{1,0:T(8,128)S(1)}, f32[16,144]{1,0:T(8,128)}, u32[]{:S(2)}) copy-start(f32[16,144]{1,0:T(8,128)} %copy-done.183) | copy-start | bytes 27652
  (318 other events, 1450.6 us)
Sparse Core Ops, SparseCore 0:
  897.8 69.3 reduce-scatter.14
  971.3 69.3 reduce-scatter.16
  1044.4 69.3 reduce-scatter.12
  1117.8 70.2 reduce-scatter.10
  1191.6 69.2 reduce-scatter.8
  1264.8 69.9 reduce-scatter.6

commit v2 on v1

v2 whole, which is shorter than its diff:
```python
import math

import jax
import jax.numpy as jnp
from jax import lax
from jax.experimental import pallas as pl
from jax.experimental.pallas import tpu as pltpu
from jax.sharding import PartitionSpec as P

PRECISE = lax.Precision.HIGHEST
EPSILON = 1e-06
NEGATIVE = -1e30
MESH = pl.DeviceIdType.MESH
BF = jnp.bfloat16
VMEM_BYTES = 62 * 1024 * 1024
F32 = jnp.float32


def time_features(step_ids, model_width):
    half_width = model_width // 2
    frequency = jnp.exp(-math.log(10000.0) * jnp.arange(half_width).astype(F32) / half_width)
    angles = step_ids.astype(F32)[..., None] * frequency
    return jnp.concatenate([jnp.cos(angles), jnp.sin(angles)], axis=-1)


def swap(value, axis):
    return lax.ppermute(value, axis, [(0, 1), (1, 0)])


def pick(index, first, second):
    return jnp.where(index == 0, first, second)


def mine(c, pair):
    return pick(c, pair[0], pair[1])


def both(value):
    c = lax.axis_index("section")
    got = swap(value, "section")
    return pick(c, value, got), pick(c, got, value)


HEAD_LANES = 384


def nn(a, b):
    return lax.dot_general(a, b, (((1,), (0,)), ((), ())), preferred_element_type=F32)


def nt(a, b):
    return lax.dot_general(a, b, (((1,), (1,)), ((), ())), preferred_element_type=F32)


def tn(a, b):
    return lax.dot_general(a, b, (((0,), (0,)), ((), ())), preferred_element_type=F32)


def flat(value):
    return value.reshape(value.shape[0] * value.shape[1], value.shape[2])


GELU_SCALE = math.sqrt(2.0 / math.pi)


def gelu_both(v):
    t = jnp.tanh(GELU_SCALE * (v + 0.044715 * v * v * v))
    slope = 0.5 * (1.0 + t) + (0.5 * GELU_SCALE) * v * (1.0 - t * t) * (1.0 + 0.134145 * v * v)
    return 0.5 * v * (1.0 + t), slope


class Place:
    def __init__(self, chain):
        self.chain = chain
        self.core = lax.axis_index("section")
        self.dp = lax.axis_index("dp")
        self.head = lax.axis_index("head")
        self.z = self.dp // 2
        self.y = self.dp % 2
        self.mate_z = self.z + 1 - 2 * (self.z % 2)
        self.above = (self.core, self.dp + 2, self.head)
        self.below = (self.core, self.dp - 2, self.head)
        self.across = (self.core, self.z * 2 + 1 - self.y, self.head)
        self.mate = (self.core, self.mate_z * 2 + self.y, self.head)
        self.other = (1 - self.core, self.dp, self.head)
        self.beside = (self.core, self.dp, 1 - self.head)

    def greet(self, whole):
        barrier = pltpu.get_barrier_semaphore()

        def tell(device):
            pl.semaphore_signal(barrier, inc=1, device_id=device, device_id_type=MESH)

        tell(self.other)
        tell(self.beside)
        if not whole:
            pl.semaphore_wait(barrier, 2)
            return
        tell(self.across)

        @pl.when(self.z < self.chain - 1)
        def _():
            tell(self.above)

        @pl.when(self.z > 0)
        def _():
            tell(self.below)

        @pl.when((self.z > 0) & (self.z < self.chain - 1))
        def _():
            pl.semaphore_wait(barrier, 5)

        @pl.when((self.z == 0) | (self.z == self.chain - 1))
        def _():
            pl.semaphore_wait(barrier, 4)


def remote(src, dst, ssem, rsem, device):
    return pltpu.make_async_remote_copy(
        src_ref=src, dst_ref=dst, send_sem=ssem, recv_sem=rsem, device_id=device, device_id_type=MESH
    )


class Numbered:
    def __init__(self, ref):
        self.ref = ref
        self.count = 0

    def next(self):
        self.count += 1
        assert self.count <= self.ref.shape[0]
        return self.ref.at[self.count - 1]


class Gather:
    def __init__(self, at, own, w, ssem, rsem, lsem):
        self.at, self.own, self.w = at, own, w
        self.ssem, self.rsem, self.lsem = ssem, rsem, lsem
        self.pieces = own.shape[0]

    def block(self, p, zz, yy):
        return self.w.at[p, self.at.core, zz * 2 + yy]

    def copy(self, src, dst, p, kind, device):
        return remote(src, dst, self.ssem.at[p, kind], self.rsem.at[p, kind], device)

    def up(self, p, k):
        b = self.block(p, self.at.z - (k - 1), self.at.y)
        return self.copy(self.own.at[p] if k == 1 else b, b, p, k - 1, self.at.above)

    def up_in(self, p, k):
        b = self.block(p, self.at.z - k, self.at.y)
        return self.copy(b, b, p, k - 1, self.at.below)

    def down(self, p, k):
        b = self.block(p, self.at.z + (k - 1), self.at.y)
        return self.copy(
            self.own.at[p] if k == 1 else b, b, p, self.at.chain + k - 1, self.at.below
        )

    def down_in(self, p, k):
        b = self.block(p, self.at.z + k, self.at.y)
        return self.copy(b, b, p, self.at.chain + k - 1, self.at.above)

    def cross(self, p, zz, own=False):
        b = self.block(p, zz, self.at.y)
        return self.copy(self.own.at[p] if own else b, b, p, 2 * self.at.chain + zz, self.at.across)

    def cross_in(self, p, zz):
        b = self.block(p, zz, 1 - self.at.y)
        return self.copy(b, b, p, 2 * self.at.chain + zz, self.at.across)

    def mate_out(self, p):
        b = self.block(p, self.at.z, 1 - self.at.y)
        return self.copy(b, b, p, 3 * self.at.chain, self.at.mate)

    def mate_in(self, p):
        b = self.block(p, self.at.mate_z, 1 - self.at.y)
        return self.copy(b, b, p, 3 * self.at.chain, self.at.mate)

    def other_out(self, p):
        b = self.w.at[p, self.at.core]
        return self.copy(b, b, p, 3 * self.at.chain + 1, self.at.other)

    def other_in(self, p):
        b = self.w.at[p, 1 - self.at.core]
        return self.copy(b, b, p, 3 * self.at.chain + 1, self.at.other)

    def local(self, p):
        return pltpu.make_async_copy(
            self.own.at[p], self.block(p, self.at.z, self.at.y), self.lsem.at[p]
        )

    def start(self, p):
        self.local(p).start()
        self.cross(p, self.at.z, True).start()

        @pl.when(self.at.z < self.at.chain - 1)
        def _():
            self.up(p, 1).start()

        @pl.when(self.at.z > 0)
        def _():
            self.down(p, 1).start()

    def step(self, p, k):
        z, chain = self.at.z, self.at.chain
        odd = p % 2 == 1

        @pl.when(z >= k)
        def _():
            self.up_in(p, k).wait_recv()

            @pl.when(z < chain - 1)
            def _():
                self.up(p, k + 1).start()

            if k == 1 and odd:

                @pl.when(z % 2 == 0)
                def _():
                    self.cross(p, z - k).start()

            else:
                self.cross(p, z - k).start()

        @pl.when(z + k < chain)
        def _():
            self.down_in(p, k).wait_recv()

            @pl.when(z > 0)
            def _():
                self.down(p, k + 1).start()

            if k == 1 and odd:

                @pl.when(z % 2 == 1)
                def _():
                    self.cross(p, z + k).start()

            else:
                self.cross(p, z + k).start()

        if k == 1 and odd:
            self.cross_in(p, z).wait_recv()
            self.mate_out(p).start()

    def finish(self, p):
        z = self.at.z
        self.local(p).wait()
        for j in range(self.at.chain):
            if p % 2 == 1:

                @pl.when((j != z) & (j != self.at.mate_z))
                def _():
                    self.cross_in(p, j).wait_recv()

            else:
                self.cross_in(p, j).wait_recv()
        if p % 2 == 1:
            self.mate_in(p).wait_recv()
        self.other_out(p).start()

    def drain(self, p):
        z, chain = self.at.z, self.at.chain
        for j in range(chain):
            if p % 2 == 1:

                @pl.when(j != self.at.mate_z)
                def _():
                    self.cross(p, j).wait_send()

            else:
                self.cross(p, j).wait_send()
        if p % 2 == 1:
            self.mate_out(p).wait_send()
        for k in range(1, chain):

            @pl.when((z < chain - 1) & (z >= k - 1))
            def _():
                self.up(p, k).wait_send()

            @pl.when((z > 0) & (z + k - 1 < chain))
            def _():
                self.down(p, k).wait_send()

        self.other_out(p).wait_send()


TILE = 32


def by_rows(rows, body, carry, tile=TILE):
    def step(i, c):
        return body(pl.ds(pl.multiple_of(i * tile, tile), tile), c)

    return lax.fori_loop(0, rows // tile, step, carry)


def column_sum(value):
    rows, width = value.shape
    return jnp.sum(value.reshape(rows // 8, 8, width), axis=0)


def layer_norm(v):
    cen = v - jnp.mean(v, axis=-1, keepdims=True)
    inv = lax.rsqrt(jnp.mean(cen * cen, axis=-1, keepdims=True) + EPSILON)
    return cen * inv, inv


def layer_norm_back(w, hat, inv):
    return inv * (
        w - jnp.mean(w, axis=-1, keepdims=True) - hat * jnp.mean(w * hat, axis=-1, keepdims=True)
    )


def head_mask(i, head_dim):
    lane = lax.broadcasted_iota(jnp.int32, (1, HEAD_LANES), 1)
    return ((lane >= i * head_dim) & (lane < (i + 1) * head_dim)).astype(F32)


def forward_kernel(cfg, *refs):
    fused, chain, heads, head_dim = cfg
    refs = list(refs)
    own = refs.pop(0)
    tok, mod, bqv, bout, bup, bdown, rel, pos, seg, place, drop, mtok = refs[:12]
    refs = refs[12:]
    w = refs.pop(0) if fused else own
    s_hat1, s_inv, s_n1, s_qkv, s_p, s_o, s_branch, s_hat2, s_n2, s_hid, s_slope, s_y, outs = refs[:13]
    refs = refs[13:]
    (
        wa, wu, wd, res, hat, inv, n, r, qkv, prob, o, branch, hid, slope, y_keep,
        xs, xr, toep, gs, gr, gl, ssem, rsem, lsem,
    ) = refs
    at = Place(chain)
    rows, width = res.shape
    half_heads = heads // 2
    scale = 1.0 / math.sqrt(head_dim)
    sends, recvs, locals_ = Numbered(ssem), Numbered(rsem), Numbered(lsem)
    at.greet(fused)
    gather = Gather(at, own, w, gs, gr, gl) if fused else None
    waiting = {}

    def keep(name, src, dst):
        copy = pltpu.make_async_copy(src, dst, locals_.next())
        copy.start()
        waiting.setdefault(name, []).append(copy.wait)

    def give(name, src, dst):
        copy = remote(src, dst, sends.next(), recvs.next(), at.other)
        copy.start()
        waiting.setdefault(name, []).append(copy.wait_send)
        waiting.setdefault("end", []).append(copy.wait_recv)

    def settle(name):
        for wait in waiting.pop(name, []):
            wait()

    def pump(*what):
        if not fused:
            return
        for name, p, *k in what:
            if p < gather.pieces:
                getattr(gather, name)(p, *k)

    def load(p, slot):
        if fused:
            gather.other_in(p).wait_recv()
        copy = pltpu.make_async_copy(w.at[p], slot, locals_.next())
        copy.start()
        copy.wait()

    def send_across(i):
        copy = remote(xs.at[i], xr.at[i], sends.next(), recvs.next(), at.beside)
        copy.start()
        waiting.setdefault("end", []).append(copy.wait_send)
        return copy

    def total(i, ds):
        return xs[i, ds, :].astype(F32) + xr[i, ds, :].astype(F32)

    def norm_one(s):
        settle("hat1")
        settle("n1")
        settle("inv")

        def body(ds, c):
            v, iv = layer_norm(res[ds, :])
            hat[0, ds, :] = v.astype(BF)
            inv[0, ds, :] = jnp.broadcast_to(iv, (TILE, 128))
            n[0, ds, :] = (v * (1.0 + mod[s, 1:2, :]) + mod[s, 0:1, :]).astype(BF)
            return c

        by_rows(rows, body, 0)
        keep("hat1", hat.at[0], s_hat1.at[s])
        keep("n1", n.at[0], s_n1.at[s, 0])
        give("n1", n.at[0], s_n1.at[s, 1])

    def project(s):
        settle("qkv")
        for half in range(2):
            for j in range(3):
                cols = slice(j * 384, (j + 1) * 384)
                r[:, cols] = nn(n[0], flat(wa[half, :, :, cols]))

            def body(ds, c):
                v = r[ds, :]
                for kind, shift in ((0, 864), (1, 576), (2, 288)):
                    part = pltpu.roll(v, shift, 1)[:, :HEAD_LANES]
                    row = s * 8 + half * 4 + kind
                    qkv[kind, half, ds, :] = (part + bqv[row : row + 1, :]).astype(BF)
                return c

            by_rows(rows, body, 0)
        keep("qkv", qkv, s_qkv.at[s])

    def attend(s, half):
        if half == 0:
            settle("p")
            settle("o")
        o[half] = jnp.zeros_like(o[half])

        def one(i, c):
            index = half * half_heads + i
            mask = head_mask(i, head_dim).astype(BF)
            line = rel[pl.ds(s * heads + index, 1), :]
            skew = pltpu.roll(jnp.broadcast_to(line, (rows, 2 * rows)), 0, 1, stride=1, stride_axis=0)
            bias = skew[:, :rows]
            if s == 0:
                toep[...] = bias.astype(BF)
                left = nn(pos[...], toep[...]).astype(BF)
                bias = nt(left, pos[...]) + seg[...]
            z = nt(qkv[0, half] * mask, qkv[1, half]) * scale + bias
            e = jnp.exp(z - jnp.max(z, axis=-1, keepdims=True))
            p = (e / jnp.sum(e, axis=-1, keepdims=True)).astype(BF)
            prob[index] = p
            o[half] = o[half] + nn(p, qkv[2, half]).astype(BF) * mask
            return c

        lax.fori_loop(0, half_heads, one, 0)
        if half == 1:
            keep("p", prob, s_p.at[s])
            keep("o", o.at[at.core], s_o.at[s, 0])
            give("o", o.at[1 - at.core], s_o.at[s, 1])

    def project_out(i):
        xs[i] = (
            nt(o[0], flat(wa[0, :, :, :HEAD_LANES])) + nt(o[1], flat(wa[1, :, :, :HEAD_LANES]))
        ).astype(BF)
        return send_across(i)

    def norm_two(s, i, copy):
        copy.wait_recv()
        settle("branch")
        settle("hat2")
        settle("n2")

        def body(ds, c):
            b = total(i, ds) + bout[s : s + 1, :]
            branch[ds, :] = b.astype(BF)
            xm = res[ds, :] + mod[s, 2:3, :] * b
            res[ds, :] = xm
            v, iv = layer_norm(xm)
            hat[1, ds, :] = v.astype(BF)
            inv[1, ds, :] = jnp.broadcast_to(iv, (TILE, 128))
            n[1, ds, :] = (v * (1.0 + mod[s, 4:5, :]) + mod[s, 3:4, :]).astype(BF)
            return c

        by_rows(rows, body, 0)
        keep("branch", branch, s_branch.at[s])
        keep("inv", inv, s_inv.at[s])
        keep("hat2", hat.at[1], s_hat2.at[s])
        keep("n2", n.at[1], s_n2.at[s, 0])
        give("n2", n.at[1], s_n2.at[s, 1])

    def hidden(s, half):
        if half == 0:
            settle("hid")
            settle("slope")
        for j in range(3):
            cols = slice(j * 384, (j + 1) * 384)
            r[:, cols] = nn(n[1], flat(wu[half, :, :, cols])) + bup[s, half : half + 1, cols]

        def body(ds, c):
            value, sl = gelu_both(r[ds, :])
            hid[half, ds, :] = value.astype(BF)
            slope[half, ds, :] = sl.astype(BF)
            return c

        by_rows(rows, body, 0)
        if half == 1:
            keep("slope", slope, s_slope.at[s])
            keep("hid", hid.at[at.core], s_hid.at[s, 0])
            give("hid", hid.at[1 - at.core], s_hid.at[s, 1])

    def project_down(i):
        xs[i] = (nt(hid[0], flat(wd[0])) + nt(hid[1], flat(wd[1]))).astype(BF)
        return send_across(i)

    def end_block(s, i, copy):
        copy.wait_recv()
        settle("y")
        settle("out")

        def body(ds, c):
            v = total(i, ds) + bdown[s : s + 1, :]
            y_keep[ds, :] = v.astype(BF)
            res[ds, :] = res[ds, :] + mod[s, 5:6, :] * v
            return c

        by_rows(rows, body, 0)
        keep("y", y_keep, s_y.at[s])
        keep("out", res, outs.at[s])

    def spread():
        r[...] = nn(place[...], res[...].astype(BF))
        settle("out")

        def body(ds, c):
            res[ds, :] = r[ds, :] + drop[ds, 0:1] * mtok[...]
            return c

        by_rows(rows, body, 0)

    if fused:
        gather.start(0)
        gather.start(1)

    def start_residual(ds, c):
        res[ds, :] = tok[ds, :].astype(F32)
        return c

    by_rows(rows, start_residual, 0)
    norm_one(0)
    pump(("step", 0, 1), ("start", 2), ("step", 0, 2), ("step", 0, 3))
    for s in range(2):
        p = 3 * s
        pump(("step", p + 1, 1), ("start", p + 3), ("finish", p), ("step", p + 1, 2))
        load(p, wa)
        project(s)
        pump(("step", p + 1, 3))
        attend(s, 0)
        pump(("step", p + 2, 1), ("start", p + 4), ("finish", p + 1))
        attend(s, 1)
        copy = project_out(2 * s)
        pump(("step", p + 2, 2))
        norm_two(s, 2 * s, copy)
        pump(("step", p + 2, 3))
        load(p + 1, wu)
        hidden(s, 0)
        pump(("step", p + 3, 1), ("start", p + 5))
        pump(("finish", p + 2))
        hidden(s, 1)
        pump(("step", p + 3, 2))
        load(p + 2, wd)
        copy = project_down(2 * s + 1)
        pump(("step", p + 3, 3))
        end_block(s, 2 * s + 1, copy)
        if s == 0:
            spread()
            norm_one(1)
    if fused:
        for p in range(gather.pieces):
            gather.drain(p)
    for name in list(waiting):
        settle(name)


def forward_call(cfg, own, small, dp_count):
    fused, chain, heads, head_dim = cfg
    rows, width = small[0].shape
    pieces = own.shape[0]
    shard = own.shape[-2]
    groups = width // shard
    bf, f = lambda *s: jax.ShapeDtypeStruct(s, BF), lambda *s: jax.ShapeDtypeStruct(s, F32)
    out_shape = [
        bf(2, rows, width),
        f(2, 2, rows, 128),
        bf(2, 2, rows, width),
        bf(2, 3, 2, rows, HEAD_LANES),
        bf(2, heads, rows, rows),
        bf(2, 2, rows, HEAD_LANES),
        bf(2, rows, width),
        bf(2, rows, width),
        bf(2, 2, rows, width),
        bf(2, 2, rows, width),
        bf(2, 2, rows, width),
        bf(2, rows, width),
        f(2, rows, width),
    ]
    if fused:
        out_shape = [bf(pieces, 2, groups, shard, width)] + out_shape
    kinds = 3 * chain + 2
    slot = pltpu.VMEM((2, groups, shard, width), BF)
    scratch = [
        slot,
        slot,
        slot,
        pltpu.VMEM((rows, width), F32),
        pltpu.VMEM((2, rows, width), BF),
        pltpu.VMEM((2, rows, 128), F32),
        pltpu.VMEM((2, rows, width), BF),
        pltpu.VMEM((rows, width), F32),
        pltpu.VMEM((3, 2, rows, HEAD_LANES), BF),
        pltpu.VMEM((heads, rows, rows), BF),
        pltpu.VMEM((2, rows, HEAD_LANES), BF),
        pltpu.VMEM((rows, width), BF),
        pltpu.VMEM((2, rows, width), BF),
        pltpu.VMEM((2, rows, width), BF),
        pltpu.VMEM((rows, width), BF),
        pltpu.VMEM((4, rows, width), BF),
        pltpu.VMEM((4, rows, width), BF),
        pltpu.VMEM((rows, rows), BF),
        pltpu.SemaphoreType.DMA((pieces, kinds)),
        pltpu.SemaphoreType.DMA((pieces, kinds)),
        pltpu.SemaphoreType.DMA((pieces,)),
        pltpu.SemaphoreType.DMA((16,)),
        pltpu.SemaphoreType.DMA((16,)),
        pltpu.SemaphoreType.DMA((40,)),
    ]

    def body(*refs):
        forward_kernel(cfg, *refs)

    vm = pl.BlockSpec(memory_space=pltpu.VMEM)
    hbm = pl.BlockSpec(memory_space=pl.ANY)
    result = pl.pallas_call(
        body,
        out_shape=out_shape,
        in_specs=[hbm] + [vm] * len(small),
        out_specs=[hbm] * len(out_shape),
        scratch_shapes=scratch,
        compiler_params=pltpu.CompilerParams(
            collective_id=0, has_side_effects=True, vmem_limit_bytes=VMEM_BYTES
        ),
        name="forward_blocks",
    )(own, *small)
    return (result if fused else [own] + list(result))


class Scatter:
    def __init__(self, at, order, g, yr, zr, mr, red, out, ssem, rsem, osem, isem, lsem, credit):
        self.at, self.order = at, order
        self.g, self.yr, self.zr, self.mr, self.red, self.out = g, yr, zr, mr, red, out
        self.ssem, self.rsem, self.osem, self.isem, self.lsem = ssem, rsem, osem, isem, lsem
        self.credit = credit
        chain = at.chain
        need = lambda z, t: chain if t == z else (chain - t + z if t > z else chain - z + t)
        self.table = [sorted(range(chain), key=lambda t: (need(z, t), t)) for z in range(chain)]

    def slots(self, r):
        return r % self.g.shape[0], r % self.yr.shape[0]

    def target(self, i):
        return sum(jnp.where(self.at.z == z, self.table[z][i], 0) for z in range(self.at.chain))

    def own(self, r, t):
        return self.g.at[self.slots(r)[0], t * 2 + self.at.y]

    def theirs(self, r, t):
        return self.g.at[self.slots(r)[0], t * 2 + 1 - self.at.y]

    def copy(self, src, dst, r, kind, device):
        return remote(src, dst, self.ssem.at[r, kind], self.rsem.at[r, kind], device)

    def cross(self, r, t):
        return self.copy(
            self.theirs(r, t), self.yr.at[self.slots(r)[1], t], r, t, self.at.across
        )

    def up(self, r, t):
        return self.copy(
            self.own(r, t), self.zr.at[self.slots(r)[1], t], r, self.at.chain + t, self.at.above
        )

    def down(self, r, t, last=None):
        z = self.at.z - 1 if last is None else last
        place = jnp.where(t == z, self.at.chain, t)
        return self.copy(
            self.own(r, t), self.zr.at[self.slots(r)[1], place], r, 2 * self.at.chain + t, self.at.below
        )

    def to_mate(self, r):
        return self.copy(
            self.theirs(r, self.at.mate_z), self.mr.at[self.slots(r)[1]], r, 3 * self.at.chain, self.at.mate
        )

    def add(self, block, got):
        block[...] = (block[...].astype(F32) + got[...].astype(F32)).astype(BF)

    def begin(self, r):
        at, chain = self.at, self.at.chain
        if r >= self.yr.shape[0]:
            pl.semaphore_wait(self.credit.at[0], 1)

            @pl.when(at.z < chain - 1)
            def _():
                pl.semaphore_wait(self.credit.at[1], 1)

            @pl.when(at.z > 0)
            def _():
                pl.semaphore_wait(self.credit.at[2], 1)

        if r % 2 == 1:
            self.to_mate(r).start()
        for i in range(chain - 1):
            t = self.target(i)
            if r % 2 == 1:

                @pl.when(t != at.mate_z)
                def _():
                    self.cross(r, t).start()

            else:
                self.cross(r, t).start()
        if r % 2 == 0:
            self.cross(r, at.z).start()

    def mated(self, r):
        if r % 2 == 1:
            self.to_mate(r).wait_recv()
            self.add(self.theirs(r, self.at.z), self.mr.at[self.slots(r)[1]])
            self.cross(r, self.at.z).start()

    def arrive(self, r, i):
        t = self.target(i)

        def take():
            self.cross(r, t).wait_recv()
            self.add(self.own(r, t), self.yr.at[self.slots(r)[1], t])

        if r % 2 == 1:
            pl.when(t != self.at.mate_z)(take)
        else:
            take()

    def step(self, r, k):
        z, chain = self.at.z, self.at.chain

        @pl.when((z <= k - 1) & (z < chain - 1))
        def _():
            t = chain - k + z
            if k > 1:

                @pl.when(z > 0)
                def _():
                    self.up(r, t).wait_recv()
                    self.add(self.own(r, t), self.zr.at[self.slots(r)[1], t])

            self.up(r, t).start()

        @pl.when((chain - 1 - z <= k - 1) & (z > 0))
        def _():
            t = k - chain + z
            if k > 1:

                @pl.when(z < chain - 1)
                def _():
                    self.down(r, t, last=z).wait_recv()
                    self.add(self.own(r, t), self.zr.at[self.slots(r)[1], t])

            self.down(r, t).start()

    def finish(self, r):
        at, chain = self.at, self.at.chain
        z = at.z
        slot = self.slots(r)[1]
        if r >= self.yr.shape[0]:
            self.hand_over_done(r - self.yr.shape[0])
        red = self.red.at[slot]
        red[...] = self.own(r, z)[...].astype(F32)

        @pl.when(z > 0)
        def _():
            self.up(r, z).wait_recv()
            red[...] = red[...] + self.zr[slot, z].astype(F32)

        @pl.when(z < chain - 1)
        def _():
            self.down(r, z, last=z).wait_recv()
            red[...] = red[...] + self.zr[slot, chain].astype(F32)

        if r + self.yr.shape[0] < len(self.order):
            pl.semaphore_signal(self.credit.at[0], inc=1, device_id=at.across, device_id_type=MESH)

            @pl.when(z > 0)
            def _():
                pl.semaphore_signal(self.credit.at[1], inc=1, device_id=at.below, device_id_type=MESH)

            @pl.when(z < chain - 1)
            def _():
                pl.semaphore_signal(self.credit.at[2], inc=1, device_id=at.above, device_id_type=MESH)

        s, t = self.order[r]

        @pl.when(at.core == s)
        def _():
            self.keep(r).start()

        @pl.when(at.core != s)
        def _():
            self.hand_over(r).start()

    def keep(self, r):
        return pltpu.make_async_copy(
            self.red.at[self.slots(r)[1]], self.out.at[self.order[r][1], self.at.core], self.lsem.at[r]
        )

    def hand_over(self, r):
        return remote(
            self.red.at[self.slots(r)[1]],
            self.out.at[self.order[r][1], self.at.core],
            self.osem.at[r],
            self.isem.at[r],
            self.at.other,
        )

    def hand_over_done(self, r):
        s, t = self.order[r]

        @pl.when(self.at.core == s)
        def _():
            self.keep(r).wait()

        @pl.when(self.at.core != s)
        def _():
            self.hand_over(r).wait_send()

    def drain(self, r):
        z, chain = self.at.z, self.at.chain
        if r % 2 == 1:
            self.to_mate(r).wait_send()
        for t in range(chain):
            if r % 2 == 1:

                @pl.when(t != self.at.mate_z)
                def _():
                    self.cross(r, t).wait_send()

            else:
                self.cross(r, t).wait_send()

            @pl.when(t > z)
            def _():
                self.up(r, t).wait_send()

            @pl.when(t < z)
            def _():
                self.down(r, t).wait_send()

    def end(self):
        for r in range(len(self.order)):
            if r + self.yr.shape[0] >= len(self.order):
                self.hand_over_done(r)
            s, t = self.order[r]

            @pl.when(self.at.core == s)
            def _():
                remote(
                    self.red.at[0],
                    self.out.at[t, 1 - self.at.core],
                    self.osem.at[r],
                    self.isem.at[r],
                    self.at.other,
                ).wait_recv()


ORDER = ((1, 2), (1, 1), (1, 0), (0, 2), (0, 1), (0, 0))


def backward_kernel(cfg, *refs):
    fused, chain, heads, head_dim = cfg
    refs = list(refs)
    w = refs.pop(0)
    i_hat1, i_inv, i_n1, i_qkv, i_p, i_o, i_branch, i_hat2, i_n2, i_hid, i_slope, i_y = refs[:12]
    refs = refs[12:]
    dout, mod, flips, pos, place, drop = refs[:6]
    refs = refs[6:]
    red_out, o_dx, stats, rel_out = refs[:4]
    refs = refs[4:]
    (
        wslot, hat1, inv, n1, qkv, prob, o, branch, hat2, n2, hid, slope, y_keep,
        d, r, dy, dpre, dattn, dqkv, do, acc, xs, xr, g, yr, zr, mr, red,
        gs, gr, go, gi, gl, credit, ssem, rsem, lsem,
    ) = refs
    at = Place(chain)
    rows, width = d.shape
    half_heads = heads // 2
    scale = 1.0 / math.sqrt(head_dim)
    sends, recvs, locals_ = Numbered(ssem), Numbered(rsem), Numbered(lsem)
    at.greet(fused)
    scatter = (
        Scatter(at, ORDER, g, yr, zr, mr, red, red_out, gs, gr, go, gi, gl, credit) if fused else None
    )
    slots = g.shape[0]
    waiting = {}

    def fetch(name, src, dst):
        copy = pltpu.make_async_copy(src, dst, locals_.next())
        copy.start()
        waiting.setdefault(name, []).append(copy.wait)

    def settle(name):
        for wait in waiting.pop(name, []):
            wait()

    def give(name, src, dst):
        copy = remote(src, dst, sends.next(), recvs.next(), at.other)
        copy.start()
        waiting.setdefault(name + " in", []).append(copy.wait_recv)
        waiting.setdefault(name + " out", []).append(copy.wait_send)

    def pump(*what):
        if not fused:
            return
        for name, r_, *k in what:
            if 0 <= r_ < len(ORDER):
                getattr(scatter, name)(r_, *k)

    def pump_rest(r_, start):
        for i in range(start, chain):
            pump(("arrive", r_, i))
            if i < chain - 1:
                pump(("step", r_, i + 1))
        pump(("finish", r_))

    def send_across(i):
        if i > 1:
            settle("x out %d" % (i - 2))
        copy = remote(xs.at[i % 2], xr.at[i], sends.next(), recvs.next(), at.beside)
        copy.start()
        waiting.setdefault("x in %d" % i, []).append(copy.wait_recv)
        waiting.setdefault("x out %d" % i, []).append(copy.wait_send)

    def total(i, ds):
        return xs[i % 2, ds, :].astype(F32) + xr[i, ds, :].astype(F32)

    def stat(s, row, value):
        stats[s, row : row + 1, :] = jnp.sum(value, axis=0, keepdims=True)

    zero8 = lambda: jnp.zeros((8, width), F32)
    spot = lambda half: jnp.where(half == at.core, 0, 2)

    def loads(s):
        fetch("y", i_y.at[s], y_keep)
        fetch("slope", i_slope.at[s], slope)
        fetch("hid", i_hid.at[s], hid)
        fetch("n2", i_n2.at[s], n2)
        fetch("hat2", i_hat2.at[s], hat2)
        fetch("inv", i_inv.at[s], inv)
        fetch("branch", i_branch.at[s], branch)
        fetch("p", i_p.at[s], prob)
        fetch("qkv", i_qkv.at[s], qkv)
        fetch("o", i_o.at[s], o)
        fetch("n1", i_n1.at[s], n1)
        fetch("hat1", i_hat1.at[s], hat1)

    def product(r_, parts):
        slot = r_ % slots
        if r_ >= slots:
            if fused:
                scatter.drain(r_ - slots)
            else:
                settle("g%d" % (r_ - slots))
        for j in range(width // 384):
            cols = slice(j * 384, (j + 1) * 384)
            value = 0.0
            for lhs, rhs in parts(j):
                value = value + tn(lhs, rhs)
            g[slot, :, :, cols] = value.astype(BF).reshape(g.shape[1], g.shape[2], 384)
        if not fused:
            s, t = ORDER[r_]
            fetch("g%d" % r_, g.at[slot], red_out.at[s * 3 + t])

    def cols_of(ref, j):
        return flat(ref[0:2, :, j * 384 : (j + 1) * 384])

    def block_back(s):
        base = 0 if s == 1 else 3
        xi = 0 if s == 1 else 2
        first, second, third = (0, 1, 0) if s == 1 else (1, 0, 1)
        settle("y")
        settle("dy out")

        def one(ds, c):
            a, b = c
            dv = d[ds, :]
            v = (dv * mod[s, 5:6, :]).astype(BF)
            dy[0, ds, :] = v
            return (
                a + column_sum(dv * y_keep[ds, :].astype(F32)),
                b + column_sum(v.astype(F32)),
            )

        a, b = by_rows(rows, one, (zero8(), zero8()))
        stat(s, 5, a)
        stat(s, 6, b)
        give("dy", dy.at[0], dy.at[1])
        settle("w%d" % first)
        settle("slope")
        settle("dpre out")
        for half in range(2):
            for j in range(3):
                cols = slice(j * 384, (j + 1) * 384)
                v = (nn(dy[0], flat(wslot[first, half, :, :, cols])) * slope[half, :, cols].astype(F32)).astype(BF)
                dpre[spot(half), :, cols] = v
                stats[s, 8 + half : 9 + half, cols] = jnp.sum(v.astype(F32), axis=0, keepdims=True)
        give("dpre", dpre.at[2], dpre.at[1])
        fetch("w%d" % first, w.at[3 * s], wslot.at[first])
        settle("w%d" % second)
        if xi > 1:
            settle("x out %d" % (xi - 2))
        xs[xi % 2] = (
            nt(dpre[spot(0)], flat(wslot[second, 0])) + nt(dpre[spot(1)], flat(wslot[second, 1]))
        ).astype(BF)
        send_across(xi)
        if s == 1:
            fetch("w%d" % second, w.at[2], wslot.at[second])
        settle("dy in")
        settle("hid")
        product(base, lambda j: [(flat(dy[...]), cols_of(hid, j))])
        pump(("begin", base))
        if s == 0:
            pump_rest(2, 0)
        settle("dpre in")
        settle("n2")
        product(base + 1, lambda j: [(flat(n2[...]), cols_of(dpre, j))])
        pump(("begin", base + 1))
        settle("x in %d" % xi)
        settle("hat2")
        settle("inv")
        settle("branch")
        settle("dattn out")

        def two(ds, c):
            c0, c1, c2, c3 = c
            dn = total(xi, ds)
            hv = hat2[ds, :].astype(F32)
            dxm = d[ds, :] + layer_norm_back(dn * (1.0 + mod[s, 4:5, :]), hv, inv[1, ds, 0:1])
            d[ds, :] = dxm
            da = (dxm * mod[s, 2:3, :]).astype(BF)
            dattn[0, ds, :] = da
            return (
                c0 + column_sum(dn),
                c1 + column_sum(dn * hv),
                c2 + column_sum(dxm * branch[ds, :].astype(F32)),
                c3 + column_sum(da.astype(F32)),
            )

        c0, c1, c2, c3 = by_rows(rows, two, (zero8(),) * 4)
        stat(s, 3, c0)
        stat(s, 4, c1)
        stat(s, 2, c2)
        stat(s, 7, c3)
        give("dattn", dattn.at[0], dattn.at[1])
        settle("w%d" % third)
        settle("p")
        settle("qkv")
        settle("dqkv out")
        for half in range(2):
            if half == 0:
                pump(("mated", base))
            pump(("arrive", base, half))
            if half < chain - 1:
                pump(("step", base, half + 1))
            do[half] = nn(dattn[0], flat(wslot[third, half, :, :, :HEAD_LANES])).astype(BF)
            acc[...] = jnp.zeros_like(acc)

            def head(i, c):
                index = half * half_heads + i
                mask = head_mask(i, head_dim)
                low_mask = mask.astype(BF)
                p = prob[index]
                dom = do[half] * low_mask
                acc[2] = acc[2] + tn(p, dom)
                ds = nt(dom, qkv[2, half])
                pf = p.astype(F32)
                dz = (pf * (ds - jnp.sum(pf * ds, axis=-1, keepdims=True))).astype(BF)
                acc[0] = acc[0] + nn(dz, qkv[1, half]) * mask
                acc[1] = acc[1] + tn(dz, qkv[0, half]) * mask
                square = tn(flips[s], dz)
                if s == 0:
                    high = square.astype(BF)
                    low = (square - high.astype(F32)).astype(BF)
                    square = nn(high, pos[...]) + nn(low, pos[...])
                wide = jnp.concatenate([square, jnp.zeros_like(square)], axis=1)
                skew = pltpu.roll(wide, 0, 1, stride=1, stride_axis=0)
                rel_out[pl.ds(s * heads + index, 1), :] = jnp.sum(skew, axis=0, keepdims=True)
                return c

            lax.fori_loop(0, half_heads, head, 0)
            where = spot(half)

            def gather_rows(ds, c):
                blank = jnp.zeros((TILE, HEAD_LANES), F32)
                v = 0.0
                for kind, shift, factor in ((0, 288, scale), (1, 576, scale), (2, 864, 1.0)):
                    part = jnp.concatenate([acc[kind, ds, :] * factor, blank, blank], axis=1)
                    v = v + pltpu.roll(part, shift, 1)
                v = v.astype(BF)
                dqkv[where, ds, :] = v
                return c + column_sum(v.astype(F32))

            stat(s, 10 + half, by_rows(rows, gather_rows, zero8()))
        give("dqkv", dqkv.at[2], dqkv.at[1])
        xs_free = xi + 1
        if xs_free > 1:
            settle("x out %d" % (xs_free - 2))
        xs[xs_free % 2] = (
            nt(dqkv[spot(0)], flat(wslot[third, 0])) + nt(dqkv[spot(1)], flat(wslot[third, 1]))
        ).astype(BF)
        send_across(xs_free)
        if s == 1:
            fetch("w%d" % third, w.at[1], wslot.at[third])
        settle("dqkv in")
        settle("dattn in")
        settle("n1")
        settle("o")
        product(
            base + 2,
            lambda j: [(flat(n1[...]), cols_of(dqkv, j))]
            + ([(flat(dattn[...]), flat(o[...]))] if j == 0 else []),
        )
        pump(("begin", base + 2))
        settle("x in %d" % xs_free)
        settle("hat1")

        def three(ds, c):
            c0, c1, c2 = c
            dn = total(xs_free, ds)
            hv = hat1[ds, :].astype(F32)
            dx = d[ds, :] + layer_norm_back(dn * (1.0 + mod[s, 1:2, :]), hv, inv[0, ds, 0:1])
            d[ds, :] = dx
            return (c0 + column_sum(dn), c1 + column_sum(dn * hv), c2 + column_sum(dx * drop[ds, 0:1]))

        c0, c1, c2 = by_rows(rows, three, (zero8(),) * 3)
        stat(s, 0, c0)
        stat(s, 1, c1)
        stat(s, 12, c2)
        fetch("dx", d, o_dx.at[s])
        pump_rest(base, 2)

    loads(1)
    fetch("w0", w.at[5], wslot.at[0])
    fetch("w1", w.at[4], wslot.at[1])

    def start_rows(ds, c):
        d[ds, :] = dout[ds, :].astype(F32)
        return c

    by_rows(rows, start_rows, 0)
    block_back(1)
    loads(0)
    r[...] = tn(place[...], d[...].astype(BF))
    settle("dx")

    def move(ds, c):
        d[ds, :] = r[ds, :]
        return c

    by_rows(rows, move, 0)
    pump(("mated", 1))
    pump_rest(1, 0)
    block_back(0)
    for r_ in (4, 5):
        pump(("mated", r_))
        pump_rest(r_, 0)
    if fused:
        for r_ in range(len(ORDER) - slots, len(ORDER)):
            scatter.drain(r_)
        scatter.end()
    for name in list(waiting):
        settle(name)


def backward_call(cfg, w, saved, small):
    fused, chain, heads, head_dim = cfg
    rows, width = small[0].shape
    pieces, _, groups, shard, _ = w.shape
    bf, f = lambda *s: pltpu.VMEM(s, BF), lambda *s: pltpu.VMEM(s, F32)
    dma = lambda *s: pltpu.SemaphoreType.DMA(s)
    out_shape = [
        jax.ShapeDtypeStruct((3, 2, shard, width), F32)
        if fused
        else jax.ShapeDtypeStruct((pieces, groups, shard, width), BF),
        jax.ShapeDtypeStruct((2, rows, width), F32),
        jax.ShapeDtypeStruct((2, 16, width), F32),
        jax.ShapeDtypeStruct((2 * heads, 2 * rows), F32),
    ]
    some = 3 if fused else 1
    links = chain if fused else 1
    block = shard if fused else 16
    scratch = [
        bf(2, 2, groups, shard, width),
        bf(rows, width),
        f(2, rows, 128),
        bf(2, rows, width),
        bf(3, 2, rows, HEAD_LANES),
        bf(heads, rows, rows),
        bf(2, rows, HEAD_LANES),
        bf(rows, width),
        bf(rows, width),
        bf(2, rows, width),
        bf(2, rows, width),
        bf(2, rows, width),
        bf(rows, width),
        f(rows, width),
        f(rows, width),
        bf(2, rows, width),
        bf(3, rows, width),
        bf(2, rows, width),
        bf(3, rows, width),
        bf(2, rows, HEAD_LANES),
        f(3, rows, HEAD_LANES),
        bf(2, rows, width),
        bf(4, rows, width),
        bf(4, groups, shard, width),
        bf(some, links, block, width),
        bf(some, links + 1, block, width),
        bf(some, block, width),
        f(some, block, width),
        dma(6, 3 * links + 1),
        dma(6, 3 * links + 1),
        dma(6),
        dma(6),
        dma(6),
        pltpu.SemaphoreType.REGULAR((3,)),
        dma(16),
        dma(16),
        dma(48),
    ]

    def body(*refs):
        backward_kernel(cfg, *refs)

    vm = pl.BlockSpec(memory_space=pltpu.VMEM)
    hbm = pl.BlockSpec(memory_space=pl.ANY)
    return pl.pallas_call(
        body,
        out_shape=out_shape,
        in_specs=[hbm] * (1 + len(saved)) + [vm] * len(small),
        out_specs=[hbm, hbm, vm, vm],
        scratch_shapes=scratch,
        compiler_params=pltpu.CompilerParams(
            collective_id=1, has_side_effects=True, vmem_limit_bytes=VMEM_BYTES
        ),
        name="backward_blocks",
    )(w, *saved, *small)


def per_device(
    tokens,
    kept_mask,
    timesteps,
    labels,
    w_qkv,
    b_qv,
    w_out,
    b_out,
    w_up,
    b_up,
    w_down,
    b_down,
    w_ada,
    b_ada,
    rel_table,
    mask_token,
    class_table,
    out_grad,
):
    micro, rows, width = tokens.shape
    length = kept_mask.shape[2]
    classes = class_table.shape[0]
    heads = rel_table.shape[1]
    lw = w_qkv.shape[3]
    head_dim = lw // heads
    hw = lw // 2
    ff = w_up.shape[2]
    fw = ff // 2
    dp_count = lax.axis_size("dp")
    c = lax.axis_index("section")
    dp = lax.axis_index("dp")
    h = lax.axis_index("head")

    qkv = jnp.transpose(w_qkv[0], (1, 0, 2))
    out_t = w_out[0].T
    down_t = w_down[0].T
    pack = []
    for half in range(2):
        at = slice(half * hw, (half + 1) * hw)
        fat = slice(half * fw, (half + 1) * fw)
        a = jnp.concatenate([out_t[:, at], qkv[0][:, at], qkv[1][:, at], qkv[2][:, at]], axis=1)
        pack.append(jnp.stack([a, w_up[0][:, fat], down_t[:, fat]]))
    keep = mine(c, pack)
    got = swap(mine(1 - c, pack), "section")
    own = jnp.concatenate([pick(c, keep, got), pick(c, got, keep)])
    ids = lax.all_gather(jnp.stack([labels[:, 0], timesteps[:, 0]]), "dp")
    labels_all = ids[:, 0].reshape(-1)
    steps_all = ids[:, 1].reshape(-1)
    label_pick = (labels_all[:, None] == jnp.arange(classes)[None, :]).astype(BF)
    cond = nn(label_pick, class_table) + time_features(steps_all, width)
    cond_low = jax.nn.silu(cond)
    fr = width // dp_count
    cond_part = lax.dynamic_slice_in_dim(cond_low, dp * fr, fr, 1)
    ada = w_ada[0].astype(F32).reshape(fr, 6 * lw)
    part = jnp.dot(cond_part, ada, precision=PRECISE).reshape(dp_count, micro, 6, lw)
    summed = jnp.sum(lax.all_to_all(part, "dp", 0, 0, tiled=True), axis=0) + b_ada[0].astype(F32)
    mod_own = mine(c, summed)
    mod_got = swap(mine(1 - c, summed), "section")
    mod_half = jnp.stack([pick(c, mod_own, mod_got), pick(c, mod_got, mod_own)])
    mod_other = swap(mod_half, "head")
    mod = jnp.concatenate(
        [pick(h, mod_half, mod_other), pick(h, mod_other, mod_half)], axis=2
    )

    def shared(value):
        return both(value[0].astype(BF))

    b_qv2, b_out2, b_up2, b_down2, rel2 = [
        [v.astype(F32) for v in shared(t)] for t in (b_qv, b_out, b_up, b_down, rel_table)
    ]


    kept = kept_mask[c, 0]
    source = jnp.cumsum(kept) - 1
    count = jnp.sum(kept)
    span = jnp.arange(length, dtype=jnp.int32)
    place = ((kept[:, None] == 1) & (source[:, None] == span[None, :])).astype(BF)
    pad = span >= count
    pos = place.T + (pad[:, None] & (span[None, :] == 0)).astype(BF)
    seg = jnp.where(pad[:, None] == pad[None, :], 0.0, NEGATIVE)
    mirror = (span[:, None] + span[None, :] == length - 1).astype(BF)
    flips = jnp.stack([pos[:, ::-1], mirror])
    drop = jnp.broadcast_to((1 - kept)[:, None].astype(F32), (rows, 128))

    lanes = HEAD_LANES - hw
    rel_rows = jnp.stack(rel2)
    blank = jnp.zeros((2, heads, 1), F32)
    rel_rows = jnp.concatenate(
        [rel_rows[:, :, length - 1 :: -1], blank, rel_rows[:, :, : length - 1 : -1]], axis=2
    ).reshape(2 * heads, 2 * length)
    bqv = jnp.stack(b_qv2).reshape(2, 2, 2, hw)
    none = jnp.zeros((2, 2, hw), F32)
    bqv = jnp.stack([bqv[:, 0], none, bqv[:, 1], none], axis=2)
    bqv = jnp.pad(bqv, ((0, 0), (0, 0), (0, 0), (0, lanes))).reshape(16, HEAD_LANES)
    mod = jnp.pad(mod, ((0, 0), (0, 2), (0, 0)))
    fused = (width // dp_count) % 16 == 0
    cfg = (fused, dp_count // 2, heads, head_dim)
    if fused:
        source_w = own
    else:
        half_w_ = lax.all_gather(own, "dp", axis=1, tiled=True)
        other_w = swap(half_w_, "section")
        source_w = jnp.stack([pick(c, half_w_, other_w), pick(c, other_w, half_w_)], axis=1)
        source_w = source_w.reshape(6, 2, 8, width // 8, own.shape[2])
    small_in = (
        tokens[c],
        mod,
        bqv,
        jnp.stack(b_out2),
        jnp.stack(b_up2).reshape(2, 2, fw),
        jnp.stack(b_down2),
        rel_rows,
        pos,
        seg,
        place,
        drop,
        mask_token.astype(F32)[None, :],
    )
    full, *saved, outs = forward_call(cfg, source_w, small_in, dp_count)
    small_back = (out_grad[c], mod, flips, pos, place, drop)
    red, dx, stats, rel_out = backward_call(cfg, full, saved, small_back)
    rel_out = rel_out.reshape(2, heads, 2 * length)[:, :, 2 * length - 2 :: -1]

    if fused:
        g0, g1 = red[:, 0], red[:, 1]
    else:
        red = lax.psum_scatter(
            red.reshape(6, width, own.shape[2]), "dp", scatter_dimension=1, tiled=True
        ).astype(F32)
        red = red.reshape(2, 3, fr, own.shape[2])
        g_own = mine(c, red)
        g_got = swap(mine(1 - c, red), "section")
        g0, g1 = pick(c, g_own, g_got), pick(c, g_got, g_own)
    g_qkv = jnp.stack(
        [
            jnp.concatenate([g0[0][:, i * hw : (i + 1) * hw], g1[0][:, i * hw : (i + 1) * hw]], axis=1)
            for i in (1, 2, 3)
        ],
        axis=1,
    )
    g_out = jnp.concatenate([g0[0][:, :hw], g1[0][:, :hw]], axis=1).T
    g_up = jnp.concatenate([g0[1], g1[1]], axis=1)
    g_down = jnp.concatenate([g0[2], g1[2]], axis=1).T
    dmod0, dmod1 = stats[0, :6], stats[1, :6]
    mask_sum = stats[1, 12]

    def small_of(s):
        qv = [stats[s, 10 + half, at * hw : (at + 1) * hw] for at in (1, 3) for half in range(2)]
        return (jnp.concatenate(qv), stats[s, 7], stats[s, 8:10].reshape(-1), stats[s, 6])

    small0, small1 = small_of(0), small_of(1)
    rel0, rel1 = rel_out[0], rel_out[1]

    half_w = width // 2

    def half(v):
        return lax.dynamic_slice_in_dim(v, h * half_w, half_w, v.ndim - 1)

    vecs = []
    for small, rel in ((small0, rel0), (small1, rel1)):
        vecs.append(
            jnp.concatenate([small[0], half(small[1]), small[2], half(small[3]), rel.reshape(-1)])
        )
    mask_half = half(mask_sum)
    sent = jnp.concatenate([mine(1 - c, vecs), mask_half])
    total = jnp.concatenate([mine(c, vecs), mask_half]) + swap(sent, "section")
    total = lax.psum(total, "dp")
    cuts = [2 * lw, half_w, ff, half_w, heads * (2 * length - 1), half_w]
    parts = []
    at = 0
    for n in cuts:
        parts.append(total[at : at + n])
        at += n
    g_b_qv = parts[0].reshape(2, lw)
    g_rel = parts[4].reshape(heads, 2 * length - 1)

    dm = [half(dmod0), half(dmod1)]
    dm_own = mine(c, dm)
    dm_got = swap(mine(1 - c, dm), "section")
    dm_pair = jnp.stack([pick(c, dm_own, dm_got), pick(c, dm_got, dm_own)])
    dm_all = lax.all_gather(dm_pair, "dp").reshape(dp_count * micro, 6 * lw)
    g_ada = jnp.einsum("id,ie->de", cond_part, dm_all, precision=PRECISE).reshape(fr, 6, lw)
    g_b_ada = jnp.sum(dm_all, axis=0).reshape(6, lw)
    dcl = jnp.einsum("ie,de->id", dm_all, ada, precision=PRECISE)
    dcl = lax.psum(dcl, ("section", "head"))
    dcl = lax.all_gather(dcl, "dp", axis=1, tiled=True)
    sig = jax.nn.sigmoid(cond)
    dcond = half(dcl * (sig * (1.0 + cond * (1.0 - sig))))
    g_class = jnp.einsum("ic,id->cd", label_pick.astype(F32), dcond, precision=PRECISE)

    def settle(first, second):
        got = swap(pick(c, second, first), "section")
        own_part = pick(c, first, second)
        return jnp.stack([pick(c, own_part, got), pick(c, got, own_part)])[None]

    return (
        settle(outs[0], outs[1]),
        settle(dx[0], dx[1]),
        g_qkv[None],
        g_b_qv[None],
        g_out[None],
        parts[1][None],
        g_up[None],
        parts[2][None],
        g_down[None],
        parts[3][None],
        g_ada[None],
        g_b_ada[None],
        g_rel[None],
        parts[5],
        g_class,
    )


def solution(mesh):
    placed = (
        P(None, "dp", None),
        P(None, "dp", None),
        P(None, "dp"),
        P(None, "dp"),
        P("section", "dp", None, "head"),
        P("section", None, "head"),
        P("section", "head", "dp"),
        P("section", None),
        P("section", "dp", "head"),
        P("section", "head"),
        P("section", "head", "dp"),
        P("section", None),
        P("section", "dp", None, "head"),
        P("section", None, "head"),
        P("section", "head", None),
        P(),
        P(),
        P(None, "dp", None),
    )
    return jax.shard_map(
        per_device,
        mesh=mesh,
        in_specs=placed,
        out_specs=(
            P("section", None, "dp", None),
            P("section", None, "dp", None),
            P("section", "dp", None, "head"),
            P("section", None, "head"),
            P("section", "head", "dp"),
            P("section", "head"),
            P("section", "dp", "head"),
            P("section", "head"),
            P("section", "head", "dp"),
            P("section", "head"),
            P("section", "dp", None, "head"),
            P("section", None, "head"),
            P("section", "head", None),
            P("head"),
            P(None, "head"),
        ),
        check_vma=False,
    )
```

time: 1450 us -> 676 us (0.47)
  local copies, waits for them, and re-layouts: 609 us -> 39.1 us
  Pallas kernels: 168 us -> 436 us
  waiting for transfers between devices: 195 us -> 2.29 us
  matrix products: 192 us -> 12 us
  other arithmetic: 103 us -> 36.1 us
  between operations: 19.6 us -> 1.7 us
    gather x4 -> x0, local copies, waits for them, and re-layouts: 482 us -> none  [toeplitz(): return jnp.take(rel, span[:, None] - span[None, :] + length - 1, axis=1)]
    pallas_call x1 -> x2, Pallas kernels: 168 us -> 436 us  [the longest x1 224 us: backward_call(): pl.pallas_call(body, out_shape=out_shape, in_specs=[hbm] * (1 + len(saved...]
    reduce_scatter x6 -> x0, waiting for transfers between devices: 143 us -> none  [per_device(): lax.psum_scatter(t, 'dp', scatter_dimension=0, tiled=True)]
    dot_general x92 -> x0, matrix products: 109 us -> none  [the longest x48 54.5 us: nt(): lax.dot_general(a, b, (((1,), (1,)), ((), ())), preferred_element_type=F32)]
    dot_general x50 -> x1, matrix products: 74.5 us -> 2.22 us  [nn(): lax.dot_general(a, b, (((1,), (0,)), ((), ())), preferred_element_type=F32)]
    ppermute x37 -> x12, waiting for transfers between devices: 51.2 us -> 2.29 us  [swap(): return lax.ppermute(value, axis, [(0, 1), (1, 0)])]
    rev x2, local copies, waits for them, and re-layouts: 30.6 us -> 1.68 us  [the longest x1 1.52 us: per_device(): flips = jnp.stack([pos[:, ::-1], mirror])]
    reduce_sum x39 -> x1, other arithmetic: 28 us -> 0.63 us  [per_device(): count = jnp.sum(kept)]
  transfers between devices with their start and end apart: 44 -> 13, of which waited for: 9 -> 2; matrix products, arithmetic and copies ran while one was open for 59% -> 10% of each run, Pallas kernels for 12% -> 0%
where the time goes in v2:
time: 676 us; the launch traced here: 668 us
  Pallas kernels  436 us (64%)
  blocking collectives  133 us (20%)
  local copies, waits for them, and re-layouts  39.1 us (6%)
  other arithmetic  36.1 us (5%)
  matrix products  12 us (2%)
  starting transfers between devices  8.21 us (1%)
    pallas_call x1, Pallas kernels, backward_call(): pl.pallas_call(body, out_shape=out_shape, in_specs=[hbm] * (1 + len(saved...  224 us
    pallas_call x1, Pallas kernels, forward_call(): pl.pallas_call(body, out_shape=out_shape, in_specs=[hbm] + [vm] * len(sma...  212 us
    psum x1, blocking collectives, per_device(): total = lax.psum(total, 'dp')  36.5 us
    all_gather x1, blocking collectives, per_device(): dm_all = lax.all_gather(dm_pair, 'dp').reshape(dp_count * micro, 6 * lw)  32.9 us
    all_gather x1, blocking collectives, per_device(): dcl = lax.all_gather(dcl, 'dp', axis=1, tiled=True)  30.5 us
    all_gather x1, blocking collectives, per_device(): ids = lax.all_gather(jnp.stack([labels[:, 0], timesteps[:, 0]]), 'dp')  21.9 us
  transfers between devices with their start and end apart: 13, of which 2 were waited for; matrix products, arithmetic and copies ran while one was open for 10% of the time, Pallas kernels for 0%

profile of v2, /device:TPU:0, one launch (start us, length us, event | category | flops | bytes accessed | tf_op | source)
XLA Modules:
  0.0 668.4 jit_solution(9599856489366482298)
XLA Ops:
  1.2 1.3 reduce.7
  2.6 1.3 reduce.5
  4.3 0.7 reduce.6
  6.3 21.9 %all-gather.2 = s32[8,2,2]{2,1,0:T(2,128)S(1)} all-gather(s32[1,2,2]{2,1,0:T(2,128)S(1)} %add_bitcast_fusion), channel_id=2, replica_groups=mesh['section'=2,'dp'=8,'head'=2] {'dp'}, dimensions={0}, use_global_device_ids=true | all-gather | bytes 144 | tf_op jit(solution)/shard_map/all_gather | solution.py:1297
  28.7 2.2 add_divide_fusion
  31.7 1.4 copy.59
  33.1 2.6 reshape.199
  35.7 2.2 dot_general.30
  37.9 2.0 fusion.4
  39.9 0.8 copy.62
  40.7 3.4 all-to-all-start
  47.3 0.8 compare_select_fusion.refs_9_
  48.1 0.8 fusion.10.refs_10_.refs_17_
  49.0 1.5 rev.12
  50.6 0.9 dynamic-slice_bitcast_fusion.1.refs_1_
  51.5 2.0 dynamic-slice_bitcast_fusion.refs_13_
  53.6 0.8 fusion.42
  54.5 1.2 concatenate.52
  56.9 0.7 pad_maximum_fusion.3.refs_15_
  59.2 0.7 broadcast_select_fusion.13
  60.0 0.7 broadcast_select_fusion.15
  62.0 0.7 broadcast_select_fusion.9
  63.4 0.7 select_bitcast_fusion.5
  65.6 1.6 collective-permute-start.2
  67.9 1.8 collective-permute-done.2
  69.7 0.7 select_maximum_fusion.refs_2_.refs_14_
  70.4 1.6 broadcast_select_fusion.2
  72.0 1.5 pad_maximum_fusion.refs_0_
  73.5 0.7 broadcast_in_dim.60.refs_11_.refs_18_
  74.3 212.0 %forward_blocks.1 = (bf16[6,2,8,144,1152]{4,3,2,1,0:T(8,128)(2,1)}, bf16[2,256,1152]{2,1,0:T(8,128)(2,1)}, f32[2,2,256,128]{3,2,1,0:T(8,128)}, bf16[2,2,256,1152...) custom-call(bf16[6,144,1152]{2,1,0:T(8,128)(2,1)} %pad_maximum_fusio, ...), custom_call_target="tpu_custom_call" | custom-call | tf_op jit(solution)/shard_map/forward_blocks/pallas_call | solution.py:627
  286.3 223.8 %backward_blocks.1 = (f32[3,2,144,1152]{3,2,1,0:T(8,128)}, f32[2,256,1152]{2,1,0:T(8,128)}, f32[2,16,1152]{2,1,0:T(8,128)}, f32[16,512]{1,0:T(8,128)}) custom-call(bf16[6,2,8,144,1152]{4,3,2,1,0:T(8,128)(2,1)} %get-tuple-element.34.refs_0_, bf16[2,256,1152]{2,1,0:T(8,128)(2,1)} %get-tuple-element.35.refs_1_, f32[2,2,256,128]{3,2,1,0:T(8,128)} %get-tuple-element.36.refs_2_, ...), custom_call_target="tpu_custom_call" | custom-call | tf_op jit(solution)/shard_map/backward_blocks/pallas_call | solution.py:1238
  510.1 1.0 slice_reduce_fusion.1
  511.1 0.8 fusion.46
  511.9 0.9 fusion.45
  512.7 0.8 fusion.44
  513.5 3.6 slice_bitcast_fusion.1
  518.6 0.7 select_bitcast_fusion.2
  520.1 0.7 pad_maximum_fusion.4
  521.8 1.2 copy-done.3
  523.0 1.1 select_bitcast_fusion
  524.1 1.0 copy-done.2
  525.1 1.1 select_bitcast_fusion.1
  526.8 1.1 maximum_bitcast_fusion.3
  528.3 0.7 copy-done.8
  529.2 1.1 maximum_bitcast_fusion.2
  530.4 1.1 maximum_bitcast_fusion.4
  531.5 0.9 maximum_bitcast_fusion.8
  532.3 0.8 fusion.24
  533.2 32.9 %all-gather.1 = f32[16,6,576]{2,1,0:T(8,128)} all-gather(f32[2,6,576]{2,1,0:T(8,128)S(1)} %pad_maximum_fusion.7), channel_id=3, replica_groups=mesh['section'=2,'dp'=8,'head'=2] {'dp'}, dimensions={0}, use_global_device_ids=true | all-gather | bytes 248832 | tf_op jit(solution)/shard_map/all_gather | solution.py:1432
  566.0 1.8 reshape.205
  567.8 1.9 fusion.49
  569.7 1.1 dot_general.33
  570.7 11.5 %psum.15 = f32[16,144]{1,0:T(8,128)S(1)} all-reduce(f32[16,144]{1,0:T(8,128)S(1)} %fusion.49), channel_id=1, replica_groups=mesh['section'=2,'dp'=8,'head'=2] {'section','head'}, use_global_device_ids=true, to_apply=%region_6.7 | all-reduce | flops 2304 | bytes 18432 | tf_op jit(solution)/shard_map/psum | solution.py:1436
  582.3 30.5 %all-gather.3 = f32[8,144,16]{1,2,0:T(8,128)S(1)} all-gather(f32[1,144,16]{1,2,0:T(8,128)S(1)} %bitcast.186), channel_id=1, replica_groups=mesh['section'=2,'dp'=8,'head'=2] {'dp'}, dimensions={0}, use_global_device_ids=true | all-gather | bytes 82944 | tf_op jit(solution)/shard_map/all_gather | solution.py:1437
  613.0 2.7 fusion.14
  615.7 3.3 convolution_bitcast_fusion
  619.6 0.9 fusion.15
  620.5 36.5 %psum.14 = f32[9272]{0:T(1024)S(1)} all-reduce(f32[9272]{0:T(1024)S(1)} %fusion.15), channel_id=1, replica_groups=mesh['section'=2,'dp'=8,'head'=2] {'dp'}, use_global_device_ids=true, to_apply=%region_4.5 | all-reduce | flops 9272 | bytes 74176 | tf_op jit(solution)/shard_map/psum | solution.py:1418
  658.3 0.7 broadcast_in_dim_reshape.12
  660.8 1.5 fusion.2
  662.3 1.6 maximum_bitcast_fusion
  663.9 0.9 copy-done.4
  664.8 1.5 fusion
  666.3 1.6 maximum_bitcast_fusion.1
  (184 shorter events, 22.5 us)
Async XLA Ops:
  0.6 49.9 %copy-start = (bf16[2,256,1152]{2,1,0:T(8,128)(2,1)S(1)}, bf16[2,256,1152]{2,1,0:T(8,128)(2,1)}, u32[]{:S(2)}) copy-start(bf16[2,256,1152]{2,1,0:T(8,128)(2,1)} %param.18) | copy-start | bytes 3538948
  0.7 57.6 %collective-permute-start.3 = (bf16[2,576]{1,0:T(2,128)(2,1)}, bf16[2,576]{1,0:T(2,128)(2,1)}, u32[]{:S(2)}, u32[]{:S(2)}) collective-permute-start(bf16[2,576]{1,0:T(2,128)(2,1)} %bitcast.194), channel_id=1, source_target_pairs={{0,16},{16,0},{1,17},{17,1},{2,18},{18,2},{3,19},{19,3},{4,20},{20... | collective-permute-start | bytes 6920 | tf_op jit(solution)/shard_map/ppermute | solution.py:27
  2.5 56.7 %collective-permute-start.6 = (bf16[1152]{0:T(1024)(128)(2,1)}, bf16[1152]{0:T(1024)(128)(2,1)}, u32[]{:S(2)}, u32[]{:S(2)}) collective-permute-start(bf16[1152]{0:T(1024)(128)(2,1)} %reduce.7), channel_id=1, source_target_pairs={{0,16},{16,0},{1,17},{17,1},{2,18},{18,2},{3,19},{19,3},{4,20},{20... | collective-permute-start | bytes 6920 | tf_op jit(solution)/shard_map/ppermute | solution.py:27
  3.9 56.1 %collective-permute-start.4 = (bf16[1152]{0:T(1024)(128)(2,1)}, bf16[1152]{0:T(1024)(128)(2,1)}, u32[]{:S(2)}, u32[]{:S(2)}) collective-permute-start(bf16[1152]{0:T(1024)(128)(2,1)} %reduce.5), channel_id=1, source_target_pairs={{0,16},{16,0},{1,17},{17,1},{2,18},{18,2},{3,19},{19,3},{4,20},{20... | collective-permute-start | bytes 6920 | tf_op jit(solution)/shard_map/ppermute | solution.py:27
  5.0 57.0 %collective-permute-start.5 = (bf16[2304]{0:T(1024)(128)(2,1)S(1)}, bf16[2304]{0:T(1024)(128)(2,1)}, u32[]{:S(2)}, u32[]{:S(2)}) collective-permute-start(bf16[2304]{0:T(1024)(128)(2,1)S(1)} %reduce.6), channel_id=1, source_target_pairs={{0,16},{16,0},{1,17},{17,1},{2,18},{18,2},{3,19},{19,3},{4,20},{20... | collective-permute-start | bytes 13832 | tf_op jit(solution)/shard_map/ppermute | solution.py:27
  5.2 58.1 %collective-permute-start.7 = (bf16[8,511]{1,0:T(8,128)(2,1)}, bf16[8,511]{1,0:T(8,128)(2,1)}, u32[]{:S(2)}, u32[]{:S(2)}) collective-permute-start(bf16[8,511]{1,0:T(8,128)(2,1)} %bitcast.192), channel_id=1, source_target_pairs={{0,16},{16,0},{1,17},{17,1},{2,18},{18,2},{3,19},{19,3},{4,20},{20... | collective-permute-start | bytes 24536 | tf_op jit(solution)/shard_map/ppermute | solution.py:27
  28.3 2.6 copy-start.29
  28.6 3.0 copy-start.13
  30.9 0.6 copy-start.19
  30.9 0.7 copy-start.21
  31.6 4.0 copy-start.23
  35.7 4.2 copy-start.5
  37.9 6.3 copy-start.34
  37.9 8.8 %copy-start.28 = (bf16[1,6,576]{2,1,0:T(8,128)(2,1)S(1)}, bf16[1,6,576]{2,1,0:T(8,128)(2,1)}, u32[]{:S(2)}) copy-start(bf16[1,6,576]{2,1,0:T(8,128)(2,1)} %param.31) | copy-start | bytes 20740
  39.9 10.7 %copy-start.16 = (bf16[1,144,3,576]{3,1,2,0:T(8,128)(2,1)S(1)}, bf16[1,144,3,576]{3,1,2,0:T(8,128)(2,1)}, u32[]{:S(2)}) copy-start(bf16[1,144,3,576]{3,1,2,0:T(8,128)(2,1)} %param.22) | copy-start | bytes 1492996
  40.7 23.4 %all-to-all-start = ((f32[8,2,6,576]{3,1,2,0:T(2,128)}), f32[8,2,6,576]{3,1,2,0:T(2,128)S(1)}, u32[]{:S(2)}, u32[]{:S(2)}) async-start(f32[8,2,6,576]{3,1,2,0:T(2,128)} %copy.62), calls=%async_computation | async-start | bytes 491520 | tf_op jit(solution)/shard_map/all_to_all | solution.py:1307
  49.0 4.5 copy-start.12
  51.4 2.2 copy-start.18
  51.4 3.0 copy-start.14
  51.5 3.0 copy-start.15
  56.0 0.9 copy-start.17
  56.0 1.6 copy-start.32
  56.0 2.3 copy-start.33
  56.0 8.2 %copy-start.26 = (f32[6,576]{1,0:T(8,128)S(1)}, f32[6,576]{1,0:T(8,128)}, u32[]{:S(2)}) copy-start(f32[6,576]{1,0:T(8,128)} %bitcast_convert_fusion) | copy-start | bytes 41476
  58.2 12.2 %collective-permute-start = (bf16[3,144,1152]{2,1,0:T(8,128)(2,1)S(1)}, bf16[3,144,1152]{2,1,0:T(8,128)(2,1)}, u32[]{:S(2)}, u32[]{:S(2)}) collective-permute-start(bf16[3,144,1152]{2,1,0:T(8,128)(2,1)S(1)} %broadcast_select_fusion), channel_id=1, source_target_pairs={{0,16},{16,0},{1,17},{17,1},{2,18},{18,2},{3,19},{19,3},{4,20},{20... | collective-permute-start | bytes 2985992 | tf_op jit(solution)/shard_map/ppermute | solution.py:27
  64.2 1.4 collective-permute-start.1
  65.6 4.1 collective-permute-start.2
  72.0 1.5 copy-start.31
  513.5 3.6 copy-start.27
  519.3 13.0 %collective-permute-start.11 = (f32[6,576]{1,0:T(8,128)}, f32[6,576]{1,0:T(8,128)}, u32[]{:S(2)}, u32[]{:S(2)}) collective-permute-start(f32[6,576]{1,0:T(8,128)} %select_bitcast_fusion.2), channel_id=1, source_target_pairs={{0,16},{16,0},{1,17},{17,1},{2,18},{18,2},{3,19},{19,3},{4,20},{20... | collective-permute-start | bytes 41480 | tf_op jit(solution)/shard_map/ppermute | solution.py:27
  520.8 98.8 %collective-permute-start.10 = (f32[9272]{0:T(1024)}, f32[9272]{0:T(1024)}, u32[]{:S(2)}, u32[]{:S(2)}) collective-permute-start(f32[9272]{0:T(1024)} %pad_maximum_fusion.4), channel_id=1, source_target_pairs={{0,16},{16,0},{1,17},{17,1},{2,18},{18,2},{3,19},{19,3},{4,20},{20... | collective-permute-start | bytes 111272 | tf_op jit(solution)/shard_map/ppermute | solution.py:27
  521.3 1.7 copy-start.3
  523.0 2.1 copy-start.2
  525.1 1.7 copy-start.10
  525.1 1.7 copy-start.11
  526.2 134.6 %collective-permute-start.8 = (f32[256,1152]{1,0:T(8,128)}, f32[256,1152]{1,0:T(8,128)}, u32[]{:S(2)}, u32[]{:S(2)}) collective-permute-start(f32[256,1152]{1,0:T(8,128)} %select_bitcast_fusion.1), channel_id=1, source_target_pairs={{0,16},{16,0},{1,17},{17,1},{2,18},{18,2},{3,19},{19,3},{4,20},{20... | collective-permute-start | bytes 3538952 | tf_op jit(solution)/shard_map/ppermute | solution.py:27
  526.2 137.6 %collective-permute-start.9 = (f32[256,1152]{1,0:T(8,128)}, f32[256,1152]{1,0:T(8,128)}, u32[]{:S(2)}, u32[]{:S(2)}) collective-permute-start(f32[256,1152]{1,0:T(8,128)} %select_bitcast_fusion), channel_id=1, source_target_pairs={{0,16},{16,0},{1,17},{17,1},{2,18},{18,2},{3,19},{19,3},{4,20},{20... | collective-permute-start | bytes 3538952 | tf_op jit(solution)/shard_map/ppermute | solution.py:27
  527.9 1.1 copy-start.8
  527.9 1.3 copy-start.9
  531.5 36.3 %copy-start.6 = (bf16[144,3456]{1,0:T(8,128)(2,1)S(1)}, bf16[144,3456]{1,0:T(8,128)(2,1)}, u32[]{:S(2)}) copy-start(bf16[144,3456]{1,0:T(8,128)(2,1)} %copy-done.5) | copy-start | bytes 2985988
  567.8 45.2 %copy-start.20 = (f32[16,1152]{1,0:T(8,128)S(1)}, f32[16,1152]{1,0:T(8,128)}, u32[]{:S(2)}) copy-start(f32[16,1152]{1,0:T(8,128)} %copy-done.19) | copy-start | bytes 221188
  567.8 45.2 %copy-start.22 = (f32[16,1152]{1,0:T(8,128)S(1)}, f32[16,1152]{1,0:T(8,128)}, u32[]{:S(2)}) copy-start(f32[16,1152]{1,0:T(8,128)} %copy-done.21) | copy-start | bytes 221188
  567.8 45.2 %copy-start.30 = (s32[16]{0:T(128)S(1)}, s32[16]{0:T(128)}, u32[]{:S(2)}) copy-start(s32[16]{0:T(128)} %copy-done.29) | copy-start | bytes 196
  612.9 2.8 copy-start.24
  615.7 3.3 copy-start.7
  615.7 3.9 copy-start.25
  662.3 2.5 copy-start.4
  666.3 1.7 copy-start.1

commit v3 on v2

--- a/solution.py
+++ b/solution.py
@@ -42,6 +42,7 @@
 
 
 HEAD_LANES = 384
+ADA_LANES = 640
 
 
 def nn(a, b):
@@ -85,34 +86,29 @@
         self.other = (1 - self.core, self.dp, self.head)
         self.beside = (self.core, self.dp, 1 - self.head)
 
-    def greet(self, whole):
+        self.beyond = (1 - self.core, self.dp, 1 - self.head)
+        self.count = 2 * chain
+
+    def peer(self, k):
+        return lax.rem(self.dp + k, self.count)
+
+    def source(self, k):
+        return lax.rem(self.dp + self.count - k, self.count)
+
+    def flip(self, b):
+        bit = lax.rem(self.dp // (1 << b), 2)
+        return self.dp + (1 << b) * (1 - 2 * bit)
+
+    def in_dp(self, dp):
+        return (self.core, dp, self.head)
+
+    def greet(self):
         barrier = pltpu.get_barrier_semaphore()
-
-        def tell(device):
+        others = [self.other, self.beside, self.beyond]
+        others += [self.in_dp(self.peer(k)) for k in range(1, self.count)]
+        for device in others:
             pl.semaphore_signal(barrier, inc=1, device_id=device, device_id_type=MESH)
-
-        tell(self.other)
-        tell(self.beside)
-        if not whole:
-            pl.semaphore_wait(barrier, 2)
-            return
-        tell(self.across)
-
-        @pl.when(self.z < self.chain - 1)
-        def _():
-            tell(self.above)
-
-        @pl.when(self.z > 0)
-        def _():
-            tell(self.below)
-
-        @pl.when((self.z > 0) & (self.z < self.chain - 1))
-        def _():
-            pl.semaphore_wait(barrier, 5)
-
-        @pl.when((self.z == 0) | (self.z == self.chain - 1))
-        def _():
-            pl.semaphore_wait(barrier, 4)
+        pl.semaphore_wait(barrier, len(others))
 
 
 def remote(src, dst, ssem, rsem, device):
@@ -132,11 +128,69 @@
         return self.ref.at[self.count - 1]
 
 
+class Links:
+    def __init__(self, at, ssem, rsem):
+        self.at, self.sends, self.recvs = at, Numbered(ssem), Numbered(rsem)
+        self.waiting = []
+
+    def copy(self, src, dst, device):
+        copy = remote(src, dst, self.sends.next(), self.recvs.next(), device)
+        copy.start()
+        self.waiting.append(copy.wait_send)
+        return copy
+
+    def to_all(self, src_of, dst):
+        copies = []
+        for k in range(1, self.at.count):
+            peer = self.at.peer(k)
+            copies.append(self.copy(src_of(peer), dst, self.at.in_dp(peer)))
+        return copies
+
+    def around(self, ref):
+        mine_ = ref.at[self.at.core, self.at.head]
+        return [
+            self.copy(mine_, mine_, device)
+            for device in (self.at.other, self.at.beside, self.at.beyond)
+        ]
+
+
 class Gather:
-    def __init__(self, at, own, w, ssem, rsem, lsem):
-        self.at, self.own, self.w = at, own, w
+    def __init__(self, at, pack, w, ssem, rsem, lsem):
+        self.at, self.pack, self.w = at, pack, w
         self.ssem, self.rsem, self.lsem = ssem, rsem, lsem
-        self.pieces = own.shape[0]
+        self.pieces = w.shape[0]
+
+    def local(self, t):
+        core = self.at.core
+        return pltpu.make_async_copy(
+            self.pack.at[core, t], self.w.at[3 * core + t, core, self.at.dp], self.lsem.at[t]
+        )
+
+    def share(self, t):
+        core = self.at.core
+        return remote(
+            self.pack.at[1 - core, t],
+            self.w.at[3 * core + t, 1 - core, self.at.dp],
+            self.ssem.at[t, 3 * self.at.chain + 2],
+            self.rsem.at[t, 3 * self.at.chain + 2],
+            self.at.other,
+        )
+
+    def shared(self, t):
+        core = self.at.core
+        block = self.w.at[3 * (1 - core) + t, core, self.at.dp]
+        return remote(
+            self.pack.at[1 - core, t],
+            block,
+            self.ssem.at[t, 3 * self.at.chain + 2],
+            self.rsem.at[t, 3 * self.at.chain + 2],
+            self.at.other,
+        )
+
+    def split(self):
+        for t in range(3):
+            self.local(t).start()
+            self.share(t).start()
 
     def block(self, p, zz, yy):
         return self.w.at[p, self.at.core, zz * 2 + yy]
@@ -146,7 +200,7 @@
 
     def up(self, p, k):
         b = self.block(p, self.at.z - (k - 1), self.at.y)
-        return self.copy(self.own.at[p] if k == 1 else b, b, p, k - 1, self.at.above)
+        return self.copy(b, b, p, k - 1, self.at.above)
 
     def up_in(self, p, k):
         b = self.block(p, self.at.z - k, self.at.y)
@@ -154,17 +208,15 @@
 
     def down(self, p, k):
         b = self.block(p, self.at.z + (k - 1), self.at.y)
-        return self.copy(
-            self.own.at[p] if k == 1 else b, b, p, self.at.chain + k - 1, self.at.below
-        )
+        return self.copy(b, b, p, self.at.chain + k - 1, self.at.below)
 
     def down_in(self, p, k):
         b = self.block(p, self.at.z + k, self.at.y)
         return self.copy(b, b, p, self.at.chain + k - 1, self.at.above)
 
-    def cross(self, p, zz, own=False):
+    def cross(self, p, zz):
         b = self.block(p, zz, self.at.y)
-        return self.copy(self.own.at[p] if own else b, b, p, 2 * self.at.chain + zz, self.at.across)
+        return self.copy(b, b, p, 2 * self.at.chain + zz, self.at.across)
 
     def cross_in(self, p, zz):
         b = self.block(p, zz, 1 - self.at.y)
@@ -186,14 +238,18 @@
         b = self.w.at[p, 1 - self.at.core]
         return self.copy(b, b, p, 3 * self.at.chain + 1, self.at.other)
 
-    def local(self, p):
-        return pltpu.make_async_copy(
-            self.own.at[p], self.block(p, self.at.z, self.at.y), self.lsem.at[p]
-        )
-
     def start(self, p):
-        self.local(p).start()
-        self.cross(p, self.at.z, True).start()
+        s, t = divmod(p, 3)
+
+        @pl.when(self.at.core == s)
+        def _():
+            self.local(t).wait()
+
+        @pl.when(self.at.core != s)
+        def _():
+            self.shared(t).wait_recv()
+
+        self.cross(p, self.at.z).start()
 
         @pl.when(self.at.z < self.at.chain - 1)
         def _():
@@ -247,7 +303,6 @@
 
     def finish(self, p):
         z = self.at.z
-        self.local(p).wait()
         for j in range(self.at.chain):
             if p % 2 == 1:
 
@@ -285,9 +340,22 @@
                 self.down(p, k).wait_send()
 
         self.other_out(p).wait_send()
+        if p < 3:
+            self.share(p).wait_send()
 
 
 TILE = 32
+
+
+def silu(v):
+    return v / (1.0 + jnp.exp(-v))
+
+
+def thirds(v):
+    a = v.astype(BF)
+    rest = v - a.astype(F32)
+    b = rest.astype(BF)
+    return a, b, (rest - b.astype(F32)).astype(BF)
 
 
 def by_rows(rows, body, carry, tile=TILE):
@@ -322,23 +390,29 @@
 def forward_kernel(cfg, *refs):
     fused, chain, heads, head_dim = cfg
     refs = list(refs)
-    own = refs.pop(0)
-    tok, mod, bqv, bout, bup, bdown, rel, pos, seg, place, drop, mtok = refs[:12]
-    refs = refs[12:]
-    w = refs.pop(0) if fused else own
-    s_hat1, s_inv, s_n1, s_qkv, s_p, s_o, s_branch, s_hat2, s_n2, s_hid, s_slope, s_y, outs = refs[:13]
-    refs = refs[13:]
+    pack = refs.pop(0)
+    tok, cond, wada, bada, small_own, pos, seg, place, drop, mtok = refs[:10]
+    refs = refs[10:]
+    w = refs.pop(0) if fused else pack
+    (
+        s_hat1, s_inv, s_n1, s_qkv, s_p, s_o, s_branch, s_hat2, s_n2, s_hid, s_slope, s_y,
+        s_full, s_xm, o_mod, o_cl, o_small, outs,
+    ) = refs[:18]
+    refs = refs[18:]
     (
         wa, wu, wd, res, hat, inv, n, r, qkv, prob, o, branch, hid, slope, y_keep,
-        xs, xr, toep, gs, gr, gl, ssem, rsem, lsem,
+        xs, xr, toep, small, cl, part, got, pair, mod, gs, gr, gl, ssem, rsem, lsem, ms, mr,
     ) = refs
     at = Place(chain)
     rows, width = res.shape
+    lw = heads * head_dim
+    shard = width // at.count
     half_heads = heads // 2
     scale = 1.0 / math.sqrt(head_dim)
     sends, recvs, locals_ = Numbered(ssem), Numbered(rsem), Numbered(lsem)
-    at.greet(fused)
-    gather = Gather(at, own, w, gs, gr, gl) if fused else None
+    at.greet()
+    gather = Gather(at, pack, w, gs, gr, gl) if fused else None
+    links = Links(at, ms, mr)
     waiting = {}
 
     def keep(name, src, dst):
@@ -366,9 +440,59 @@
     def load(p, slot):
         if fused:
             gather.other_in(p).wait_recv()
-        copy = pltpu.make_async_copy(w.at[p], slot, locals_.next())
-        copy.start()
-        copy.wait()
+        keep("load%d" % p, w.at[p], slot)
+
+    def send_cond():
+        cl[pl.ds(at.dp, 1)] = cond[pl.ds(at.dp, 1)]
+        return links.to_all(lambda peer: cond.at[peer], cl.at[at.dp])
+
+    def modulation_terms(copies):
+        for copy in copies:
+            copy.wait_recv()
+        part[...] = jnp.zeros_like(part)
+        parts = thirds(silu(flat(cl[...])[:, :shard]))
+        for k in range(6):
+            cols = wada[:, k * ADA_LANES : (k + 1) * ADA_LANES]
+            value = nn(parts[0], cols) + (nn(parts[1], cols) + nn(parts[2], cols))
+            value = value.reshape(at.count, 8, ADA_LANES)
+            for m in range(2):
+                part[:, m * 8 + k, :] = value[:, m, :]
+        got[pl.ds(at.dp, 1)] = part[pl.ds(at.dp, 1)]
+        return links.to_all(lambda peer: part.at[peer], got.at[at.dp])
+
+    def modulation_sum(copies):
+        for copy in copies:
+            copy.wait_recv()
+        value = got[0]
+        for j in range(1, at.count):
+            value = value + got[j]
+        pair[at.core, at.head] = value + jnp.concatenate([bada[...], bada[...]], axis=0)
+        return links.around(pair)
+
+    def modulation(copies):
+        for copy in copies:
+            copy.wait_recv()
+        lane = lax.broadcasted_iota(jnp.int32, (8, ADA_LANES), 1)
+        blank = jnp.zeros((8, width - ADA_LANES), F32)
+        mine_ = pl.ds(pl.multiple_of(at.core * 8, 8), 8)
+        for s in range(2):
+            a, b = [
+                jnp.concatenate([jnp.where(lane < lw, pair[s, h, mine_, :], 0.0), blank], axis=1)
+                for h in range(2)
+            ]
+            mod[s] = a + pltpu.roll(b, lw, 1)
+        keep("mod", mod, o_mod)
+        keep("cl", cl, o_cl)
+
+    def share_small():
+        small[pl.ds(at.core, 1)] = small_own[...][None]
+        return links.copy(small_own, small.at[at.core], at.other)
+
+    def bqv_row(s, half, kind):
+        return small[s, half * 4 + kind : half * 4 + kind + 1, :HEAD_LANES]
+
+    def bup_row(s, half, cols):
+        return small[s, 10 + half : 11 + half, cols]
 
     def send_across(i):
         copy = remote(xs.at[i], xr.at[i], sends.next(), recvs.next(), at.beside)
@@ -406,9 +530,8 @@
             def body(ds, c):
                 v = r[ds, :]
                 for kind, shift in ((0, 864), (1, 576), (2, 288)):
-                    part = pltpu.roll(v, shift, 1)[:, :HEAD_LANES]
-                    row = s * 8 + half * 4 + kind
-                    qkv[kind, half, ds, :] = (part + bqv[row : row + 1, :]).astype(BF)
+                    piece = pltpu.roll(v, shift, 1)[:, :HEAD_LANES]
+                    qkv[kind, half, ds, :] = (piece + bqv_row(s, half, kind)).astype(BF)
                 return c
 
             by_rows(rows, body, 0)
@@ -423,7 +546,7 @@
         def one(i, c):
             index = half * half_heads + i
             mask = head_mask(i, head_dim).astype(BF)
-            line = rel[pl.ds(s * heads + index, 1), :]
+            line = small[s, pl.ds(16 + index, 1), : 2 * rows]
             skew = pltpu.roll(jnp.broadcast_to(line, (rows, 2 * rows)), 0, 1, stride=1, stride_axis=0)
             bias = skew[:, :rows]
             if s == 0:
@@ -456,7 +579,7 @@
         settle("n2")
 
         def body(ds, c):
-            b = total(i, ds) + bout[s : s + 1, :]
+            b = total(i, ds) + small[s, 8:9, :]
             branch[ds, :] = b.astype(BF)
             xm = res[ds, :] + mod[s, 2:3, :] * b
             res[ds, :] = xm
@@ -470,6 +593,8 @@
         keep("branch", branch, s_branch.at[s])
         keep("inv", inv, s_inv.at[s])
         keep("hat2", hat.at[1], s_hat2.at[s])
+        if s == 1:
+            keep("out", res, s_xm)
         keep("n2", n.at[1], s_n2.at[s, 0])
         give("n2", n.at[1], s_n2.at[s, 1])
 
@@ -479,7 +604,7 @@
             settle("slope")
         for j in range(3):
             cols = slice(j * 384, (j + 1) * 384)
-            r[:, cols] = nn(n[1], flat(wu[half, :, :, cols])) + bup[s, half : half + 1, cols]
+            r[:, cols] = nn(n[1], flat(wu[half, :, :, cols])) + bup_row(s, half, cols)
 
         def body(ds, c):
             value, sl = gelu_both(r[ds, :])
@@ -492,6 +617,8 @@
             keep("slope", slope, s_slope.at[s])
             keep("hid", hid.at[at.core], s_hid.at[s, 0])
             give("hid", hid.at[1 - at.core], s_hid.at[s, 1])
+            if s == 1:
+                keep("hid", hid, s_full)
 
     def project_down(i):
         xs[i] = (nt(hid[0], flat(wd[0])) + nt(hid[1], flat(wd[1]))).astype(BF)
@@ -503,14 +630,41 @@
         settle("out")
 
         def body(ds, c):
-            v = total(i, ds) + bdown[s : s + 1, :]
+            v = total(i, ds) + small[s, 9:10, :]
             y_keep[ds, :] = v.astype(BF)
             res[ds, :] = res[ds, :] + mod[s, 5:6, :] * v
             return c
 
         by_rows(rows, body, 0)
-        keep("y", y_keep, s_y.at[s])
-        keep("out", res, outs.at[s])
+        keep("y", y_keep, s_y)
+        here = pltpu.make_async_copy(res, outs.at[at.core], locals_.next())
+        there = remote(res, outs.at[at.core], sends.next(), recvs.next(), at.other)
+
+        @pl.when(at.core == 0)
+        def _():
+            here.start()
+
+        @pl.when(at.core == 1)
+        def _():
+            there.start()
+
+        def sent():
+            @pl.when(at.core == 0)
+            def _():
+                here.wait()
+
+            @pl.when(at.core == 1)
+            def _():
+                there.wait_send()
+
+        def arrived():
+            @pl.when(at.core == 0)
+            def _():
+                remote(res, outs.at[1], there_s, there_r, at.other).wait_recv()
+
+        there_s, there_r = sends.ref.at[sends.count - 1], recvs.ref.at[recvs.count - 1]
+        waiting.setdefault("out", []).append(sent)
+        waiting.setdefault("end", []).append(arrived)
 
     def spread():
         r[...] = nn(place[...], res[...].astype(BF))
@@ -522,7 +676,10 @@
 
         by_rows(rows, body, 0)
 
+    copies = send_cond()
+    small_copy = share_small()
     if fused:
+        gather.split()
         gather.start(0)
         gather.start(1)
 
@@ -531,37 +688,53 @@
         return c
 
     by_rows(rows, start_residual, 0)
+    copies = modulation_terms(copies)
+    pump(("step", 0, 1), ("start", 2))
+    copies = modulation_sum(copies)
+    pump(("step", 0, 2))
+    modulation(copies)
     norm_one(0)
-    pump(("step", 0, 1), ("start", 2), ("step", 0, 2), ("step", 0, 3))
+    small_copy.wait_recv()
+    keep("small", small, o_small)
+    pump(("step", 0, 3))
     for s in range(2):
         p = 3 * s
-        pump(("step", p + 1, 1), ("start", p + 3), ("finish", p), ("step", p + 1, 2))
+        pump(("step", p + 1, 1), ("start", p + 3), ("finish", p))
+        if s == 1:
+            end_block(0, 1, copy)
+            spread()
+            norm_one(1)
+        pump(("step", p + 1, 2))
         load(p, wa)
+        settle("load%d" % p)
         project(s)
         pump(("step", p + 1, 3))
         attend(s, 0)
         pump(("step", p + 2, 1), ("start", p + 4), ("finish", p + 1))
         attend(s, 1)
         copy = project_out(2 * s)
-        pump(("step", p + 2, 2))
+        load(p + 1, wu)
+        pump(("step", p + 2, 2), ("step", p + 2, 3))
         norm_two(s, 2 * s, copy)
-        pump(("step", p + 2, 3))
-        load(p + 1, wu)
+        if s == 0:
+            pump(("step", p + 3, 1), ("start", p + 5), ("finish", p + 2))
+        settle("load%d" % (p + 1))
         hidden(s, 0)
-        pump(("step", p + 3, 1), ("start", p + 5))
-        pump(("finish", p + 2))
+        if s == 0:
+            load(p + 2, wd)
+            pump(("step", p + 3, 2))
         hidden(s, 1)
-        pump(("step", p + 3, 2))
-        load(p + 2, wd)
-        copy = project_down(2 * s + 1)
-        pump(("step", p + 3, 3))
-        end_block(s, 2 * s + 1, copy)
         if s == 0:
-            spread()
-            norm_one(1)
+            settle("load%d" % (p + 2))
+            copy = project_down(2 * s + 1)
+            pump(("step", p + 3, 3))
     if fused:
+        gather.finish(5)
+        gather.other_in(5).wait_recv()
         for p in range(gather.pieces):
             gather.drain(p)
+    for wait in links.waiting:
+        wait()
     for name in list(waiting):
         settle(name)
 
@@ -569,9 +742,10 @@
 def forward_call(cfg, own, small, dp_count):
     fused, chain, heads, head_dim = cfg
     rows, width = small[0].shape
-    pieces = own.shape[0]
+    pieces = 6
     shard = own.shape[-2]
     groups = width // shard
+    cond_lanes = small[1].shape[2]
     bf, f = lambda *s: jax.ShapeDtypeStruct(s, BF), lambda *s: jax.ShapeDtypeStruct(s, F32)
     out_shape = [
         bf(2, rows, width),
@@ -585,12 +759,18 @@
         bf(2, 2, rows, width),
         bf(2, 2, rows, width),
         bf(2, 2, rows, width),
+        bf(rows, width),
         bf(2, rows, width),
+        f(rows, width),
+        f(2, 8, width),
+        f(dp_count, 8, cond_lanes),
+        f(2, 24, width),
         f(2, rows, width),
     ]
     if fused:
         out_shape = [bf(pieces, 2, groups, shard, width)] + out_shape
-    kinds = 3 * chain + 2
+    kinds = 3 * chain + 3
+    many = 2 * (dp_count - 1) + 8
     slot = pltpu.VMEM((2, groups, shard, width), BF)
     scratch = [
         slot,
@@ -611,12 +791,20 @@
         pltpu.VMEM((4, rows, width), BF),
         pltpu.VMEM((4, rows, width), BF),
         pltpu.VMEM((rows, rows), BF),
+        pltpu.VMEM((2, 24, width), F32),
+        pltpu.VMEM((dp_count, 8, cond_lanes), F32),
+        pltpu.VMEM((dp_count, 16, ADA_LANES), F32),
+        pltpu.VMEM((dp_count, 16, ADA_LANES), F32),
+        pltpu.VMEM((2, 2, 16, ADA_LANES), F32),
+        pltpu.VMEM((2, 8, width), F32),
         pltpu.SemaphoreType.DMA((pieces, kinds)),
         pltpu.SemaphoreType.DMA((pieces, kinds)),
-        pltpu.SemaphoreType.DMA((pieces,)),
+        pltpu.SemaphoreType.DMA((3,)),
         pltpu.SemaphoreType.DMA((16,)),
         pltpu.SemaphoreType.DMA((16,)),
-        pltpu.SemaphoreType.DMA((40,)),
+        pltpu.SemaphoreType.DMA((48,)),
+        pltpu.SemaphoreType.DMA((many,)),
+        pltpu.SemaphoreType.DMA((many,)),
     ]
 
     def body(*refs):
@@ -635,7 +823,7 @@
         ),
         name="forward_blocks",
     )(own, *small)
-    return (result if fused else [own] + list(result))
+    return result if fused else [own] + list(result)
 
 
 class Scatter:
@@ -765,9 +953,10 @@
         at, chain = self.at, self.at.chain
         z = at.z
         slot = self.slots(r)[1]
-        if r >= self.yr.shape[0]:
-            self.hand_over_done(r - self.yr.shape[0])
-        red = self.red.at[slot]
+        held = self.red.shape[0]
+        if r >= held:
+            self.hand_over_done(r - held)
+        red = self.red.at[r % held]
         red[...] = self.own(r, z)[...].astype(F32)
 
         @pl.when(z > 0)
@@ -803,12 +992,12 @@
 
     def keep(self, r):
         return pltpu.make_async_copy(
-            self.red.at[self.slots(r)[1]], self.out.at[self.order[r][1], self.at.core], self.lsem.at[r]
+            self.red.at[r % self.red.shape[0]], self.out.at[self.order[r][1], self.at.core], self.lsem.at[r]
         )
 
     def hand_over(self, r):
         return remote(
-            self.red.at[self.slots(r)[1]],
+            self.red.at[r % self.red.shape[0]],
             self.out.at[self.order[r][1], self.at.core],
             self.osem.at[r],
             self.isem.at[r],
@@ -850,7 +1039,7 @@
 
     def end(self):
         for r in range(len(self.order)):
-            if r + self.yr.shape[0] >= len(self.order):
+            if r + self.red.shape[0] >= len(self.order):
                 self.hand_over_done(r)
             s, t = self.order[r]
 
@@ -872,23 +1061,29 @@
     fused, chain, heads, head_dim = cfg
     refs = list(refs)
     w = refs.pop(0)
-    i_hat1, i_inv, i_n1, i_qkv, i_p, i_o, i_branch, i_hat2, i_n2, i_hid, i_slope, i_y = refs[:12]
-    refs = refs[12:]
-    dout, mod, flips, pos, place, drop = refs[:6]
+    (
+        i_hat1, i_inv, i_n1, i_qkv, i_p, i_o, i_branch, i_hat2, i_n2, i_hid, i_slope, i_y, i_full, i_xm,
+    ) = refs[:14]
+    refs = refs[14:]
+    dout, mod, small, cl, wada, flips, pos, place, drop = refs[:9]
+    refs = refs[9:]
+    red_out, o_dx, o_out, o_sums, o_dm, o_dc = refs[:6]
     refs = refs[6:]
-    red_out, o_dx, stats, rel_out = refs[:4]
-    refs = refs[4:]
     (
-        wslot, hat1, inv, n1, qkv, prob, o, branch, hat2, n2, hid, slope, y_keep,
-        d, r, dy, dpre, dattn, dqkv, do, acc, xs, xr, g, yr, zr, mr, red,
-        gs, gr, go, gi, gl, credit, ssem, rsem, lsem,
+        wslot, hat1, inv, qkv, prob, o, branch, hat2, n2, hid, slope,
+        d, r, dy, dpre, dattn, dqkv, do, xs, xr, g, yr, zr, mr, red,
+        stats, got, sums, rounds, dm, dc, dg, gs, gr, go, gi, gl, credit, ssem, rsem, lsem, ms, mrs,
     ) = refs
     at = Place(chain)
     rows, width = d.shape
+    lw = heads * head_dim
+    shard = width // at.count
     half_heads = heads // 2
     scale = 1.0 / math.sqrt(head_dim)
     sends, recvs, locals_ = Numbered(ssem), Numbered(rsem), Numbered(lsem)
-    at.greet(fused)
+    at.greet()
+    links = Links(at, ms, mrs)
+    stats[...] = jnp.zeros_like(stats)
     scatter = (
         Scatter(at, ORDER, g, yr, zr, mr, red, red_out, gs, gr, go, gi, gl, credit) if fused else None
     )
@@ -927,23 +1122,27 @@
     def send_across(i):
         if i > 1:
             settle("x out %d" % (i - 2))
-        copy = remote(xs.at[i % 2], xr.at[i], sends.next(), recvs.next(), at.beside)
+        copy = remote(xs.at[i % 2], xr.at[i % 2], sends.next(), recvs.next(), at.beside)
         copy.start()
         waiting.setdefault("x in %d" % i, []).append(copy.wait_recv)
         waiting.setdefault("x out %d" % i, []).append(copy.wait_send)
 
     def total(i, ds):
-        return xs[i % 2, ds, :].astype(F32) + xr[i, ds, :].astype(F32)
+        return xs[i % 2, ds, :].astype(F32) + xr[i % 2, ds, :].astype(F32)
 
     def stat(s, row, value):
         stats[s, row : row + 1, :] = jnp.sum(value, axis=0, keepdims=True)
 
     zero8 = lambda: jnp.zeros((8, width), F32)
+    spans = [slice(k * HEAD_LANES, (k + 1) * HEAD_LANES) for k in range(3)]
     spot = lambda half: jnp.where(half == at.core, 0, 2)
 
     def loads(s):
-        fetch("y", i_y.at[s], y_keep)
         fetch("slope", i_slope.at[s], slope)
+        if s == 0:
+            fetch("y", i_y, xs.at[2])
+        else:
+            fetch("full", i_full, dqkv.at[0:2])
         fetch("hid", i_hid.at[s], hid)
         fetch("n2", i_n2.at[s], n2)
         fetch("hat2", i_hat2.at[s], hat2)
@@ -952,7 +1151,6 @@
         fetch("p", i_p.at[s], prob)
         fetch("qkv", i_qkv.at[s], qkv)
         fetch("o", i_o.at[s], o)
-        fetch("n1", i_n1.at[s], n1)
         fetch("hat1", i_hat1.at[s], hat1)
 
     def product(r_, parts):
@@ -987,18 +1185,21 @@
             dv = d[ds, :]
             v = (dv * mod[s, 5:6, :]).astype(BF)
             dy[0, ds, :] = v
-            return (
-                a + column_sum(dv * y_keep[ds, :].astype(F32)),
-                b + column_sum(v.astype(F32)),
-            )
+            if s == 0:
+                a = a + column_sum(dv * xs[2, ds, :].astype(F32))
+            return (a, b + column_sum(v.astype(F32)))
 
         a, b = by_rows(rows, one, (zero8(), zero8()))
-        stat(s, 5, a)
+        if s == 0:
+            stat(s, 5, a)
         stat(s, 6, b)
         give("dy", dy.at[0], dy.at[1])
         settle("w%d" % first)
         settle("slope")
         settle("dpre out")
+        if s == 1:
+            settle("full")
+            project_down()
         for half in range(2):
             for j in range(3):
                 cols = slice(j * 384, (j + 1) * 384)
@@ -1007,6 +1208,11 @@
                 stats[s, 8 + half : 9 + half, cols] = jnp.sum(v.astype(F32), axis=0, keepdims=True)
         give("dpre", dpre.at[2], dpre.at[1])
         fetch("w%d" % first, w.at[3 * s], wslot.at[first])
+        settle("dy in")
+        settle("hid")
+        product(base, lambda j: [(flat(dy[...]), cols_of(hid, j))])
+        fetch("n1", i_n1.at[s], hid)
+        pump(("begin", base))
         settle("w%d" % second)
         if xi > 1:
             settle("x out %d" % (xi - 2))
@@ -1016,16 +1222,16 @@
         send_across(xi)
         if s == 1:
             fetch("w%d" % second, w.at[2], wslot.at[second])
-        settle("dy in")
-        settle("hid")
-        product(base, lambda j: [(flat(dy[...]), cols_of(hid, j))])
-        pump(("begin", base))
         if s == 0:
-            pump_rest(2, 0)
+            pump(("arrive", 1, 3), ("finish", 1))
         settle("dpre in")
         settle("n2")
         product(base + 1, lambda j: [(flat(n2[...]), cols_of(dpre, j))])
         pump(("begin", base + 1))
+        if s == 1:
+            pump(("arrive", 0, 0), ("step", 0, 1), ("arrive", 0, 1), ("step", 0, 2))
+        else:
+            pump(("arrive", 2, 0), ("step", 2, 1), ("arrive", 2, 1), ("step", 2, 2), ("arrive", 2, 2), ("step", 2, 3))
         settle("x in %d" % xi)
         settle("hat2")
         settle("inv")
@@ -1058,13 +1264,16 @@
         settle("qkv")
         settle("dqkv out")
         for half in range(2):
-            if half == 0:
-                pump(("mated", base))
-            pump(("arrive", base, half))
-            if half < chain - 1:
-                pump(("step", base, half + 1))
+            if s == 1 and half == 0:
+                pump(("arrive", 0, 2), ("step", 0, 3))
+            if s == 1 and half == 1:
+                pump(("arrive", 0, 3))
+            if s == 0 and half == 0:
+                pump(("arrive", 2, 3), ("finish", 2))
+            if s == 0 and half == 1:
+                pump(("mated", 3), ("arrive", 3, 0), ("step", 3, 1))
             do[half] = nn(dattn[0], flat(wslot[third, half, :, :, :HEAD_LANES])).astype(BF)
-            acc[...] = jnp.zeros_like(acc)
+            r[...] = jnp.zeros_like(r)
 
             def head(i, c):
                 index = half * half_heads + i
@@ -1072,12 +1281,12 @@
                 low_mask = mask.astype(BF)
                 p = prob[index]
                 dom = do[half] * low_mask
-                acc[2] = acc[2] + tn(p, dom)
+                r[:, spans[2]] = r[:, spans[2]] + tn(p, dom)
                 ds = nt(dom, qkv[2, half])
                 pf = p.astype(F32)
                 dz = (pf * (ds - jnp.sum(pf * ds, axis=-1, keepdims=True))).astype(BF)
-                acc[0] = acc[0] + nn(dz, qkv[1, half]) * mask
-                acc[1] = acc[1] + tn(dz, qkv[0, half]) * mask
+                r[:, spans[0]] = r[:, spans[0]] + nn(dz, qkv[1, half]) * mask
+                r[:, spans[1]] = r[:, spans[1]] + tn(dz, qkv[0, half]) * mask
                 square = tn(flips[s], dz)
                 if s == 0:
                     high = square.astype(BF)
@@ -1085,7 +1294,7 @@
                     square = nn(high, pos[...]) + nn(low, pos[...])
                 wide = jnp.concatenate([square, jnp.zeros_like(square)], axis=1)
                 skew = pltpu.roll(wide, 0, 1, stride=1, stride_axis=0)
-                rel_out[pl.ds(s * heads + index, 1), :] = jnp.sum(skew, axis=0, keepdims=True)
+                stats[s, pl.ds(16 + index, 1), : 2 * rows] = jnp.sum(skew, axis=0, keepdims=True)
                 return c
 
             lax.fori_loop(0, half_heads, head, 0)
@@ -1095,7 +1304,7 @@
                 blank = jnp.zeros((TILE, HEAD_LANES), F32)
                 v = 0.0
                 for kind, shift, factor in ((0, 288, scale), (1, 576, scale), (2, 864, 1.0)):
-                    part = jnp.concatenate([acc[kind, ds, :] * factor, blank, blank], axis=1)
+                    part = jnp.concatenate([r[ds, spans[kind]] * factor, blank, blank], axis=1)
                     v = v + pltpu.roll(part, shift, 1)
                 v = v.astype(BF)
                 dqkv[where, ds, :] = v
@@ -1103,6 +1312,8 @@
 
             stat(s, 10 + half, by_rows(rows, gather_rows, zero8()))
         give("dqkv", dqkv.at[2], dqkv.at[1])
+        if s == 1:
+            fetch("xm", i_xm, r)
         xs_free = xi + 1
         if xs_free > 1:
             settle("x out %d" % (xs_free - 2))
@@ -1112,16 +1323,24 @@
         send_across(xs_free)
         if s == 1:
             fetch("w%d" % third, w.at[1], wslot.at[third])
+        if s == 1:
+            pump(("finish", 0))
         settle("dqkv in")
         settle("dattn in")
         settle("n1")
         settle("o")
         product(
             base + 2,
-            lambda j: [(flat(n1[...]), cols_of(dqkv, j))]
+            lambda j: [(flat(hid[...]), cols_of(dqkv, j))]
             + ([(flat(dattn[...]), flat(o[...]))] if j == 0 else []),
         )
         pump(("begin", base + 2))
+        if s == 1:
+            pump(("mated", 1), ("arrive", 1, 0), ("step", 1, 1))
+            end_forward()
+            pump(("arrive", 1, 1), ("step", 1, 2))
+        else:
+            pump(("arrive", 3, 1), ("step", 3, 2), ("arrive", 3, 2), ("step", 3, 3))
         settle("x in %d" % xs_free)
         settle("hat1")
 
@@ -1137,9 +1356,119 @@
         stat(s, 0, c0)
         stat(s, 1, c1)
         stat(s, 12, c2)
-        fetch("dx", d, o_dx.at[s])
-        pump_rest(base, 2)
-
+        to_section("dx", s, d, o_dx)
+
+    def to_section(name, s, src, out):
+        here = pltpu.make_async_copy(src, out.at[at.core], locals_.next())
+        ss, rs = sends.next(), recvs.next()
+
+        @pl.when(at.core == s)
+        def _():
+            here.start()
+
+        @pl.when(at.core != s)
+        def _():
+            remote(src, out.at[at.core], ss, rs, at.other).start()
+
+        def sent():
+            @pl.when(at.core == s)
+            def _():
+                here.wait()
+
+            @pl.when(at.core != s)
+            def _():
+                remote(src, out.at[at.core], ss, rs, at.other).wait_send()
+
+        def arrived():
+            @pl.when(at.core == s)
+            def _():
+                remote(src, out.at[1 - at.core], ss, rs, at.other).wait_recv()
+
+        waiting.setdefault(name, []).append(sent)
+        waiting.setdefault("end", []).append(arrived)
+
+    def project_down():
+        xs[2] = (nt(dqkv[0], flat(wslot[0, 0])) + nt(dqkv[1], flat(wslot[0, 1]))).astype(BF)
+        copy = remote(xs.at[2], xr.at[2], sends.next(), recvs.next(), at.beside)
+        copy.start()
+        waiting.setdefault("y in", []).append(copy.wait_recv)
+        waiting.setdefault("y out", []).append(copy.wait_send)
+
+    def end_forward():
+        settle("y in")
+        settle("y out")
+        settle("xm")
+
+        def body(ds, c):
+            v = xs[2, ds, :].astype(F32) + xr[2, ds, :].astype(F32) + small[1, 9:10, :]
+            r[ds, :] = r[ds, :] + mod[1, 5:6, :] * v
+            return c + column_sum(dout[ds, :].astype(F32) * v)
+
+        stat(1, 5, by_rows(rows, body, zero8()))
+        to_section("result", 1, r, o_out)
+
+    def sums_begin():
+        stats[0, 12:13, :] = stats[1, 12:13, :]
+        return links.copy(stats.at[1 - at.core], got, at.other)
+
+    def sums_share(copy):
+        copy.wait_recv()
+        sums[0] = stats[at.core] + got[...]
+        row = lax.broadcasted_iota(jnp.int32, (8, ADA_LANES), 0)
+        lane = lax.broadcasted_iota(jnp.int32, (8, ADA_LANES), 1)
+        for m, value in ((at.core, stats[at.core, 0:8, :]), (1 - at.core, got[0:8, :])):
+            cut = jnp.where(
+                at.head == 0, value[:, :ADA_LANES], pltpu.roll(value, width - lw, 1)[:, :ADA_LANES]
+            )
+            cut = jnp.where((row < 6) & (lane < lw), cut, 0.0)
+            dm[at.dp, pl.ds(pl.multiple_of(m * 8, 8), 8), :] = cut
+        copies = links.to_all(lambda peer: dm.at[at.dp], dm.at[at.dp])
+        return copies, sums_round(0)
+
+    def sums_round(b):
+        return links.copy(sums.at[b], rounds.at[b], at.in_dp(at.flip(b)))
+
+    def sums_next(b, copy):
+        copy.wait_recv()
+        sums[b + 1] = sums[b] + rounds[b]
+        if b + 1 < rounds.shape[0]:
+            return sums_round(b + 1)
+        fetch("sums", sums.at[b + 1], o_sums)
+        return None
+
+    def cond_terms(copies):
+        for copy in copies:
+            copy.wait_recv()
+        fetch("dm", dm, o_dm)
+        lhs = flat(dm[...])
+        high = lhs.astype(BF)
+        low = (lhs - high.astype(F32)).astype(BF)
+        row = lax.rem(lax.broadcasted_iota(jnp.int32, (lhs.shape[0], 1), 0), 8)
+        total_ = jnp.zeros((lhs.shape[0], shard), F32)
+        for k in range(6):
+            cols = wada[:, k * ADA_LANES : (k + 1) * ADA_LANES]
+            total_ = total_ + jnp.where(row == k, nt(high, cols) + nt(low, cols), 0.0)
+        total_ = total_.reshape(at.count, 16, shard)
+        for m in range(2):
+            dc[at.core, at.head, m, :, :shard] = jnp.sum(total_[:, m * 8 : (m + 1) * 8, :], axis=1)
+        return links.around(dc)
+
+    def cond_share(copies):
+        for copy in copies:
+            copy.wait_recv()
+        for m in range(2):
+            value = (dc[0, 0, m] + dc[0, 1, m]) + (dc[1, 0, m] + dc[1, 1, m])
+            v = cl[:, m, :]
+            sig = 1.0 / (1.0 + jnp.exp(-v))
+            dg[at.dp, m] = value * (sig * (1.0 + v * (1.0 - sig)))
+        return links.to_all(lambda peer: dg.at[at.dp], dg.at[at.dp])
+
+    def cond_end(copies):
+        for copy in copies:
+            copy.wait_recv()
+        fetch("dg", dg, o_dc)
+
+    dc[...] = jnp.zeros_like(dc)
     loads(1)
     fetch("w0", w.at[5], wslot.at[0])
     fetch("w1", w.at[4], wslot.at[1])
@@ -1151,24 +1480,39 @@
     by_rows(rows, start_rows, 0)
     block_back(1)
     loads(0)
+    settle("result")
     r[...] = tn(place[...], d[...].astype(BF))
     settle("dx")
+    pump(("arrive", 1, 2), ("step", 1, 3))
 
     def move(ds, c):
         d[ds, :] = r[ds, :]
         return c
 
     by_rows(rows, move, 0)
-    pump(("mated", 1))
-    pump_rest(1, 0)
     block_back(0)
-    for r_ in (4, 5):
-        pump(("mated", r_))
-        pump_rest(r_, 0)
+    copy = sums_begin()
+    pump(("arrive", 3, 3), ("finish", 3))
+    copies, copy = sums_share(copy)
+    pump(("arrive", 4, 0), ("step", 4, 1))
+    copy = sums_next(0, copy)
+    copies = cond_terms(copies)
+    pump(("arrive", 4, 1), ("step", 4, 2))
+    for b in range(1, rounds.shape[0]):
+        copy = sums_next(b, copy)
+        pump(("arrive", 4, b + 1))
+        if b + 2 < chain:
+            pump(("step", 4, b + 2))
+    copies = cond_share(copies)
+    pump(("finish", 4), ("mated", 5), ("arrive", 5, 0), ("step", 5, 1))
+    cond_end(copies)
+    pump_rest(5, 1)
     if fused:
         for r_ in range(len(ORDER) - slots, len(ORDER)):
             scatter.drain(r_)
         scatter.end()
+    for wait in links.waiting:
+        wait()
     for name in list(waiting):
         settle(name)
 
@@ -1177,6 +1521,9 @@
     fused, chain, heads, head_dim = cfg
     rows, width = small[0].shape
     pieces, _, groups, shard, _ = w.shape
+    count, _, cond_lanes = small[3].shape
+    steps = count.bit_length() - 1
+    many = 2 * (count - 1) + 6 + steps
     bf, f = lambda *s: pltpu.VMEM(s, BF), lambda *s: pltpu.VMEM(s, F32)
     dma = lambda *s: pltpu.SemaphoreType.DMA(s)
     out_shape = [
@@ -1184,8 +1531,10 @@
         if fused
         else jax.ShapeDtypeStruct((pieces, groups, shard, width), BF),
         jax.ShapeDtypeStruct((2, rows, width), F32),
-        jax.ShapeDtypeStruct((2, 16, width), F32),
-        jax.ShapeDtypeStruct((2 * heads, 2 * rows), F32),
+        jax.ShapeDtypeStruct((2, rows, width), F32),
+        jax.ShapeDtypeStruct((24, width), F32),
+        jax.ShapeDtypeStruct((count, 16, ADA_LANES), F32),
+        jax.ShapeDtypeStruct((count, 2, count, cond_lanes), F32),
     ]
     some = 3 if fused else 1
     links = chain if fused else 1
@@ -1194,7 +1543,6 @@
         bf(2, 2, groups, shard, width),
         bf(rows, width),
         f(2, rows, 128),
-        bf(2, rows, width),
         bf(3, 2, rows, HEAD_LANES),
         bf(heads, rows, rows),
         bf(2, rows, HEAD_LANES),
@@ -1203,7 +1551,6 @@
         bf(2, rows, width),
         bf(2, rows, width),
         bf(2, rows, width),
-        bf(rows, width),
         f(rows, width),
         f(rows, width),
         bf(2, rows, width),
@@ -1211,14 +1558,20 @@
         bf(2, rows, width),
         bf(3, rows, width),
         bf(2, rows, HEAD_LANES),
-        f(3, rows, HEAD_LANES),
-        bf(2, rows, width),
-        bf(4, rows, width),
+        bf(3, rows, width),
+        bf(3, rows, width),
         bf(4, groups, shard, width),
         bf(some, links, block, width),
         bf(some, links + 1, block, width),
         bf(some, block, width),
-        f(some, block, width),
+        f(2, block, width),
+        f(2, 24, width),
+        f(24, width),
+        f(steps + 1, 24, width),
+        f(steps, 24, width),
+        f(count, 16, ADA_LANES),
+        f(2, 2, 2, count, cond_lanes),
+        f(count, 2, count, cond_lanes),
         dma(6, 3 * links + 1),
         dma(6, 3 * links + 1),
         dma(6),
@@ -1227,7 +1580,9 @@
         pltpu.SemaphoreType.REGULAR((3,)),
         dma(16),
         dma(16),
-        dma(48),
+        dma(56),
+        dma(many),
+        dma(many),
     ]
 
     def body(*refs):
@@ -1239,7 +1594,7 @@
         body,
         out_shape=out_shape,
         in_specs=[hbm] * (1 + len(saved)) + [vm] * len(small),
-        out_specs=[hbm, hbm, vm, vm],
+        out_specs=[hbm] * len(out_shape),
         scratch_shapes=scratch,
         compiler_params=pltpu.CompilerParams(
             collective_id=1, has_side_effects=True, vmem_limit_bytes=VMEM_BYTES
@@ -1285,41 +1640,46 @@
     qkv = jnp.transpose(w_qkv[0], (1, 0, 2))
     out_t = w_out[0].T
     down_t = w_down[0].T
-    pack = []
+    halves = []
     for half in range(2):
         at = slice(half * hw, (half + 1) * hw)
         fat = slice(half * fw, (half + 1) * fw)
         a = jnp.concatenate([out_t[:, at], qkv[0][:, at], qkv[1][:, at], qkv[2][:, at]], axis=1)
-        pack.append(jnp.stack([a, w_up[0][:, fat], down_t[:, fat]]))
-    keep = mine(c, pack)
-    got = swap(mine(1 - c, pack), "section")
-    own = jnp.concatenate([pick(c, keep, got), pick(c, got, keep)])
-    ids = lax.all_gather(jnp.stack([labels[:, 0], timesteps[:, 0]]), "dp")
-    labels_all = ids[:, 0].reshape(-1)
-    steps_all = ids[:, 1].reshape(-1)
-    label_pick = (labels_all[:, None] == jnp.arange(classes)[None, :]).astype(BF)
-    cond = nn(label_pick, class_table) + time_features(steps_all, width)
-    cond_low = jax.nn.silu(cond)
+        halves.append(jnp.stack([a, w_up[0][:, fat], down_t[:, fat]]))
+    pack = jnp.stack(halves)
     fr = width // dp_count
-    cond_part = lax.dynamic_slice_in_dim(cond_low, dp * fr, fr, 1)
-    ada = w_ada[0].astype(F32).reshape(fr, 6 * lw)
-    part = jnp.dot(cond_part, ada, precision=PRECISE).reshape(dp_count, micro, 6, lw)
-    summed = jnp.sum(lax.all_to_all(part, "dp", 0, 0, tiled=True), axis=0) + b_ada[0].astype(F32)
-    mod_own = mine(c, summed)
-    mod_got = swap(mine(1 - c, summed), "section")
-    mod_half = jnp.stack([pick(c, mod_own, mod_got), pick(c, mod_got, mod_own)])
-    mod_other = swap(mod_half, "head")
-    mod = jnp.concatenate(
-        [pick(h, mod_half, mod_other), pick(h, mod_other, mod_half)], axis=2
+
+    label_pick = (labels == jnp.arange(classes)[None, :]).astype(BF)
+    cond = nn(label_pick, class_table) + time_features(timesteps[:, 0], width)
+    blocks = jnp.transpose(cond.reshape(micro, dp_count, fr), (1, 0, 2))
+    tags = jnp.broadcast_to(labels.astype(F32)[None], (dp_count, micro, 1))
+    cond_lanes = -(-(fr + 1) // 128) * 128
+    blocks = jnp.concatenate([blocks, tags], axis=2)
+    blocks = jnp.pad(blocks, ((0, 0), (0, 8 - micro), (0, cond_lanes - fr - 1)))
+    ada = jnp.pad(w_ada[0], ((0, 0), (0, 0), (0, ADA_LANES - lw))).reshape(fr, 6 * ADA_LANES)
+    b_ada_in = jnp.pad(b_ada[0].astype(F32), ((0, 2), (0, ADA_LANES - lw)))
+
+    def row_block(value):
+        return jnp.pad(value.astype(F32), ((0, 0), (0, width - value.shape[1])))
+
+    qv = b_qv[0].reshape(2, 2, hw)
+    none = jnp.zeros((2, hw), BF)
+    qv_rows = jnp.stack([qv[0], none, qv[1], none], axis=1).reshape(8, hw)
+    qv_rows = jnp.pad(qv_rows, ((0, 0), (0, HEAD_LANES - hw)))
+    rel = rel_table[0]
+    rel = jnp.concatenate(
+        [rel[:, length - 1 :: -1], jnp.zeros((heads, 1), BF), rel[:, : length - 1 : -1]], axis=1
     )
-
-    def shared(value):
-        return both(value[0].astype(BF))
-
-    b_qv2, b_out2, b_up2, b_down2, rel2 = [
-        [v.astype(F32) for v in shared(t)] for t in (b_qv, b_out, b_up, b_down, rel_table)
-    ]
-
+    small_own = jnp.concatenate(
+        [
+            row_block(qv_rows),
+            row_block(b_out),
+            row_block(b_down),
+            row_block(b_up[0].reshape(2, fw)),
+            jnp.zeros((4, width), F32),
+            row_block(rel),
+        ]
+    )
 
     kept = kept_mask[c, 0]
     source = jnp.cumsum(kept) - 1
@@ -1333,52 +1693,41 @@
     flips = jnp.stack([pos[:, ::-1], mirror])
     drop = jnp.broadcast_to((1 - kept)[:, None].astype(F32), (rows, 128))
 
-    lanes = HEAD_LANES - hw
-    rel_rows = jnp.stack(rel2)
-    blank = jnp.zeros((2, heads, 1), F32)
-    rel_rows = jnp.concatenate(
-        [rel_rows[:, :, length - 1 :: -1], blank, rel_rows[:, :, : length - 1 : -1]], axis=2
-    ).reshape(2 * heads, 2 * length)
-    bqv = jnp.stack(b_qv2).reshape(2, 2, 2, hw)
-    none = jnp.zeros((2, 2, hw), F32)
-    bqv = jnp.stack([bqv[:, 0], none, bqv[:, 1], none], axis=2)
-    bqv = jnp.pad(bqv, ((0, 0), (0, 0), (0, 0), (0, lanes))).reshape(16, HEAD_LANES)
-    mod = jnp.pad(mod, ((0, 0), (0, 2), (0, 0)))
-    fused = (width // dp_count) % 16 == 0
+    fused = dp_count == 8 and fr % 16 == 0
     cfg = (fused, dp_count // 2, heads, head_dim)
     if fused:
-        source_w = own
+        source_w = pack
     else:
-        half_w_ = lax.all_gather(own, "dp", axis=1, tiled=True)
+        other_w = swap(mine(1 - c, halves), "section")
+        own_w = mine(c, halves)
+        own_w = jnp.concatenate([pick(c, own_w, other_w), pick(c, other_w, own_w)])
+        half_w_ = lax.all_gather(own_w, "dp", axis=1, tiled=True)
         other_w = swap(half_w_, "section")
         source_w = jnp.stack([pick(c, half_w_, other_w), pick(c, other_w, half_w_)], axis=1)
-        source_w = source_w.reshape(6, 2, 8, width // 8, own.shape[2])
+        source_w = source_w.reshape(6, 2, 8, width // 8, pack.shape[3])
     small_in = (
         tokens[c],
-        mod,
-        bqv,
-        jnp.stack(b_out2),
-        jnp.stack(b_up2).reshape(2, 2, fw),
-        jnp.stack(b_down2),
-        rel_rows,
+        blocks,
+        ada,
+        b_ada_in,
+        small_own,
         pos,
         seg,
         place,
         drop,
         mask_token.astype(F32)[None, :],
     )
-    full, *saved, outs = forward_call(cfg, source_w, small_in, dp_count)
-    small_back = (out_grad[c], mod, flips, pos, place, drop)
-    red, dx, stats, rel_out = backward_call(cfg, full, saved, small_back)
-    rel_out = rel_out.reshape(2, heads, 2 * length)[:, :, 2 * length - 2 :: -1]
+    full, *saved, mod, cond_all, small_all, outs = forward_call(cfg, source_w, small_in, dp_count)
+    small_back = (out_grad[c], mod, small_all, cond_all, ada, flips, pos, place, drop)
+    red, dx, outs_b, sums, dm, dc = backward_call(cfg, full, saved, small_back)
 
     if fused:
         g0, g1 = red[:, 0], red[:, 1]
     else:
         red = lax.psum_scatter(
-            red.reshape(6, width, own.shape[2]), "dp", scatter_dimension=1, tiled=True
+            red.reshape(6, width, pack.shape[3]), "dp", scatter_dimension=1, tiled=True
         ).astype(F32)
-        red = red.reshape(2, 3, fr, own.shape[2])
+        red = red.reshape(2, 3, fr, pack.shape[3])
         g_own = mine(c, red)
         g_got = swap(mine(1 - c, red), "section")
         g0, g1 = pick(c, g_own, g_got), pick(c, g_got, g_own)
@@ -1392,73 +1741,45 @@
     g_out = jnp.concatenate([g0[0][:, :hw], g1[0][:, :hw]], axis=1).T
     g_up = jnp.concatenate([g0[1], g1[1]], axis=1)
     g_down = jnp.concatenate([g0[2], g1[2]], axis=1).T
-    dmod0, dmod1 = stats[0, :6], stats[1, :6]
-    mask_sum = stats[1, 12]
-
-    def small_of(s):
-        qv = [stats[s, 10 + half, at * hw : (at + 1) * hw] for at in (1, 3) for half in range(2)]
-        return (jnp.concatenate(qv), stats[s, 7], stats[s, 8:10].reshape(-1), stats[s, 6])
-
-    small0, small1 = small_of(0), small_of(1)
-    rel0, rel1 = rel_out[0], rel_out[1]
 
     half_w = width // 2
 
     def half(v):
         return lax.dynamic_slice_in_dim(v, h * half_w, half_w, v.ndim - 1)
 
-    vecs = []
-    for small, rel in ((small0, rel0), (small1, rel1)):
-        vecs.append(
-            jnp.concatenate([small[0], half(small[1]), small[2], half(small[3]), rel.reshape(-1)])
-        )
-    mask_half = half(mask_sum)
-    sent = jnp.concatenate([mine(1 - c, vecs), mask_half])
-    total = jnp.concatenate([mine(c, vecs), mask_half]) + swap(sent, "section")
-    total = lax.psum(total, "dp")
-    cuts = [2 * lw, half_w, ff, half_w, heads * (2 * length - 1), half_w]
-    parts = []
-    at = 0
-    for n in cuts:
-        parts.append(total[at : at + n])
-        at += n
-    g_b_qv = parts[0].reshape(2, lw)
-    g_rel = parts[4].reshape(heads, 2 * length - 1)
-
-    dm = [half(dmod0), half(dmod1)]
-    dm_own = mine(c, dm)
-    dm_got = swap(mine(1 - c, dm), "section")
-    dm_pair = jnp.stack([pick(c, dm_own, dm_got), pick(c, dm_got, dm_own)])
-    dm_all = lax.all_gather(dm_pair, "dp").reshape(dp_count * micro, 6 * lw)
-    g_ada = jnp.einsum("id,ie->de", cond_part, dm_all, precision=PRECISE).reshape(fr, 6, lw)
-    g_b_ada = jnp.sum(dm_all, axis=0).reshape(6, lw)
-    dcl = jnp.einsum("ie,de->id", dm_all, ada, precision=PRECISE)
-    dcl = lax.psum(dcl, ("section", "head"))
-    dcl = lax.all_gather(dcl, "dp", axis=1, tiled=True)
-    sig = jax.nn.sigmoid(cond)
-    dcond = half(dcl * (sig * (1.0 + cond * (1.0 - sig))))
-    g_class = jnp.einsum("ic,id->cd", label_pick.astype(F32), dcond, precision=PRECISE)
-
-    def settle(first, second):
-        got = swap(pick(c, second, first), "section")
-        own_part = pick(c, first, second)
-        return jnp.stack([pick(c, own_part, got), pick(c, got, own_part)])[None]
+    g_b_qv = jnp.stack(
+        [
+            jnp.concatenate([sums[10, at * hw : (at + 1) * hw], sums[11, at * hw : (at + 1) * hw]])
+            for at in (1, 3)
+        ]
+    )
+    g_b_up = sums[8:10, :fw].reshape(-1)
+    g_rel = sums[16 : 16 + heads, 2 * length - 2 :: -1]
+
+    dm = dm.reshape(dp_count, micro, 8, ADA_LANES)[:, :, :6, :lw]
+    cond_part = jax.nn.silu(cond_all[:, :micro, :fr])
+    g_ada = jnp.einsum("jmf,jmke->fke", cond_part, dm, precision=PRECISE)
+    g_b_ada = jnp.sum(dm, axis=(0, 1))
+    labels_all = cond_all[:, :micro, fr].astype(jnp.int32).T.reshape(-1)
+    dcond = jnp.transpose(dc[..., :fr], (1, 2, 0, 3)).reshape(micro * dp_count, width)
+    pick_all = (labels_all[:, None] == jnp.arange(classes)[None, :]).astype(F32)
+    g_class = jnp.einsum("ic,id->cd", pick_all, half(dcond), precision=PRECISE)
 
     return (
-        settle(outs[0], outs[1]),
-        settle(dx[0], dx[1]),
+        pick(c, outs, outs_b)[None],
+        dx[None],
         g_qkv[None],
         g_b_qv[None],
         g_out[None],
-        parts[1][None],
+        half(sums[7])[None],
         g_up[None],
-        parts[2][None],
+        g_b_up[None],
         g_down[None],
-        parts[3][None],
+        half(sums[6])[None],
         g_ada[None],
         g_b_ada[None],
         g_rel[None],
-        parts[5],
+        half(sums[12]),
         g_class,
     )
 

time: 676 us -> 473 us (0.70)
  blocking collectives: 133 us -> 0 us
  other arithmetic: 36.1 us -> 18.8 us
  local copies, waits for them, and re-layouts: 39.1 us -> 22.5 us
  Pallas kernels: 436 us -> 420 us
  starting transfers between devices: 8.21 us -> 0 us
    all_gather x3 -> x0, blocking collectives: 85.3 us -> none  [the longest x1 32.9 us: per_device(): dm_all = lax.all_gather(dm_pair, 'dp').reshape(dp_count * micro, 6 * lw)]
    psum x2 -> x0, blocking collectives: 48 us -> none  [the longest x1 36.5 us: per_device(): total = lax.psum(total, 'dp')]
    pallas_call x1, Pallas kernels: 212 us -> 195 us  [forward_call(): pl.pallas_call(body, out_shape=out_shape, in_specs=[hbm] + [vm] * len(sma...]
    select_n x12 -> x0, other arithmetic: 8.27 us -> none  [pick(): return jnp.where(index == 0, first, second)]
  transfers between devices with their start and end apart: 13 -> 0, of which waited for: 2 -> 0; matrix products, arithmetic and copies ran while one was open for 10% -> 0% of each run, Pallas kernels for 0% -> 0%
where the time goes in v3:
time: 473 us; the launch traced here: 469 us
  Pallas kernels  420 us (89%)
  local copies, waits for them, and re-layouts  22.5 us (5%)
  other arithmetic  18.8 us (4%)
  matrix products  6.38 us (1%)
    pallas_call x1, Pallas kernels, backward_call(): pl.pallas_call(body, out_shape=out_shape, in_specs=[hbm] * (1 + len(saved...  226 us
    pallas_call x1, Pallas kernels, forward_call(): pl.pallas_call(body, out_shape=out_shape, in_specs=[hbm] + [vm] * len(sma...  195 us

profile of v3, /device:TPU:0, one launch (start us, length us, event | category | flops | bytes accessed | tf_op | source)
XLA Modules:
  0.0 469.5 jit_solution(18019415206160596170)
XLA Ops:
  0.7 1.2 slice_bitcast_fusion.8
  1.9 1.1 slice_bitcast_fusion.9
  3.0 0.1 fusion.21
  3.2 0.1 fusion.20
  3.3 0.1 fusion.19
  3.4 0.1 fusion.18
  3.5 0.2 concatenate.42
  3.8 0.2 concatenate.43
  4.0 0.3 maximum_bitcast_fusion.3
  4.3 1.5 pad_maximum_fusion.refs_0_
  5.8 2.5 dynamic-slice_bitcast_fusion
  8.4 0.2 multiply_cosine_fusion
  8.6 0.4 convolution_add_fusion
  9.0 0.1 reshape.162
  9.1 0.7 select_maximum_fusion.refs_2_
  9.8 0.3 copy.59
  10.1 0.3 pad.33.clone
  10.5 1.1 copy.61
  11.7 0.6 pad_convert_fusion.2.refs_4_
  12.5 0.4 reverse
  13.0 0.2 rev.12
  13.3 1.9 concatenate.47.refs_5_
  15.2 0.3 reduce-window.9
  15.6 0.1 slice_reduce_fusion.6
  15.8 0.6 reduce_sum.18
  16.5 0.6 iota_compare_fusion.6
  17.1 0.8 fusion.6.refs_6_.refs_21_
  17.9 0.8 compare_select_fusion.refs_7_
  18.7 0.8 fusion.3.refs_8_.refs_22_
  19.5 0.8 broadcast_in_dim.79.refs_9_.refs_23_
  20.2 0.6 reshape.170.refs_10_
  20.8 194.6 %forward_blocks.1 = (bf16[6,2,8,144,1152]{4,3,2,1,0:T(8,128)(2,1)}, bf16[2,256,1152]{2,1,0:T(8,128)(2,1)}, f32[2,2,256,128]{3,2,1,0:T(8,128)}, bf16[2,2,256,1152...) custom-call(bf16[2,3,144,1152]{3,2,1,0:T(8,128)(2,1)} %pad_maximum_f, ...), custom_call_target="tpu_custom_call" | custom-call | tf_op jit(solution)/shard_map/forward_blocks/pallas_call | solution.py:815
  215.5 0.4 rev.14
  215.9 0.7 pad_maximum_fusion.1.refs_20_
  216.7 225.9 %backward_blocks.1 = (f32[3,2,144,1152]{3,2,1,0:T(8,128)}, f32[2,256,1152]{2,1,0:T(8,128)}, f32[2,256,1152]{2,1,0:T(8,128)}, f32[24,1152]{1,0:T(8,128)}, f32[8,1...) custom-call(bf16[6,2,8,144,1152]{4,3,2,1,0:T(8,128)(2,1)} %get-tuple-element.41.refs_0_, ...), custom_call_target="tpu_custom_call" | custom-call | tf_op jit(solution)/shard_map/backward_blocks/pallas_call | solution.py:1593
  442.5 3.5 select_bitcast_fusion
  446.0 0.3 slice_bitcast_fusion.1
  446.3 0.2 fusion.17
  446.5 0.2 fusion.16
  446.7 0.1 maximum_bitcast_fusion.7
  446.9 0.1 maximum_bitcast_fusion.6
  447.0 0.1 maximum_bitcast_fusion.5
  447.1 1.1 maximum_bitcast_fusion.2
  448.2 0.9 slice_reduce_fusion.5
  449.2 0.6 maximum_bitcast_fusion.9
  449.9 0.9 maximum_bitcast_fusion.8
  450.7 0.9 fusion.22
  451.6 0.7 constant_dynamic-slice_fusion.1
  452.2 1.1 maximum_bitcast_fusion
  453.4 0.8 slice_bitcast_fusion.14
  454.2 0.6 copy.62
  454.8 1.1 maximum_bitcast_fusion.1
  456.0 0.7 constant_dynamic-slice_fusion
  456.7 0.9 divide_multiply_fusion
  457.5 3.3 convolution_bitcast_fusion
  460.8 0.6 broadcast_in_dim.90
  461.4 0.8 slice.214
  462.3 0.3 reverse.1
  462.5 0.7 slice_bitcast_fusion.15
  463.2 0.7 dynamic-slice_reduce_fusion
  464.0 0.1 reshape.168
  464.1 0.8 slice_convert_fusion
  465.1 2.7 fusion.7
  467.8 1.4 copy.72
  (74 shorter events, 1.4 us)
Async XLA Ops:
  0.6 2.4 copy-start.7
  0.7 2.5 copy-start.5
  5.8 2.5 copy-start.16
  5.8 2.6 copy-start.18
  5.8 2.8 copy-start.2
  5.8 4.1 copy-start.4
  10.4 1.2 copy-start.10
  10.4 1.8 copy-start.9
  10.5 2.1 copy-start.12
  10.5 2.8 copy-start.11
  10.5 2.8 copy-start.13
  10.5 2.8 copy-start.14
  10.5 4.7 %copy-start.17 = (s32[2,1,256]{2,1,0:T(1,128)S(1)}, s32[2,1,256]{2,1,0:T(1,128)}, u32[]{:S(2)}) copy-start(s32[2,1,256]{2,1,0:T(1,128)} %param.19) | copy-start | bytes 6148
  10.5 9.7 %copy-start.15 = (bf16[1152]{0:T(1024)(128)(2,1)S(1)}, bf16[1152]{0:T(1024)(128)(2,1)}, u32[]{:S(2)}) copy-start(bf16[1152]{0:T(1024)(128)(2,1)} %param.33) | copy-start | bytes 6916
  20.8 194.6 %copy-start.3 = (bf16[256,256]{1,0:T(8,128)(2,1)S(1)}, bf16[256,256]{1,0:T(8,128)(2,1)}, u32[]{:S(2)}) copy-start(bf16[256,256]{1,0:T(8,128)(2,1)} %fusion.6.refs_6_.refs_21_) | copy-start | bytes 393220
  442.5 3.5 copy-start
  453.4 3.2 copy-start.6
  456.0 7.9 %copy-start.8 = (f32[8,2,8,256]{3,2,1,0:T(8,128)S(1)}, f32[8,2,8,256]{3,2,1,0:T(8,128)}, u32[]{:S(2)}) copy-start(f32[8,2,8,256]{3,2,1,0:T(8,128)} %get-tuple-element.64) | copy-start | bytes 393220
  460.8 7.0 %copy-start.1 = (f32[2,256,1152]{2,1,0:T(8,128)S(1)}, f32[2,256,1152]{2,1,0:T(8,128)}, u32[]{:S(2)}) copy-start(f32[2,256,1152]{2,1,0:T(8,128)} %get-tuple-element.60) | copy-start | bytes 7077892

commit v4 on v3

--- a/solution.py
+++ b/solution.py
@@ -154,6 +154,10 @@
         ]
 
 
+COPY_BY_MATE = (1, 3, 5)
+SUM_BY_MATE = (1, 2, 3, 4)
+
+
 class Gather:
     def __init__(self, at, pack, w, ssem, rsem, lsem):
         self.at, self.pack, self.w = at, pack, w
@@ -171,8 +175,8 @@
         return remote(
             self.pack.at[1 - core, t],
             self.w.at[3 * core + t, 1 - core, self.at.dp],
-            self.ssem.at[t, 3 * self.at.chain + 2],
-            self.rsem.at[t, 3 * self.at.chain + 2],
+            self.ssem.at[t, 5 * self.at.chain + 1],
+            self.rsem.at[t, 5 * self.at.chain + 1],
             self.at.other,
         )
 
@@ -182,8 +186,8 @@
         return remote(
             self.pack.at[1 - core, t],
             block,
-            self.ssem.at[t, 3 * self.at.chain + 2],
-            self.rsem.at[t, 3 * self.at.chain + 2],
+            self.ssem.at[t, 5 * self.at.chain + 1],
+            self.rsem.at[t, 5 * self.at.chain + 1],
             self.at.other,
         )
 
@@ -230,13 +234,20 @@
         b = self.block(p, self.at.mate_z, 1 - self.at.y)
         return self.copy(b, b, p, 3 * self.at.chain, self.at.mate)
 
-    def other_out(self, p):
-        b = self.w.at[p, self.at.core]
-        return self.copy(b, b, p, 3 * self.at.chain + 1, self.at.other)
+    def over(self, p, zz, yy):
+        b = self.block(p, zz, yy)
+        own = jnp.where(yy == self.at.y, 0, 1)
+        return self.copy(b, b, p, 3 * self.at.chain + 1 + 2 * zz + own, self.at.other)
+
+    def over_in(self, p, zz, own):
+        yy = self.at.y if own == 0 else 1 - self.at.y
+        b = self.w.at[p, 1 - self.at.core, zz * 2 + yy]
+        return self.copy(b, b, p, 3 * self.at.chain + 1 + 2 * zz + own, self.at.other)
 
     def other_in(self, p):
-        b = self.w.at[p, 1 - self.at.core]
-        return self.copy(b, b, p, 3 * self.at.chain + 1, self.at.other)
+        for zz in range(self.at.chain):
+            for own in range(2):
+                self.over_in(p, zz, own).wait_recv()
 
     def start(self, p):
         s, t = divmod(p, 3)
@@ -259,9 +270,11 @@
         def _():
             self.down(p, 1).start()
 
+        self.over(p, self.at.z, self.at.y).start()
+
     def step(self, p, k):
         z, chain = self.at.z, self.at.chain
-        odd = p % 2 == 1
+        odd = p in COPY_BY_MATE
 
         @pl.when(z >= k)
         def _():
@@ -279,6 +292,7 @@
 
             else:
                 self.cross(p, z - k).start()
+            self.over(p, z - k, self.at.y).start()
 
         @pl.when(z + k < chain)
         def _():
@@ -296,30 +310,34 @@
 
             else:
                 self.cross(p, z + k).start()
+            self.over(p, z + k, self.at.y).start()
 
         if k == 1 and odd:
             self.cross_in(p, z).wait_recv()
             self.mate_out(p).start()
+            self.over(p, z, 1 - self.at.y).start()
 
     def finish(self, p):
         z = self.at.z
         for j in range(self.at.chain):
-            if p % 2 == 1:
+            if p in COPY_BY_MATE:
 
                 @pl.when((j != z) & (j != self.at.mate_z))
                 def _():
                     self.cross_in(p, j).wait_recv()
+                    self.over(p, j, 1 - self.at.y).start()
 
             else:
                 self.cross_in(p, j).wait_recv()
-        if p % 2 == 1:
+                self.over(p, j, 1 - self.at.y).start()
+        if p in COPY_BY_MATE:
             self.mate_in(p).wait_recv()
-        self.other_out(p).start()
+            self.over(p, self.at.mate_z, 1 - self.at.y).start()
 
     def drain(self, p):
         z, chain = self.at.z, self.at.chain
         for j in range(chain):
-            if p % 2 == 1:
+            if p in COPY_BY_MATE:
 
                 @pl.when(j != self.at.mate_z)
                 def _():
@@ -327,7 +345,7 @@
 
             else:
                 self.cross(p, j).wait_send()
-        if p % 2 == 1:
+        if p in COPY_BY_MATE:
             self.mate_out(p).wait_send()
         for k in range(1, chain):
 
@@ -339,7 +357,9 @@
             def _():
                 self.down(p, k).wait_send()
 
-        self.other_out(p).wait_send()
+        for j in range(chain):
+            for yy in range(2):
+                self.over(p, j, yy).wait_send()
         if p < 3:
             self.share(p).wait_send()
 
@@ -382,6 +402,30 @@
     )
 
 
+def spread_masks(kept, place, pos, drop, seg=None):
+    length = kept.shape[1]
+    u = lax.broadcasted_iota(jnp.int32, (length, length), 0)
+    v = lax.broadcasted_iota(jnp.int32, (length, length), 1)
+    uf, vf = u.astype(F32), v.astype(F32)
+    column = jnp.sum(jnp.where(u == v, kept, 0.0), axis=1, keepdims=True)
+    source = jnp.sum(jnp.where(v <= u, kept, 0.0), axis=1, keepdims=True) - 1.0
+    source_row = jnp.sum(jnp.where(u <= v, column, 0.0), axis=0, keepdims=True) - 1.0
+    count = jnp.sum(kept, axis=1, keepdims=True)
+    place[...] = (jnp.where(source == vf, 1.0, 0.0) * column).astype(BF)
+    pad = jnp.where(uf >= count, 1.0, 0.0)
+    first = jnp.where(v == 0, pad, 0.0)
+    pos[...] = (jnp.where(source_row == uf, 1.0, 0.0) * kept + first).astype(BF)
+    drop[...] = jnp.broadcast_to(1.0 - column, drop.shape)
+    if seg is not None:
+        seg[...] = jnp.where(pad == jnp.where(vf >= count, 1.0, 0.0), 0.0, NEGATIVE)
+
+
+def diagonal(length, mirrored=False):
+    u = lax.broadcasted_iota(jnp.int32, (length, length), 0)
+    v = lax.broadcasted_iota(jnp.int32, (length, length), 1)
+    return jnp.where(u + v == length - 1 if mirrored else u == v, 1.0, 0.0).astype(BF)
+
+
 def head_mask(i, head_dim):
     lane = lax.broadcasted_iota(jnp.int32, (1, HEAD_LANES), 1)
     return ((lane >= i * head_dim) & (lane < (i + 1) * head_dim)).astype(F32)
@@ -391,17 +435,19 @@
     fused, chain, heads, head_dim = cfg
     refs = list(refs)
     pack = refs.pop(0)
-    tok, cond, wada, bada, small_own, pos, seg, place, drop, mtok = refs[:10]
-    refs = refs[10:]
+    i_tok, cond, i_wada, b_ada, kept, b_qv, b_out, b_down, b_up, rel, mtok = refs[:11]
+    refs = refs[11:]
     w = refs.pop(0) if fused else pack
     (
         s_hat1, s_inv, s_n1, s_qkv, s_p, s_o, s_branch, s_hat2, s_n2, s_hid, s_slope, s_y,
-        s_full, s_xm, o_mod, o_cl, o_small, outs,
+        s_full, s_xm, o_mod, o_cl, o_small, s_e,
     ) = refs[:18]
     refs = refs[18:]
     (
         wa, wu, wd, res, hat, inv, n, r, qkv, prob, o, branch, hid, slope, y_keep,
-        xs, xr, toep, small, cl, part, got, pair, mod, gs, gr, gl, ssem, rsem, lsem, ms, mr,
+        xs, xr, toep, small, cl, part, got, pair, mod, tok, wada, pos, seg, place, drop,
+        eye, small_own, wide, bada,
+        gs, gr, gl, ssem, rsem, lsem, ms, mr,
     ) = refs
     at = Place(chain)
     rows, width = res.shape
@@ -439,7 +485,7 @@
 
     def load(p, slot):
         if fused:
-            gather.other_in(p).wait_recv()
+            gather.other_in(p)
         keep("load%d" % p, w.at[p], slot)
 
     def send_cond():
@@ -485,6 +531,22 @@
         keep("cl", cl, o_cl)
 
     def share_small():
+        wide[...] = jnp.zeros_like(wide)
+        wide[0:2, :lw] = b_qv[0].astype(F32)
+        small_own[...] = jnp.zeros_like(small_own)
+        value = wide[...]
+        for half in range(2):
+            for k in range(2):
+                row = half * 4 + 2 * k
+                small_own[row : row + 1, :HEAD_LANES] = value[k : k + 1, :HEAD_LANES]
+            value = pltpu.roll(value, ADA_LANES - lw // 2, 1)
+        small_own[8:9, :] = b_out[...].astype(F32)
+        small_own[9:10, :] = b_down[...].astype(F32)
+        small_own[10:11, :] = b_up[:, :width].astype(F32)
+        small_own[11:12, :] = b_up[:, width:].astype(F32)
+        small_own[16 : 16 + heads, : 2 * rows - 1] = rel[0].astype(F32)
+        bada[...] = jnp.zeros_like(bada)
+        bada[0:6, :lw] = b_ada[0].astype(F32)
         small[pl.ds(at.core, 1)] = small_own[...][None]
         return links.copy(small_own, small.at[at.core], at.other)
 
@@ -547,12 +609,15 @@
             index = half * half_heads + i
             mask = head_mask(i, head_dim).astype(BF)
             line = small[s, pl.ds(16 + index, 1), : 2 * rows]
-            skew = pltpu.roll(jnp.broadcast_to(line, (rows, 2 * rows)), 0, 1, stride=1, stride_axis=0)
-            bias = skew[:, :rows]
+            skew = pltpu.roll(
+                jnp.broadcast_to(line, (rows, 2 * rows)), rows + 1, 1, stride=1, stride_axis=0
+            )
+            toep[...] = skew[:, :rows].astype(BF)
             if s == 0:
-                toep[...] = bias.astype(BF)
-                left = nn(pos[...], toep[...]).astype(BF)
+                left = nt(pos[...], toep[...]).astype(BF)
                 bias = nt(left, pos[...]) + seg[...]
+            else:
+                bias = nt(eye[...], toep[...])
             z = nt(qkv[0, half] * mask, qkv[1, half]) * scale + bias
             e = jnp.exp(z - jnp.max(z, axis=-1, keepdims=True))
             p = (e / jnp.sum(e, axis=-1, keepdims=True)).astype(BF)
@@ -637,41 +702,14 @@
 
         by_rows(rows, body, 0)
         keep("y", y_keep, s_y)
-        here = pltpu.make_async_copy(res, outs.at[at.core], locals_.next())
-        there = remote(res, outs.at[at.core], sends.next(), recvs.next(), at.other)
-
-        @pl.when(at.core == 0)
-        def _():
-            here.start()
-
-        @pl.when(at.core == 1)
-        def _():
-            there.start()
-
-        def sent():
-            @pl.when(at.core == 0)
-            def _():
-                here.wait()
-
-            @pl.when(at.core == 1)
-            def _():
-                there.wait_send()
-
-        def arrived():
-            @pl.when(at.core == 0)
-            def _():
-                remote(res, outs.at[1], there_s, there_r, at.other).wait_recv()
-
-        there_s, there_r = sends.ref.at[sends.count - 1], recvs.ref.at[recvs.count - 1]
-        waiting.setdefault("out", []).append(sent)
-        waiting.setdefault("end", []).append(arrived)
+        keep("out", res, s_e)
 
     def spread():
         r[...] = nn(place[...], res[...].astype(BF))
         settle("out")
 
         def body(ds, c):
-            res[ds, :] = r[ds, :] + drop[ds, 0:1] * mtok[...]
+            res[ds, :] = r[ds, :] + drop[ds, 0:1] * mtok[...].astype(F32)
             return c
 
         by_rows(rows, body, 0)
@@ -682,55 +720,69 @@
         gather.split()
         gather.start(0)
         gather.start(1)
+    keep("tok", i_tok.at[at.core], tok)
+    keep("wada", i_wada, wada)
+    spread_masks(kept[at.core].astype(F32), place, pos, drop, seg)
+    eye[...] = diagonal(rows)
+    settle("tok")
 
     def start_residual(ds, c):
         res[ds, :] = tok[ds, :].astype(F32)
         return c
 
     by_rows(rows, start_residual, 0)
+    pump(("step", 0, 1))
+    settle("wada")
     copies = modulation_terms(copies)
-    pump(("step", 0, 1), ("start", 2))
+    pump(("step", 0, 2), ("start", 2), ("step", 0, 3))
     copies = modulation_sum(copies)
-    pump(("step", 0, 2))
+    small_copy.wait_recv()
+    keep("small", small, o_small)
+    pump(("step", 1, 1))
     modulation(copies)
     norm_one(0)
-    small_copy.wait_recv()
-    keep("small", small, o_small)
-    pump(("step", 0, 3))
-    for s in range(2):
-        p = 3 * s
-        pump(("step", p + 1, 1), ("start", p + 3), ("finish", p))
-        if s == 1:
-            end_block(0, 1, copy)
-            spread()
-            norm_one(1)
-        pump(("step", p + 1, 2))
-        load(p, wa)
-        settle("load%d" % p)
-        project(s)
-        pump(("step", p + 1, 3))
-        attend(s, 0)
-        pump(("step", p + 2, 1), ("start", p + 4), ("finish", p + 1))
-        attend(s, 1)
-        copy = project_out(2 * s)
-        load(p + 1, wu)
-        pump(("step", p + 2, 2), ("step", p + 2, 3))
-        norm_two(s, 2 * s, copy)
-        if s == 0:
-            pump(("step", p + 3, 1), ("start", p + 5), ("finish", p + 2))
-        settle("load%d" % (p + 1))
-        hidden(s, 0)
-        if s == 0:
-            load(p + 2, wd)
-            pump(("step", p + 3, 2))
-        hidden(s, 1)
-        if s == 0:
-            settle("load%d" % (p + 2))
-            copy = project_down(2 * s + 1)
-            pump(("step", p + 3, 3))
+    pump(("step", 1, 2), ("start", 3), ("finish", 0), ("step", 1, 3))
+    load(0, wa)
+    settle("load0")
+    project(0)
+    pump(("step", 2, 1))
+    attend(0, 0)
+    pump(("step", 2, 2), ("start", 4), ("finish", 1))
+    attend(0, 1)
+    copy = project_out(0)
+    pump(("step", 2, 3))
+    load(1, wu)
+    pump(("step", 3, 1))
+    norm_two(0, 0, copy)
+    settle("load1")
+    pump(("step", 3, 2), ("start", 5), ("finish", 2))
+    hidden(0, 0)
+    hidden(0, 1)
+    pump(("step", 3, 3))
+    load(2, wd)
+    settle("load2")
+    copy = project_down(1)
+    pump(("step", 4, 1), ("step", 4, 2), ("finish", 3))
+    end_block(0, 1, copy)
+    spread()
+    norm_one(1)
+    pump(("step", 4, 3))
+    load(3, wa)
+    settle("load3")
+    project(1)
+    pump(("step", 5, 1))
+    attend(1, 0)
+    pump(("step", 5, 2), ("finish", 4))
+    attend(1, 1)
+    copy = project_out(2)
+    load(4, wu)
+    pump(("step", 5, 3), ("finish", 5))
+    norm_two(1, 2, copy)
+    settle("load4")
+    hidden(1, 0)
+    hidden(1, 1)
     if fused:
-        gather.finish(5)
-        gather.other_in(5).wait_recv()
+        gather.other_in(5)
         for p in range(gather.pieces):
             gather.drain(p)
     for wait in links.waiting:
@@ -741,7 +793,7 @@
 
 def forward_call(cfg, own, small, dp_count):
     fused, chain, heads, head_dim = cfg
-    rows, width = small[0].shape
+    _, rows, width = small[0].shape
     pieces = 6
     shard = own.shape[-2]
     groups = width // shard
@@ -765,11 +817,11 @@
         f(2, 8, width),
         f(dp_count, 8, cond_lanes),
         f(2, 24, width),
-        f(2, rows, width),
+        f(rows, width),
     ]
     if fused:
         out_shape = [bf(pieces, 2, groups, shard, width)] + out_shape
-    kinds = 3 * chain + 3
+    kinds = 5 * chain + 2
     many = 2 * (dp_count - 1) + 8
     slot = pltpu.VMEM((2, groups, shard, width), BF)
     scratch = [
@@ -797,6 +849,16 @@
         pltpu.VMEM((dp_count, 16, ADA_LANES), F32),
         pltpu.VMEM((2, 2, 16, ADA_LANES), F32),
         pltpu.VMEM((2, 8, width), F32),
+        pltpu.VMEM((rows, width), BF),
+        pltpu.VMEM(small[2].shape, BF),
+        pltpu.VMEM((rows, rows), BF),
+        pltpu.VMEM((rows, rows), F32),
+        pltpu.VMEM((rows, rows), BF),
+        pltpu.VMEM((rows, 128), F32),
+        pltpu.VMEM((rows, rows), BF),
+        pltpu.VMEM((24, width), F32),
+        pltpu.VMEM((8, ADA_LANES), F32),
+        pltpu.VMEM((8, ADA_LANES), F32),
         pltpu.SemaphoreType.DMA((pieces, kinds)),
         pltpu.SemaphoreType.DMA((pieces, kinds)),
         pltpu.SemaphoreType.DMA((3,)),
@@ -815,7 +877,7 @@
     result = pl.pallas_call(
         body,
         out_shape=out_shape,
-        in_specs=[hbm] + [vm] * len(small),
+        in_specs=[hbm] + [hbm, vm, hbm] + [vm] * 8,
         out_specs=[hbm] * len(out_shape),
         scratch_shapes=scratch,
         compiler_params=pltpu.CompilerParams(
@@ -889,11 +951,11 @@
             def _():
                 pl.semaphore_wait(self.credit.at[2], 1)
 
-        if r % 2 == 1:
+        if r in SUM_BY_MATE:
             self.to_mate(r).start()
         for i in range(chain - 1):
             t = self.target(i)
-            if r % 2 == 1:
+            if r in SUM_BY_MATE:
 
                 @pl.when(t != at.mate_z)
                 def _():
@@ -901,11 +963,11 @@
 
             else:
                 self.cross(r, t).start()
-        if r % 2 == 0:
+        if r not in SUM_BY_MATE:
             self.cross(r, at.z).start()
 
     def mated(self, r):
-        if r % 2 == 1:
+        if r in SUM_BY_MATE:
             self.to_mate(r).wait_recv()
             self.add(self.theirs(r, self.at.z), self.mr.at[self.slots(r)[1]])
             self.cross(r, self.at.z).start()
@@ -917,7 +979,7 @@
             self.cross(r, t).wait_recv()
             self.add(self.own(r, t), self.yr.at[self.slots(r)[1], t])
 
-        if r % 2 == 1:
+        if r in SUM_BY_MATE:
             pl.when(t != self.at.mate_z)(take)
         else:
             take()
@@ -1017,10 +1079,10 @@
 
     def drain(self, r):
         z, chain = self.at.z, self.at.chain
-        if r % 2 == 1:
+        if r in SUM_BY_MATE:
             self.to_mate(r).wait_send()
         for t in range(chain):
-            if r % 2 == 1:
+            if r in SUM_BY_MATE:
 
                 @pl.when(t != self.at.mate_z)
                 def _():
@@ -1063,16 +1125,17 @@
     w = refs.pop(0)
     (
         i_hat1, i_inv, i_n1, i_qkv, i_p, i_o, i_branch, i_hat2, i_n2, i_hid, i_slope, i_y, i_full, i_xm,
-    ) = refs[:14]
-    refs = refs[14:]
-    dout, mod, small, cl, wada, flips, pos, place, drop = refs[:9]
-    refs = refs[9:]
+        i_e,
+    ) = refs[:15]
+    refs = refs[15:]
+    i_dout, mod, i_small, i_cl, i_wada, kept = refs[:6]
+    refs = refs[6:]
     red_out, o_dx, o_out, o_sums, o_dm, o_dc = refs[:6]
     refs = refs[6:]
     (
         wslot, hat1, inv, qkv, prob, o, branch, hat2, n2, hid, slope,
         d, r, dy, dpre, dattn, dqkv, do, xs, xr, g, yr, zr, mr, red,
-        stats, got, sums, rounds, dm, dc, dg, gs, gr, go, gi, gl, credit, ssem, rsem, lsem, ms, mrs,
+        stats, got, sums, msg, dc, dg, small, cl, wada, flips, pos, place, drop, eye, dout, gs, gr, go, gi, gl, credit, ssem, rsem, lsem, ms, mrs,
     ) = refs
     at = Place(chain)
     rows, width = d.shape
@@ -1084,6 +1147,7 @@
     at.greet()
     links = Links(at, ms, mrs)
     stats[...] = jnp.zeros_like(stats)
+    dc[...] = jnp.zeros_like(dc)
     scatter = (
         Scatter(at, ORDER, g, yr, zr, mr, red, red_out, gs, gr, go, gi, gl, credit) if fused else None
     )
@@ -1137,21 +1201,24 @@
     spans = [slice(k * HEAD_LANES, (k + 1) * HEAD_LANES) for k in range(3)]
     spot = lambda half: jnp.where(half == at.core, 0, 2)
 
-    def loads(s):
-        fetch("slope", i_slope.at[s], slope)
-        if s == 0:
-            fetch("y", i_y, xs.at[2])
-        else:
-            fetch("full", i_full, dqkv.at[0:2])
-        fetch("hid", i_hid.at[s], hid)
-        fetch("n2", i_n2.at[s], n2)
-        fetch("hat2", i_hat2.at[s], hat2)
-        fetch("inv", i_inv.at[s], inv)
-        fetch("branch", i_branch.at[s], branch)
-        fetch("p", i_p.at[s], prob)
-        fetch("qkv", i_qkv.at[s], qkv)
-        fetch("o", i_o.at[s], o)
-        fetch("hat1", i_hat1.at[s], hat1)
+    def load(name, s):
+        src, dst = {
+            "slope": (i_slope, slope),
+            "hid": (i_hid, hid),
+            "n1": (i_n1, hid),
+            "n2": (i_n2, n2),
+            "hat2": (i_hat2, hat2),
+            "inv": (i_inv, inv),
+            "branch": (i_branch, branch),
+            "p": (i_p, prob),
+            "qkv": (i_qkv, qkv),
+            "o": (i_o, o),
+            "hat1": (i_hat1, hat1),
+        }[name]
+        fetch(name, src.at[s], dst)
+
+    def weight(p, slot):
+        fetch("w%d" % slot, w.at[p], wslot.at[slot])
 
     def product(r_, parts):
         slot = r_ % slots
@@ -1173,12 +1240,18 @@
     def cols_of(ref, j):
         return flat(ref[0:2, :, j * 384 : (j + 1) * 384])
 
-    def block_back(s):
-        base = 0 if s == 1 else 3
-        xi = 0 if s == 1 else 2
-        first, second, third = (0, 1, 0) if s == 1 else (1, 0, 1)
-        settle("y")
+    down_slot, up_slot, att_slot = (1, 0), (0, 1), (1, 0)
+
+    def base(s):
+        return 0 if s == 1 else 3
+
+    def exchange(s):
+        return 0 if s == 1 else 2
+
+    def back_gate(s):
         settle("dy out")
+        if s == 0:
+            settle("y")
 
         def one(ds, c):
             a, b = c
@@ -1192,46 +1265,46 @@
         a, b = by_rows(rows, one, (zero8(), zero8()))
         if s == 0:
             stat(s, 5, a)
-        stat(s, 6, b)
+        stat(s, 8, b)
         give("dy", dy.at[0], dy.at[1])
-        settle("w%d" % first)
+
+    def back_hidden(s):
+        slot = down_slot[s]
+        settle("w%d" % slot)
         settle("slope")
         settle("dpre out")
-        if s == 1:
-            settle("full")
-            project_down()
         for half in range(2):
             for j in range(3):
                 cols = slice(j * 384, (j + 1) * 384)
-                v = (nn(dy[0], flat(wslot[first, half, :, :, cols])) * slope[half, :, cols].astype(F32)).astype(BF)
+                v = (nn(dy[0], flat(wslot[slot, half, :, :, cols])) * slope[half, :, cols].astype(F32)).astype(BF)
                 dpre[spot(half), :, cols] = v
-                stats[s, 8 + half : 9 + half, cols] = jnp.sum(v.astype(F32), axis=0, keepdims=True)
+                stats[s, 10 + half : 11 + half, cols] = jnp.sum(v.astype(F32), axis=0, keepdims=True)
         give("dpre", dpre.at[2], dpre.at[1])
-        fetch("w%d" % first, w.at[3 * s], wslot.at[first])
+
+    def down_product(s):
         settle("dy in")
         settle("hid")
-        product(base, lambda j: [(flat(dy[...]), cols_of(hid, j))])
-        fetch("n1", i_n1.at[s], hid)
-        pump(("begin", base))
-        settle("w%d" % second)
+        product(base(s), lambda j: [(flat(dy[...]), cols_of(hid, j))])
+        load("n1", s)
+
+    def back_up(s):
+        slot = up_slot[s]
+        xi = exchange(s)
+        settle("w%d" % slot)
         if xi > 1:
             settle("x out %d" % (xi - 2))
         xs[xi % 2] = (
-            nt(dpre[spot(0)], flat(wslot[second, 0])) + nt(dpre[spot(1)], flat(wslot[second, 1]))
+            nt(dpre[spot(0)], flat(wslot[slot, 0])) + nt(dpre[spot(1)], flat(wslot[slot, 1]))
         ).astype(BF)
         send_across(xi)
-        if s == 1:
-            fetch("w%d" % second, w.at[2], wslot.at[second])
-        if s == 0:
-            pump(("arrive", 1, 3), ("finish", 1))
+
+    def up_product(s):
         settle("dpre in")
         settle("n2")
-        product(base + 1, lambda j: [(flat(n2[...]), cols_of(dpre, j))])
-        pump(("begin", base + 1))
-        if s == 1:
-            pump(("arrive", 0, 0), ("step", 0, 1), ("arrive", 0, 1), ("step", 0, 2))
-        else:
-            pump(("arrive", 2, 0), ("step", 2, 1), ("arrive", 2, 1), ("step", 2, 2), ("arrive", 2, 2), ("step", 2, 3))
+        product(base(s) + 1, lambda j: [(flat(n2[...]), cols_of(dpre, j))])
+
+    def back_norm_two(s):
+        xi = exchange(s)
         settle("x in %d" % xi)
         settle("hat2")
         settle("inv")
@@ -1257,22 +1330,18 @@
         stat(s, 3, c0)
         stat(s, 4, c1)
         stat(s, 2, c2)
-        stat(s, 7, c3)
+        stat(s, 9, c3)
         give("dattn", dattn.at[0], dattn.at[1])
-        settle("w%d" % third)
-        settle("p")
-        settle("qkv")
-        settle("dqkv out")
-        for half in range(2):
-            if s == 1 and half == 0:
-                pump(("arrive", 0, 2), ("step", 0, 3))
-            if s == 1 and half == 1:
-                pump(("arrive", 0, 3))
-            if s == 0 and half == 0:
-                pump(("arrive", 2, 3), ("finish", 2))
-            if s == 0 and half == 1:
-                pump(("mated", 3), ("arrive", 3, 0), ("step", 3, 1))
-            do[half] = nn(dattn[0], flat(wslot[third, half, :, :, :HEAD_LANES])).astype(BF)
+
+    def back_heads(s, half):
+        slot = att_slot[s]
+        if half == 0:
+            settle("w%d" % slot)
+            settle("p")
+            settle("qkv")
+            settle("dqkv out")
+        if True:
+            do[half] = nn(dattn[0], flat(wslot[slot, half, :, :, :HEAD_LANES])).astype(BF)
             r[...] = jnp.zeros_like(r)
 
             def head(i, c):
@@ -1287,11 +1356,13 @@
                 dz = (pf * (ds - jnp.sum(pf * ds, axis=-1, keepdims=True))).astype(BF)
                 r[:, spans[0]] = r[:, spans[0]] + nn(dz, qkv[1, half]) * mask
                 r[:, spans[1]] = r[:, spans[1]] + tn(dz, qkv[0, half]) * mask
-                square = tn(flips[s], dz)
+                square = nn(dz, flips[s])
+                high = square.astype(BF)
                 if s == 0:
-                    high = square.astype(BF)
                     low = (square - high.astype(F32)).astype(BF)
-                    square = nn(high, pos[...]) + nn(low, pos[...])
+                    square = tn(high, pos[...]) + tn(low, pos[...])
+                else:
+                    square = tn(high, eye[...])
                 wide = jnp.concatenate([square, jnp.zeros_like(square)], axis=1)
                 skew = pltpu.roll(wide, 0, 1, stride=1, stride_axis=0)
                 stats[s, pl.ds(16 + index, 1), : 2 * rows] = jnp.sum(skew, axis=0, keepdims=True)
@@ -1310,37 +1381,33 @@
                 dqkv[where, ds, :] = v
                 return c + column_sum(v.astype(F32))
 
-            stat(s, 10 + half, by_rows(rows, gather_rows, zero8()))
-        give("dqkv", dqkv.at[2], dqkv.at[1])
-        if s == 1:
-            fetch("xm", i_xm, r)
-        xs_free = xi + 1
-        if xs_free > 1:
-            settle("x out %d" % (xs_free - 2))
-        xs[xs_free % 2] = (
-            nt(dqkv[spot(0)], flat(wslot[third, 0])) + nt(dqkv[spot(1)], flat(wslot[third, 1]))
+            stat(s, 12 + half, by_rows(rows, gather_rows, zero8()))
+        if half == 1:
+            give("dqkv", dqkv.at[2], dqkv.at[1])
+
+    def back_qkv(s):
+        slot = att_slot[s]
+        xi = exchange(s) + 1
+        if xi > 1:
+            settle("x out %d" % (xi - 2))
+        xs[xi % 2] = (
+            nt(dqkv[spot(0)], flat(wslot[slot, 0])) + nt(dqkv[spot(1)], flat(wslot[slot, 1]))
         ).astype(BF)
-        send_across(xs_free)
-        if s == 1:
-            fetch("w%d" % third, w.at[1], wslot.at[third])
-        if s == 1:
-            pump(("finish", 0))
+        send_across(xi)
+
+    def att_product(s):
         settle("dqkv in")
         settle("dattn in")
         settle("n1")
         settle("o")
         product(
-            base + 2,
+            base(s) + 2,
             lambda j: [(flat(hid[...]), cols_of(dqkv, j))]
             + ([(flat(dattn[...]), flat(o[...]))] if j == 0 else []),
         )
-        pump(("begin", base + 2))
-        if s == 1:
-            pump(("mated", 1), ("arrive", 1, 0), ("step", 1, 1))
-            end_forward()
-            pump(("arrive", 1, 1), ("step", 1, 2))
-        else:
-            pump(("arrive", 3, 1), ("step", 3, 2), ("arrive", 3, 2), ("step", 3, 3))
+
+    def back_norm_one(s):
+        xs_free = exchange(s) + 1
         settle("x in %d" % xs_free)
         settle("hat1")
 
@@ -1355,7 +1422,7 @@
         c0, c1, c2 = by_rows(rows, three, (zero8(),) * 3)
         stat(s, 0, c0)
         stat(s, 1, c1)
-        stat(s, 12, c2)
+        stat(s, 14, c2)
         to_section("dx", s, d, o_dx)
 
     def to_section(name, s, src, out):
@@ -1388,6 +1455,8 @@
         waiting.setdefault("end", []).append(arrived)
 
     def project_down():
+        settle("w0")
+        settle("full")
         xs[2] = (nt(dqkv[0], flat(wslot[0, 0])) + nt(dqkv[1], flat(wslot[0, 1]))).astype(BF)
         copy = remote(xs.at[2], xr.at[2], sends.next(), recvs.next(), at.beside)
         copy.start()
@@ -1398,6 +1467,7 @@
         settle("y in")
         settle("y out")
         settle("xm")
+        settle("small")
 
         def body(ds, c):
             v = xs[2, ds, :].astype(F32) + xr[2, ds, :].astype(F32) + small[1, 9:10, :]
@@ -1408,46 +1478,43 @@
         to_section("result", 1, r, o_out)
 
     def sums_begin():
-        stats[0, 12:13, :] = stats[1, 12:13, :]
+        stats[0, 14:15, :] = stats[1, 14:15, :]
         return links.copy(stats.at[1 - at.core], got, at.other)
 
     def sums_share(copy):
         copy.wait_recv()
-        sums[0] = stats[at.core] + got[...]
+        msg[at.dp, :, :width] = (stats[at.core, 8:24, :] + got[8:24, :]).astype(BF)
         row = lax.broadcasted_iota(jnp.int32, (8, ADA_LANES), 0)
         lane = lax.broadcasted_iota(jnp.int32, (8, ADA_LANES), 1)
-        for m, value in ((at.core, stats[at.core, 0:8, :]), (1 - at.core, got[0:8, :])):
-            cut = jnp.where(
+
+        def cut(value):
+            value = jnp.where(
                 at.head == 0, value[:, :ADA_LANES], pltpu.roll(value, width - lw, 1)[:, :ADA_LANES]
             )
-            cut = jnp.where((row < 6) & (lane < lw), cut, 0.0)
-            dm[at.dp, pl.ds(pl.multiple_of(m * 8, 8), 8), :] = cut
-        copies = links.to_all(lambda peer: dm.at[at.dp], dm.at[at.dp])
-        return copies, sums_round(0)
-
-    def sums_round(b):
-        return links.copy(sums.at[b], rounds.at[b], at.in_dp(at.flip(b)))
-
-    def sums_next(b, copy):
-        copy.wait_recv()
-        sums[b + 1] = sums[b] + rounds[b]
-        if b + 1 < rounds.shape[0]:
-            return sums_round(b + 1)
-        fetch("sums", sums.at[b + 1], o_sums)
-        return None
+            return jnp.where((row < 6) & (lane < lw), value, 0.0)
+
+        own, other = cut(stats[at.core, 0:8, :]), cut(got[0:8, :])
+        both_ = [jnp.where(at.core == 0, own, other), jnp.where(at.core == 0, other, own)]
+        msg[at.dp, :, width:] = jnp.concatenate(both_, axis=0).astype(BF)
+        return links.to_all(lambda peer: msg.at[at.dp], msg.at[at.dp])
 
     def cond_terms(copies):
         for copy in copies:
             copy.wait_recv()
-        fetch("dm", dm, o_dm)
-        lhs = flat(dm[...])
-        high = lhs.astype(BF)
-        low = (lhs - high.astype(F32)).astype(BF)
+        settle("wada")
+        settle("cl")
+        fetch("dm", msg.at[:, :, pl.ds(width, ADA_LANES)], o_dm)
+        value = msg[0, :, :width].astype(F32)
+        for j in range(1, at.count):
+            value = value + msg[j, :, :width].astype(F32)
+        sums[...] = value
+        fetch("sums", sums, o_sums)
+        lhs = flat(msg[:, :, width:])
         row = lax.rem(lax.broadcasted_iota(jnp.int32, (lhs.shape[0], 1), 0), 8)
         total_ = jnp.zeros((lhs.shape[0], shard), F32)
         for k in range(6):
             cols = wada[:, k * ADA_LANES : (k + 1) * ADA_LANES]
-            total_ = total_ + jnp.where(row == k, nt(high, cols) + nt(low, cols), 0.0)
+            total_ = total_ + jnp.where(row == k, nt(lhs, cols), 0.0)
         total_ = total_.reshape(at.count, 16, shard)
         for m in range(2):
             dc[at.core, at.head, m, :, :shard] = jnp.sum(total_[:, m * 8 : (m + 1) * 8, :], axis=1)
@@ -1468,45 +1535,114 @@
             copy.wait_recv()
         fetch("dg", dg, o_dc)
 
-    dc[...] = jnp.zeros_like(dc)
-    loads(1)
-    fetch("w0", w.at[5], wslot.at[0])
-    fetch("w1", w.at[4], wslot.at[1])
+    fetch("dout", i_dout.at[at.core], dout)
+    weight(5, 0)
+    load("slope", 1)
+    load("hid", 1)
+    weight(4, 1)
+    for name in ("n2", "hat2", "inv", "branch", "p", "qkv", "o", "hat1"):
+        load(name, 1)
+    for name, src, dst in (
+        ("y", i_y, xs.at[2]),
+        ("small", i_small, small),
+        ("cl", i_cl, cl),
+        ("wada", i_wada, wada),
+    ):
+        fetch(name, src, dst)
+
+    to_section("e", 0, i_e, o_out)
+    settle("dout")
 
     def start_rows(ds, c):
         d[ds, :] = dout[ds, :].astype(F32)
         return c
 
     by_rows(rows, start_rows, 0)
-    block_back(1)
-    loads(0)
-    settle("result")
-    r[...] = tn(place[...], d[...].astype(BF))
-    settle("dx")
+
+    def to_encoder():
+        r[...] = tn(place[...], d[...].astype(BF))
+        settle("dx")
+
+        def move(ds, c):
+            d[ds, :] = r[ds, :]
+            return c
+
+        by_rows(rows, move, 0)
+
+    back_gate(1)
+    back_hidden(1)
+    weight(3, 0)
+    load("slope", 0)
+    down_product(1)
+    pump(("begin", 0))
+    back_up(1)
+    weight(2, 1)
+    up_product(1)
+    load("n2", 0)
+    pump(("begin", 1))
+    pump(("arrive", 0, 0), ("step", 0, 1), ("arrive", 0, 1), ("step", 0, 2))
+    spread_masks(kept[at.core].astype(F32), place, pos, drop)
+    eye[...] = diagonal(rows)
+    flips[1] = diagonal(rows, True)
+    flips[0] = nn(pos[...], flips[1]).astype(BF)
+    back_norm_two(1)
+    load("hat2", 0)
+    load("branch", 0)
+    back_heads(1, 0)
+    pump(("arrive", 0, 2), ("step", 0, 3))
+    back_heads(1, 1)
+    load("p", 0)
+    load("qkv", 0)
+    back_qkv(1)
+    weight(1, 0)
+    pump(("arrive", 0, 3))
+    att_product(1)
+    load("hid", 0)
+    load("o", 0)
+    pump(("begin", 2))
+    pump(("mated", 1), ("arrive", 1, 0), ("step", 1, 1), ("finish", 0))
+    back_norm_one(1)
+    load("hat1", 0)
+    load("inv", 0)
+    to_encoder()
+    back_gate(0)
+    pump(("arrive", 1, 1), ("step", 1, 2))
+    back_hidden(0)
+    weight(0, 1)
+    down_product(0)
+    pump(("begin", 3))
     pump(("arrive", 1, 2), ("step", 1, 3))
-
-    def move(ds, c):
-        d[ds, :] = r[ds, :]
-        return c
-
-    by_rows(rows, move, 0)
-    block_back(0)
+    back_up(0)
+    weight(5, 0)
+    pump(("arrive", 1, 3), ("mated", 2), ("arrive", 2, 0), ("step", 2, 1), ("finish", 1))
+    up_product(0)
+    pump(("begin", 4))
+    pump(("arrive", 2, 1), ("step", 2, 2))
+    back_norm_two(0)
+    back_heads(0, 0)
+    pump(("arrive", 2, 2), ("step", 2, 3))
+    back_heads(0, 1)
+    back_qkv(0)
+    fetch("xm", i_xm, r)
+    pump(("arrive", 2, 3), ("mated", 3), ("arrive", 3, 0), ("step", 3, 1), ("finish", 2))
+    att_product(0)
+    fetch("full", i_full, dqkv.at[0:2])
+    pump(("begin", 5))
+    pump(("arrive", 3, 1), ("step", 3, 2))
+    project_down()
+    back_norm_one(0)
+    pump(("arrive", 3, 2), ("step", 3, 3))
+    end_forward()
     copy = sums_begin()
-    pump(("arrive", 3, 3), ("finish", 3))
-    copies, copy = sums_share(copy)
-    pump(("arrive", 4, 0), ("step", 4, 1))
-    copy = sums_next(0, copy)
+    pump(("arrive", 3, 3), ("mated", 4), ("arrive", 4, 0), ("step", 4, 1), ("finish", 3))
+    copies = sums_share(copy)
+    pump(("arrive", 4, 1), ("step", 4, 2), ("arrive", 4, 2), ("step", 4, 3), ("arrive", 4, 3))
     copies = cond_terms(copies)
-    pump(("arrive", 4, 1), ("step", 4, 2))
-    for b in range(1, rounds.shape[0]):
-        copy = sums_next(b, copy)
-        pump(("arrive", 4, b + 1))
-        if b + 2 < chain:
-            pump(("step", 4, b + 2))
+    pump(("arrive", 5, 0), ("step", 5, 1), ("finish", 4))
     copies = cond_share(copies)
-    pump(("finish", 4), ("mated", 5), ("arrive", 5, 0), ("step", 5, 1))
+    pump(("arrive", 5, 1), ("step", 5, 2), ("arrive", 5, 2), ("step", 5, 3), ("arrive", 5, 3))
     cond_end(copies)
-    pump_rest(5, 1)
+    pump(("finish", 5))
     if fused:
         for r_ in range(len(ORDER) - slots, len(ORDER)):
             scatter.drain(r_)
@@ -1519,11 +1655,10 @@
 
 def backward_call(cfg, w, saved, small):
     fused, chain, heads, head_dim = cfg
-    rows, width = small[0].shape
+    _, rows, width = small[0].shape
     pieces, _, groups, shard, _ = w.shape
     count, _, cond_lanes = small[3].shape
-    steps = count.bit_length() - 1
-    many = 2 * (count - 1) + 6 + steps
+    many = 2 * (count - 1) + 6
     bf, f = lambda *s: pltpu.VMEM(s, BF), lambda *s: pltpu.VMEM(s, F32)
     dma = lambda *s: pltpu.SemaphoreType.DMA(s)
     out_shape = [
@@ -1532,8 +1667,8 @@
         else jax.ShapeDtypeStruct((pieces, groups, shard, width), BF),
         jax.ShapeDtypeStruct((2, rows, width), F32),
         jax.ShapeDtypeStruct((2, rows, width), F32),
-        jax.ShapeDtypeStruct((24, width), F32),
-        jax.ShapeDtypeStruct((count, 16, ADA_LANES), F32),
+        jax.ShapeDtypeStruct((16, width), F32),
+        jax.ShapeDtypeStruct((count, 16, ADA_LANES), BF),
         jax.ShapeDtypeStruct((count, 2, count, cond_lanes), F32),
     ]
     some = 3 if fused else 1
@@ -1567,19 +1702,27 @@
         f(2, block, width),
         f(2, 24, width),
         f(24, width),
-        f(steps + 1, 24, width),
-        f(steps, 24, width),
-        f(count, 16, ADA_LANES),
+        f(16, width),
+        bf(count, 16, width + ADA_LANES),
         f(2, 2, 2, count, cond_lanes),
         f(count, 2, count, cond_lanes),
+        f(2, 24, width),
+        f(count, 8, cond_lanes),
+        bf(*small[4].shape),
+        bf(2, rows, rows),
+        bf(rows, rows),
+        bf(rows, rows),
+        f(rows, 128),
+        bf(rows, rows),
+        bf(rows, width),
         dma(6, 3 * links + 1),
         dma(6, 3 * links + 1),
         dma(6),
         dma(6),
         dma(6),
         pltpu.SemaphoreType.REGULAR((3,)),
-        dma(16),
-        dma(16),
+        dma(20),
+        dma(20),
         dma(56),
         dma(many),
         dma(many),
@@ -1593,7 +1736,7 @@
     return pl.pallas_call(
         body,
         out_shape=out_shape,
-        in_specs=[hbm] * (1 + len(saved)) + [vm] * len(small),
+        in_specs=[hbm] * (1 + len(saved)) + [hbm, vm, hbm, hbm, hbm, vm],
         out_specs=[hbm] * len(out_shape),
         scratch_shapes=scratch,
         compiler_params=pltpu.CompilerParams(
@@ -1657,41 +1800,6 @@
     blocks = jnp.concatenate([blocks, tags], axis=2)
     blocks = jnp.pad(blocks, ((0, 0), (0, 8 - micro), (0, cond_lanes - fr - 1)))
     ada = jnp.pad(w_ada[0], ((0, 0), (0, 0), (0, ADA_LANES - lw))).reshape(fr, 6 * ADA_LANES)
-    b_ada_in = jnp.pad(b_ada[0].astype(F32), ((0, 2), (0, ADA_LANES - lw)))
-
-    def row_block(value):
-        return jnp.pad(value.astype(F32), ((0, 0), (0, width - value.shape[1])))
-
-    qv = b_qv[0].reshape(2, 2, hw)
-    none = jnp.zeros((2, hw), BF)
-    qv_rows = jnp.stack([qv[0], none, qv[1], none], axis=1).reshape(8, hw)
-    qv_rows = jnp.pad(qv_rows, ((0, 0), (0, HEAD_LANES - hw)))
-    rel = rel_table[0]
-    rel = jnp.concatenate(
-        [rel[:, length - 1 :: -1], jnp.zeros((heads, 1), BF), rel[:, : length - 1 : -1]], axis=1
-    )
-    small_own = jnp.concatenate(
-        [
-            row_block(qv_rows),
-            row_block(b_out),
-            row_block(b_down),
-            row_block(b_up[0].reshape(2, fw)),
-            jnp.zeros((4, width), F32),
-            row_block(rel),
-        ]
-    )
-
-    kept = kept_mask[c, 0]
-    source = jnp.cumsum(kept) - 1
-    count = jnp.sum(kept)
-    span = jnp.arange(length, dtype=jnp.int32)
-    place = ((kept[:, None] == 1) & (source[:, None] == span[None, :])).astype(BF)
-    pad = span >= count
-    pos = place.T + (pad[:, None] & (span[None, :] == 0)).astype(BF)
-    seg = jnp.where(pad[:, None] == pad[None, :], 0.0, NEGATIVE)
-    mirror = (span[:, None] + span[None, :] == length - 1).astype(BF)
-    flips = jnp.stack([pos[:, ::-1], mirror])
-    drop = jnp.broadcast_to((1 - kept)[:, None].astype(F32), (rows, 128))
 
     fused = dp_count == 8 and fr % 16 == 0
     cfg = (fused, dp_count // 2, heads, head_dim)
@@ -1706,20 +1814,22 @@
         source_w = jnp.stack([pick(c, half_w_, other_w), pick(c, other_w, half_w_)], axis=1)
         source_w = source_w.reshape(6, 2, 8, width // 8, pack.shape[3])
     small_in = (
-        tokens[c],
+        tokens,
         blocks,
         ada,
-        b_ada_in,
-        small_own,
-        pos,
-        seg,
-        place,
-        drop,
-        mask_token.astype(F32)[None, :],
+        b_ada,
+        kept_mask,
+        b_qv,
+        b_out,
+        b_down,
+        b_up,
+        rel_table,
+        mask_token[None, :],
     )
-    full, *saved, mod, cond_all, small_all, outs = forward_call(cfg, source_w, small_in, dp_count)
-    small_back = (out_grad[c], mod, small_all, cond_all, ada, flips, pos, place, drop)
-    red, dx, outs_b, sums, dm, dc = backward_call(cfg, full, saved, small_back)
+    full, *saved, mod, cond_all, small_all, enc = forward_call(cfg, source_w, small_in, dp_count)
+    saved.append(enc)
+    small_back = (out_grad, mod, small_all, cond_all, ada, kept_mask)
+    red, dx, outs, sums, dm, dc = backward_call(cfg, full, saved, small_back)
 
     if fused:
         g0, g1 = red[:, 0], red[:, 1]
@@ -1749,14 +1859,14 @@
 
     g_b_qv = jnp.stack(
         [
-            jnp.concatenate([sums[10, at * hw : (at + 1) * hw], sums[11, at * hw : (at + 1) * hw]])
+            jnp.concatenate([sums[4, at * hw : (at + 1) * hw], sums[5, at * hw : (at + 1) * hw]])
             for at in (1, 3)
         ]
     )
-    g_b_up = sums[8:10, :fw].reshape(-1)
-    g_rel = sums[16 : 16 + heads, 2 * length - 2 :: -1]
-
-    dm = dm.reshape(dp_count, micro, 8, ADA_LANES)[:, :, :6, :lw]
+    g_b_up = sums[2:4, :fw].reshape(-1)
+    g_rel = sums[8 : 8 + heads, : 2 * length - 1]
+
+    dm = dm.astype(F32).reshape(dp_count, micro, 8, ADA_LANES)[:, :, :6, :lw]
     cond_part = jax.nn.silu(cond_all[:, :micro, :fr])
     g_ada = jnp.einsum("jmf,jmke->fke", cond_part, dm, precision=PRECISE)
     g_b_ada = jnp.sum(dm, axis=(0, 1))
@@ -1766,20 +1876,20 @@
     g_class = jnp.einsum("ic,id->cd", pick_all, half(dcond), precision=PRECISE)
 
     return (
-        pick(c, outs, outs_b)[None],
+        outs[None],
         dx[None],
         g_qkv[None],
         g_b_qv[None],
         g_out[None],
-        half(sums[7])[None],
+        half(sums[1])[None],
         g_up[None],
         g_b_up[None],
         g_down[None],
-        half(sums[6])[None],
+        half(sums[0])[None],
         g_ada[None],
         g_b_ada[None],
         g_rel[None],
-        half(sums[12]),
+        half(sums[6]),
         g_class,
     )
 

time: 473 us -> 413 us (0.87)
  Pallas kernels: 420 us -> 377 us
  other arithmetic: 18.8 us -> 9.78 us
  local copies, waits for them, and re-layouts: 22.5 us -> 15.9 us
    pallas_call x1, Pallas kernels: 226 us -> 191 us  [backward_call(): pl.pallas_call(body, out_shape=out_shape, in_specs=[hbm] * (1 + len(saved...]
    pallas_call x1, Pallas kernels: 195 us -> 186 us  [forward_call(): pl.pallas_call(body, out_shape=out_shape, in_specs=[hbm] + [hbm, vm, hbm]...]
where the time goes in v4:
time: 413 us; the launch traced here: 410 us
  Pallas kernels  377 us (91%)
  local copies, waits for them, and re-layouts  15.9 us (4%)
  other arithmetic  9.78 us (2%)
  matrix products  5.5 us (1%)
    pallas_call x1, Pallas kernels, backward_call(): pl.pallas_call(body, out_shape=out_shape, in_specs=[hbm] * (1 + len(saved...  191 us
    pallas_call x1, Pallas kernels, forward_call(): pl.pallas_call(body, out_shape=out_shape, in_specs=[hbm] + [hbm, vm, hbm]...  186 us

profile of v4, /device:TPU:0, one launch (start us, length us, event | category | flops | bytes accessed | tf_op | source)
XLA Modules:
  0.0 409.7 jit_solution(5997508001884513487)
XLA Ops:
  0.7 1.2 slice_bitcast_fusion.10
  1.8 0.1 fusion.12
  2.0 0.0 copy-start.5
  2.0 0.1 fusion.13
  2.1 0.1 fusion.14
  2.2 0.1 fusion.15
  2.3 0.0 copy-start.6
  2.3 0.2 concatenate.37
  2.6 0.2 concatenate.36
  2.8 0.2 copy-done.5
  3.0 0.1 slice_bitcast_fusion.9
  3.1 0.3 copy-done.6
  3.4 0.1 slice_bitcast_fusion.8
  3.5 0.3 maximum_bitcast_fusion.3
  3.8 0.0 copy-start.12
  3.8 0.0 copy-start.3
  3.8 0.0 copy-start.11
  3.8 1.5 pad_maximum_fusion.refs_0_
  5.3 0.2 multiply_cosine_fusion
  5.5 0.7 copy-done.3
  6.2 0.4 convolution_add_fusion
  6.6 0.1 reshape.71
  6.8 0.1 broadcast_in_dim.48
  6.9 0.7 select_maximum_fusion.refs_2_
  7.6 0.3 copy.53
  7.9 0.3 pad.9.clone
  8.1 0.0 copy-start.10
  8.2 1.1 copy.54
  9.3 0.6 broadcast_in_dim.49.refs_11_
  9.9 186.3 %forward_blocks.1 = (bf16[6,2,8,144,1152]{4,3,2,1,0:T(8,128)(2,1)}, bf16[2,256,1152]{2,1,0:T(8,128)(2,1)}, f32[2,2,256,128]{3,2,1,0:T(8,128)}, bf16[2,2,256,1152...) custom-call(bf16[2,3,144,1152]{3,2,1,0:T(8,128)(2,1)} %pad_maximum_f, ...), custom_call_target="tpu_custom_call" | custom-call | tf_op jit(solution)/shard_map/forward_blocks/pallas_call | solution.py:877
  196.2 191.0 %backward_blocks.1 = (f32[3,2,144,1152]{3,2,1,0:T(8,128)}, f32[2,256,1152]{2,1,0:T(8,128)}, f32[2,256,1152]{2,1,0:T(8,128)}, f32[16,1152]{1,0:T(8,128)}, bf16[8,...) custom-call(bf16[6,2,8,144,1152]{4,3,2,1,0:T(8,128)(2,1)} %get-tuple-element.40.refs_0_, ...), custom_call_target="tpu_custom_call" | custom-call | tf_op jit(solution)/shard_map/backward_blocks/pallas_call | solution.py:1736
  387.3 0.9 slice_bitcast_fusion.13
  388.2 0.1 copy.50
  388.3 0.1 reshape.74
  388.4 0.8 slice_convert_fusion
  389.2 0.1 copy.49
  389.3 0.1 eq.34
  389.4 2.6 fusion.1
  392.1 0.9 divide_multiply_fusion
  392.9 2.4 convolution_bitcast_fusion
  395.4 0.3 slice_bitcast_fusion.1
  395.6 1.1 maximum_bitcast_fusion.1
  396.8 1.1 maximum_bitcast_fusion
  397.9 0.2 fusion.10
  398.2 0.2 fusion.11
  398.4 0.9 maximum_bitcast_fusion.8
  399.3 0.1 slice_reduce_fusion.3
  399.4 0.1 pad_maximum_fusion.1
  399.4 0.1 pad_maximum_fusion.2
  399.5 0.6 maximum_bitcast_fusion.9
  400.1 0.1 maximum_bitcast_fusion.5
  400.3 0.1 maximum_bitcast_fusion.6
  400.4 0.1 maximum_bitcast_fusion.7
  400.5 1.1 maximum_bitcast_fusion.2
  401.6 0.1 convert_reduce_fusion
  401.6 0.6 broadcast_in_dim.58
  402.3 0.7 dynamic-slice_reduce_fusion
  403.0 0.7 constant_dynamic-slice_fusion
  403.6 0.7 constant_dynamic-slice_fusion.1
  404.3 0.6 copy.55
  404.9 0.6 slice_bitcast_fusion.14
  405.5 1.4 copy.67
  406.9 1.1 copy-done.1
  408.0 1.4 copy.68
  (24 shorter events, 0.1 us)
Async XLA Ops:
  0.6 1.5 copy-start.8
  2.0 1.1 copy-start.5
  2.3 1.1 copy-start.6
  3.8 1.5 copy-start.12
  3.8 2.4 copy-start.3
  3.8 2.4 copy-start.11
  5.3 2.2 copy-start.4
  8.1 1.1 copy-start.10
  388.2 4.7 %copy-start.7 = (bf16[8,16,640]{2,1,0:T(8,128)(2,1)S(1)}, bf16[8,16,640]{2,1,0:T(8,128)(2,1)}, u32[]{:S(2)}) copy-start(bf16[8,16,640]{2,1,0:T(8,128)(2,1)} %get-tuple-element.63) | copy-start | bytes 491524
  389.4 6.0 %copy-start = (f32[3,2,144,1152]{3,2,1,0:T(8,128)S(1)}, f32[3,2,144,1152]{3,2,1,0:T(8,128)}, u32[]{:S(2)}) copy-start(f32[3,2,144,1152]{3,2,1,0:T(8,128)} %get-tuple-element.61) | copy-start | bytes 11943940
  398.1 1.1 copy-start.9
  400.5 5.0 %copy-start.2 = (f32[2,256,1152]{2,1,0:T(8,128)S(1)}, f32[2,256,1152]{2,1,0:T(8,128)}, u32[]{:S(2)}) copy-start(f32[2,256,1152]{2,1,0:T(8,128)} %get-tuple-element.59) | copy-start | bytes 7077892
  405.5 2.5 copy-start.1
